TPU v7x, 32 devices: a whole 2x2x4 slice. The times are simulated.
32 devices in a mesh: dp: 8 (over z, x), seq: 4 (over y, core).
Axes of the slice: x: 2, y: 2, z: 4, core: 2. Of those that a mesh axis runs over, the one named last changes fastest.
Arguments:
- tokens: bfloat16 [32, 1024, 768], P('dp', 'seq'), may hold values from -6 to 6
- doc_lengths: int32 [32, 24], P('dp'), may hold values from 1 to 1001, as said below
- teacher: bfloat16 [32, 12, 1024, 1024], P('dp', None, 'seq'), may hold values from 0.099609375 to 10
- cotangent: bfloat16 [32, 1024, 768], P('dp', 'seq'), may hold values from -6 to 6
- joint_weight: float32 [768, 2304], P(('dp', 'seq')), may hold values from -0.21650635 to 0.21650635
- output_weight: float32 [768, 768], P(('dp', 'seq')), may hold values from -0.4375 to 0.4375
- expand_weight: float32 [768, 3072], P(('dp', 'seq')), may hold values from -0.21650635 to 0.21650635
- shrink_weight: float32 [3072, 768], P(('dp', 'seq')), may hold values from -0.109375 to 0.109375
- vectors: float32 [12, 768], P(None, ('dp', 'seq')), may hold values from -2 to 3
- joint_mean: float32 [768, 2304], P(('dp', 'seq')), may hold values from -0.00061035156 to 0.00061035156
- output_mean: float32 [768, 768], P(('dp', 'seq')), may hold values from -0.00061035156 to 0.00061035156
- expand_mean: float32 [768, 3072], P(('dp', 'seq')), may hold values from -0.00061035156 to 0.00061035156
- shrink_mean: float32 [3072, 768], P(('dp', 'seq')), may hold values from -0.00061035156 to 0.00061035156
- vector_mean: float32 [12, 768], P(None, ('dp', 'seq')), may hold values from -0.00061035156 to 0.00061035156
- joint_square: float32 [768, 2304], P(('dp', 'seq')), may hold values from 1.4110135e-10 to 5.644054e-10
- output_square: float32 [768, 768], P(('dp', 'seq')), may hold values from 1.4110135e-10 to 5.644054e-10
- expand_square: float32 [768, 3072], P(('dp', 'seq')), may hold values from 1.4110135e-10 to 5.644054e-10
- shrink_square: float32 [3072, 768], P(('dp', 'seq')), may hold values from 1.4110135e-10 to 5.644054e-10
- vector_square: float32 [12, 768], P(None, ('dp', 'seq')), may hold values from 1.4110135e-10 to 5.644054e-10
Outputs:
- layer_output: bfloat16 [32, 1024, 768], P('dp', 'seq')
- token_gradient: float32 [32, 1024, 768], P('dp', 'seq')
- gradient_norm: float32 [], replicated
- joint_master: float32 [768, 2304], P(('dp', 'seq'))
- output_master: float32 [768, 768], P(('dp', 'seq'))
- expand_master: float32 [768, 3072], P(('dp', 'seq'))
- shrink_master: float32 [3072, 768], P(('dp', 'seq'))
- vector_master: float32 [12, 768], P(None, ('dp', 'seq'))
- joint_momentum: float32 [768, 2304], P(('dp', 'seq'))
- output_momentum: float32 [768, 768], P(('dp', 'seq'))
- expand_momentum: float32 [768, 3072], P(('dp', 'seq'))
- shrink_momentum: float32 [3072, 768], P(('dp', 'seq'))
- vector_momentum: float32 [12, 768], P(None, ('dp', 'seq'))
- joint_variance: float32 [768, 2304], P(('dp', 'seq'))
- output_variance: float32 [768, 768], P(('dp', 'seq'))
- expand_variance: float32 [768, 3072], P(('dp', 'seq'))
- shrink_variance: float32 [3072, 768], P(('dp', 'seq'))
- vector_variance: float32 [12, 768], P(None, ('dp', 'seq'))
Inputs may be any that keep to these rules, and one draw needn't show every extreme that they name: `doc_lengths`: each row's 24 lengths sum to 1024.
All inputs are finite; a program needn't handle non-finite values.
Results may differ from a plain program's by a relative error of at most 0.0083.
Values may be sent and summed in bfloat16 or wider, within the bound.
No kernel may reach another device: no remote copies, remote signals or barrier semaphores. Data moves between devices by JAX's collectives and lax.ppermute only.
A program may use at most 320 MiB of HBM per device.

v0:
```python
import functools

import jax
import jax.numpy as jnp
import numpy as np
from jax import lax
from jax.experimental import pallas as pl
from jax.experimental.pallas import tpu as pltpu
from jax.sharding import PartitionSpec as P

HEADS = 12
STEP = 10
NORM_EPS = 1e-05
MASK_FILL = -1e30
DISTILL = 0.5
CLIP_LEVEL = 1.0
BETA_ONE = 0.9
BETA_TWO = 0.999
ADAM_EPS = 1e-08
DECAY = 0.01
RATE_MATRIX = 0.05
RATE_VECTOR = 0.5

LANES = 128
CHIPS = 16
SLAB = 48
VMEM_BYTES = 60 * 1024 * 1024
F32 = jnp.float32
BF16 = jnp.bfloat16
INV_SQRT2 = 0.7071067811865476
INV_SQRT_2PI = 0.3989422804014327
GATHER_Z = (0, 2, 1, 3)
PLACES = [(x, y, z) for x in range(2) for y in range(2) for z in GATHER_Z]


def params(rank):
    return pltpu.CompilerParams(
        dimension_semantics=("arbitrary",) * rank,
        vmem_limit_bytes=VMEM_BYTES,
    )


def cost(flops, nbytes, trans=0):
    return pl.CostEstimate(flops=int(flops), bytes_accessed=int(nbytes), transcendentals=int(trans))


def dot(a, b):
    return lax.dot_general(a, b, (((1,), (0,)), ((), ())), preferred_element_type=F32)


def dot_nt(a, b):
    return lax.dot_general(a, b, (((1,), (1,)), ((), ())), preferred_element_type=F32)


def dot_tn(a, b):
    return lax.dot_general(a, b, (((0,), (0,)), ((), ())), preferred_element_type=F32)


def swap(x, axis, bit):
    return lax.ppermute(x, axis, [(i, i ^ bit) for i in range(lax.axis_size(axis))])


def after(x, *deps):
    return lax.optimization_barrier((x, *deps))[0]


def stage(*parts):
    return list(lax.optimization_barrier(parts))


def split_core(mine, got):
    total = mine + got.astype(F32)
    kept = (total[0, 0], total[1, 0, 2:], total[0, 1, :2])
    over_x = jnp.stack([total[1, 1, :2], total[1, 0, :2]]).astype(BF16)
    over_y = jnp.stack([total[1, 1, 2:], total[0, 1, 2:]]).astype(BF16)
    return kept, over_x, over_y


def add_first(kept, got_x, got_y):
    near, next_x, next_y = kept
    got_x, got_y = got_x.astype(F32), got_y.astype(F32)
    near = (near[:2] + got_x[1], near[2:] + got_y[1])
    return near, (next_x + got_y[0]).astype(BF16), (next_y + got_x[0]).astype(BF16)


def add_second(near, got_x, got_y):
    front = near[0] + got_y.astype(F32)
    back = near[1] + got_x.astype(F32)
    return jnp.stack([front[0], back[0]]), jnp.stack([front[1], back[1]]).astype(BF16)


def add_z(near, got):
    return near[0] + got[0].astype(F32), (near[1] + got[1].astype(F32)).astype(BF16)


JOINT_PARTS = ((0, 4, 0), (4, 4, 0), (8, 4, 0), (12, 4, 0), (0, 12, 1), (12, 4, 1))
REST_PARTS = tuple((f, n, o) for o in range(2) for f, n in ((0, 4), (4, 4), (8, 4), (12, 2), (14, 2)))


def slab_copies(meta, parts, sources, dest, sems, row_base, rows, cols, col_base, sem_base):
    copies = []
    for (first, count, other), source in zip(parts, sources):
        half = jnp.bitwise_xor(meta[0], other)
        for z in range(count):
            chip = meta[4 + first + z]
            copies.append(
                pltpu.make_async_copy(
                    source.at[z, pl.ds(row_base, rows), pl.ds(0, cols)],
                    dest.at[
                        pl.ds(pl.multiple_of(chip * rows, 16), rows),
                        pl.ds(pl.multiple_of(col_base(half), LANES), cols),
                    ],
                    sems.at[sem_base + len(copies)],
                )
            )
    return copies


def start_all(copies):
    for c in copies:
        c.start()


def wait_all(copies):
    for c in copies:
        c.wait()


def project_kernel(blocks, steps, meta, need, *refs):
    total = len(blocks)
    slabs = refs[total : total + len(JOINT_PARTS)]
    bias, q_ref, k_ref, v_ref, w_ref, sems = refs[total + len(JOINT_PARTS) :]
    width = q_ref.shape[-1]
    half_cols = w_ref.shape[1] // 2
    step = pl.program_id(0)

    @pl.when(step == 0)
    def _():
        copies = slab_copies(
            meta, JOINT_PARTS, slabs, w_ref, sems, 0, SLAB, half_cols, lambda h: h * half_cols, 0
        )
        start_all(copies)
        wait_all(copies)

    row = step % steps * 2
    for at, (d, first, count) in enumerate(blocks):
        here = (step >= first) & (step < first + count)

        @pl.when(here & (need[row, d] + need[row + 1, d] > 0))
        def _(d=d, at=at):
            x = refs[at][...]
            k_ref[0] = dot(x, w_ref[:, width : 2 * width]).astype(BF16)
            v_ref[0] = (dot(x, w_ref[:, 2 * width :]) + bias[1:2, :]).astype(BF16)
            if d == 0:
                q = dot(x, w_ref[:, :width]) + bias[0:1, :]
                q_ref[...] = q.astype(BF16) * jnp.asarray((width // HEADS) ** -0.5, BF16)


def project(meta, need, xs, slabs, vec, deps):
    width = xs[0][0].shape[1]
    tokens = xs[0][0].shape[0]
    blocks = len(xs)
    steps = need.shape[0] // 2
    size = tokens // steps
    pieces, spans = [], []
    for d, block in enumerate(xs):
        at = d * steps
        for x in block:
            pieces.append(x)
            spans.append((d, at, x.shape[0] // size))
            at += x.shape[0] // size

    def x_spec(first, count):
        return pl.BlockSpec((size, width), lambda i, *_: (jnp.clip(i - first, 0, count - 1), 0))

    hbm = pl.BlockSpec(memory_space=pl.ANY)
    kv_spec = pl.BlockSpec((1, size, width), lambda i, *_: (i // steps, i % steps, 0))
    kv_shape = jax.ShapeDtypeStruct((blocks, tokens, width), BF16)
    return pl.pallas_call(
        skipping(
            functools.partial(project_kernel, spans, steps), len(pieces) + len(slabs) + 3, len(deps)
        ),
        grid_spec=pltpu.PrefetchScalarGridSpec(
            num_scalar_prefetch=2,
            grid=(blocks * steps,),
            in_specs=[x_spec(first, count) for _, first, count in spans]
            + [hbm] * len(slabs)
            + [pl.BlockSpec(vec.shape, lambda i, *_: (0, 0))]
            + [hbm] * len(deps),
            out_specs=[
                pl.BlockSpec((size, width), lambda i, *_: (jnp.minimum(i, steps - 1), 0)),
                kv_spec,
                kv_spec,
                pl.BlockSpec((width, 3 * width), lambda i, *_: (0, 0)),
            ],
            scratch_shapes=[pltpu.SemaphoreType.DMA((2 * CHIPS,))],
        ),
        out_shape=[
            jax.ShapeDtypeStruct((tokens, width), BF16),
            kv_shape,
            kv_shape,
            jax.ShapeDtypeStruct((width, 3 * width), BF16),
        ],
        compiler_params=params(1),
        cost_estimate=cost(
            2 * tokens * width * width * (2 * blocks + 1), 4 * blocks * tokens * width
        ),
        name="project",
    )(meta, need, *pieces, *slabs, vec, *deps)


def share_kernel(start, teach_ref, segq_ref, segk_ref, out_ref, mask_scr):
    length, keys = mask_scr.shape

    @pl.when(pl.program_id(1) == 0)
    def _():
        same = spread(segq_ref[0], keys) == segk_ref[0, 0:1, :]
        mask_scr[...] = jnp.where(same, 1.0, 0.0).astype(BF16)

    ones = jnp.ones((keys, LANES), BF16)
    for pair in range(out_ref.shape[1]):
        sums = [dot(teach_ref[0, 2 * pair + h] * mask_scr[...], ones) for h in range(2)]
        out_ref[0, pair] = DISTILL / pick_lanes(sums[0], sums[1])


def share(teacher, segq, seg_row, start, count, deps):
    _, heads, length, keys = teacher.shape
    return pl.pallas_call(
        skipping(functools.partial(share_kernel, start), 3, len(deps)),
        grid=(count, 2),
        in_specs=[
            pl.BlockSpec((1, heads // 2, length, keys), lambda r, p: (r + start, p, 0, 0)),
            pl.BlockSpec((1, length, LANES), lambda r, p: (r + start, 0, 0)),
            pl.BlockSpec((1, 8, keys), lambda r, p: (r + start, 0, 0)),
        ]
        + [pl.BlockSpec(memory_space=pl.ANY)] * len(deps),
        out_specs=pl.BlockSpec((1, heads // 4, length, LANES), lambda r, p: (r, p, 0, 0)),
        scratch_shapes=[pltpu.VMEM((length, keys), BF16)],
        out_shape=jax.ShapeDtypeStruct((count, heads // 2, length, LANES), F32),
        compiler_params=params(2),
        cost_estimate=cost(4 * count * heads * length * keys, 2 * count * heads * length * keys),
        name="share",
    )(teacher, segq, seg_row, *deps)


def head_parts(x):
    lane = lax.broadcasted_iota(jnp.int32, x.shape, 1)
    zero = jnp.zeros_like(x)
    first = lane < LANES // 2
    return (jnp.where(first, x, zero), jnp.where(first, zero, x))


def pick_lanes(a, b):
    lane = lax.broadcasted_iota(jnp.int32, (a.shape[0], LANES), 1)
    return jnp.where(lane < LANES // 2, a, b)


def spread(x, length):
    return x if length == LANES else jnp.concatenate([x] * (length // LANES), axis=1)


def fold(x, op):
    out = x[:, :LANES]
    for i in range(1, x.shape[1] // LANES):
        out = op(out, x[:, i * LANES : (i + 1) * LANES])
    return out


def fill_bias(plan, r, blocks, length, segq_ref, segk_ref, bias_scr, mask_scr):
    seg_q = spread(segq_ref[0], length)
    for j in range(blocks):

        @pl.when(plan[r, 0] > j)
        def _(j=j):
            d = plan[r, 1 + j]
            same = seg_q == segk_ref[d, 0, 0:1, :]
            bias_scr[d] = jnp.where(same, 0.0, MASK_FILL)
            if mask_scr is not None:
                mask_scr[d] = jnp.where(same, 1.0, 0.0).astype(BF16)


def skipping(kernel, first, count):
    def run(*refs):
        kernel(*refs[:first], *refs[first + count :])

    return run


def attend_kernel(
    blocks, start, plan, q_ref, k_ref, v_ref, segq_ref, segk_ref, o_ref, lse_ref, bias_scr
):
    r = pl.program_id(0) + start
    length = q_ref.shape[1]

    @pl.when(pl.program_id(1) == 0)
    def _():
        fill_bias(plan, r, blocks, length, segq_ref, segk_ref, bias_scr, None)

    for count in range(1, blocks + 1):

        @pl.when(plan[r, 0] == count)
        def _(count=count):
            for pair in range(q_ref.shape[2] // LANES):
                lanes = slice(pair * LANES, (pair + 1) * LANES)
                q_heads = head_parts(q_ref[0, :, lanes])
                outs, logs = [], []
                for h in range(2):
                    scores = []
                    for j in range(count):
                        d = plan[r, 1 + j]
                        scores.append(dot_nt(q_heads[h], k_ref[d, 0, :, lanes]) + bias_scr[d])
                    top = fold(functools.reduce(jnp.maximum, scores), jnp.maximum)
                    top = jnp.max(top, axis=1, keepdims=True)
                    total = acc = None
                    for j in range(count):
                        d = plan[r, 1 + j]
                        e = jnp.exp(scores[j] - top)
                        part = fold(e, jnp.add)
                        out = dot(e.astype(BF16), v_ref[d, 0, :, lanes])
                        total = part if j == 0 else total + part
                        acc = out if j == 0 else acc + out
                    total = jnp.sum(total, axis=1, keepdims=True)
                    outs.append(acc * (1.0 / total))
                    logs.append(jnp.broadcast_to(top + jnp.log(total), (length, LANES)))
                o_ref[0, :, lanes] = pick_lanes(outs[0], outs[1]).astype(BF16)
                lse_ref[0, pair] = pick_lanes(logs[0], logs[1])


def attend(plan, q, k, v, segq, segk, start, count, before, deps):
    blocks, rows, length, width = k.shape
    pairs = width // LANES
    group = 2
    lanes = group * LANES
    extra = (*before, *deps)
    kv_spec = pl.BlockSpec((blocks, 1, length, lanes), lambda r, p, *_: (0, r + start, 0, p))
    tok_spec = pl.BlockSpec((1, length, lanes), lambda r, p, *_: (r + start, 0, p))
    return pl.pallas_call(
        skipping(functools.partial(attend_kernel, blocks, start), 6, len(extra)),
        grid_spec=pltpu.PrefetchScalarGridSpec(
            num_scalar_prefetch=1,
            grid=(count, pairs // group),
            in_specs=[
                tok_spec,
                kv_spec,
                kv_spec,
                pl.BlockSpec((1, length, LANES), lambda r, p, *_: (r + start, 0, 0)),
                pl.BlockSpec((blocks, 1, 8, length), lambda r, p, *_: (0, r + start, 0, 0)),
            ]
            + [pl.BlockSpec(memory_space=pl.ANY)] * len(extra),
            out_specs=[
                tok_spec,
                pl.BlockSpec((1, group, length, LANES), lambda r, p, *_: (r + start, p, 0, 0)),
            ],
            scratch_shapes=[pltpu.VMEM((blocks, length, length), F32)],
        ),
        out_shape=[
            jax.ShapeDtypeStruct((rows, length, width), BF16),
            jax.ShapeDtypeStruct((rows, pairs, length, LANES), F32),
        ],
        input_output_aliases={6 + i: i for i in range(len(before))},
        compiler_params=params(2),
        cost_estimate=cost(16 * count * length * length * blocks * width, k.size),
        name="attend",
    )(plan, q, k, v, segq, segk, *extra)


def attend_back_kernel(
    blocks, start, meta, plan, q_ref, k_ref, v_ref, do_ref, o_ref, lse_ref, share_ref, teach_ref,
    segq_ref, segk_ref, dq_ref, dk_ref, dv_ref, bias_scr, mask_scr
):
    r = pl.program_id(0) + start
    length = q_ref.shape[1]
    head_dim = LANES // 2
    seq_rank = meta[3]

    @pl.when(pl.program_id(1) == 0)
    def _():
        fill_bias(plan, r, blocks, length, segq_ref, segk_ref, bias_scr, mask_scr)

    def body(count):
        q = q_ref[0]
        do = do_ref[0]
        q_heads = head_parts(q)
        do_heads = head_parts(do)
        q_turned = q.T
        do_turned = do.T
        o = o_ref[0].astype(F32)
        dk = [[], []]
        dv = [[], []]
        dq = []
        for h in range(2):
            rows = slice(h * head_dim, (h + 1) * head_dim)
            shift = DISTILL - jnp.sum(do_heads[h].astype(F32) * o, axis=1, keepdims=True)
            lse = lse_ref[0, 0][:, h * head_dim : h * head_dim + 1]
            share_h = share_ref[0, 0][:, h * head_dim : h * head_dim + 1]
            for j in range(count):
                d = plan[r, 1 + j]
                k = k_ref[d, 0]
                p = jnp.exp(dot_nt(q_heads[h], k) + bias_scr[d] - lse)
                dp = dot_nt(do_heads[h], v_ref[d, 0])
                place = pl.multiple_of(jnp.bitwise_xor(seq_rank, d) * length, LANES)
                t = (teach_ref[0, h, :, pl.ds(place, length)] * mask_scr[d]).astype(F32)
                ds = (p * (dp + shift) - t * share_h).astype(BF16)
                dv[h].append(dot(do_turned[rows], p.astype(BF16)))
                dk[h].append(dot(q_turned[rows], ds))
                part = dot(ds, k)
                if j == 0:
                    dq.append(part)
                else:
                    dq[h] = dq[h] + part
        for j in range(count):
            d = plan[r, 1 + j]
            dk_ref[d, 0] = jnp.concatenate([dk[0][j], dk[1][j]]).astype(BF16).T
            dv_ref[d, 0] = jnp.concatenate([dv[0][j], dv[1][j]]).astype(BF16).T
        dq_ref[0] = (pick_lanes(dq[0], dq[1]) * head_dim**-0.5).astype(BF16)

    for count in range(1, blocks + 1):
        pl.when(plan[r, 0] == count)(functools.partial(body, count))
    for j in range(1, blocks):

        @pl.when(plan[r, 0] <= j)
        def _(j=j):
            d = plan[r, 1 + j]
            dk_ref[d, 0] = jnp.zeros((length, LANES), BF16)
            dv_ref[d, 0] = jnp.zeros((length, LANES), BF16)


def attend_back(
    meta, plan, q, k, v, d_out, out, lse, shares, teacher, segq, segk, start, count, before, deps
):
    blocks, rows, length, width = k.shape
    pairs = width // LANES
    extra = (*before, *deps)
    per = shares[0].shape[0]
    kv_spec = pl.BlockSpec((blocks, 1, length, LANES), lambda r, p, *_: (0, r + start, 0, p))
    tok_spec = pl.BlockSpec((1, length, LANES), lambda r, p, *_: (r + start, 0, p))
    kv_shape = jax.ShapeDtypeStruct(k.shape, BF16)
    return pl.pallas_call(
        skipping(functools.partial(attend_back_kernel, blocks, start), 12, len(extra)),
        grid_spec=pltpu.PrefetchScalarGridSpec(
            num_scalar_prefetch=2,
            grid=(count, pairs),
            in_specs=[
                tok_spec,
                kv_spec,
                kv_spec,
                tok_spec,
                tok_spec,
                pl.BlockSpec((1, 1, length, LANES), lambda r, p, *_: (r + start, p, 0, 0)),
                pl.BlockSpec((1, 1, length, LANES), lambda r, p, *_: (r + start % per, p, 0, 0)),
                pl.BlockSpec(
                    (1, 2, length, teacher.shape[3]), lambda r, p, *_: (r + start, p, 0, 0)
                ),
                pl.BlockSpec((1, length, LANES), lambda r, p, *_: (r + start, 0, 0)),
                pl.BlockSpec((blocks, 1, 8, length), lambda r, p, *_: (0, r + start, 0, 0)),
            ]
            + [pl.BlockSpec(memory_space=pl.ANY)] * len(extra),
            out_specs=[tok_spec, kv_spec, kv_spec],
            scratch_shapes=[
                pltpu.VMEM((blocks, length, length), F32),
                pltpu.VMEM((blocks, length, length), BF16),
            ],
        ),
        out_shape=[jax.ShapeDtypeStruct(q.shape, BF16), kv_shape, kv_shape],
        input_output_aliases={12 + i: i for i in range(len(before))},
        compiler_params=params(2),
        cost_estimate=cost(40 * count * length * length * blocks * width, 2 * k.size),
        name="attend_back",
    )(
        meta, plan, q, k, v, d_out, out, lse, shares[start // per], teacher, segq, segk, *extra
    )


def norm(values):
    centered = values - jnp.mean(values, axis=1, keepdims=True)
    inverse = lax.rsqrt(jnp.mean(centered * centered, axis=1, keepdims=True) + NORM_EPS)
    return centered * inverse, inverse


def norm_back(upstream, normed, inverse, gain):
    scaled = upstream * gain
    inner = jnp.mean(scaled, axis=1, keepdims=True)
    cross = jnp.mean(scaled * normed, axis=1, keepdims=True)
    return inverse * (scaled - inner - normed * cross)


def colsum(x):
    return jnp.sum(x, axis=0, keepdims=True)


def feed_kernel(
    meta, x_ref, o_ref, cot_ref, vec, fbias, *refs
):
    sources = refs[: len(REST_PARTS)]
    (out_ref, df1_ref, do_ref, gl_ref, du_ref, h1_ref, dz_ref, da_ref, gvec_ref, gbias_ref,
     wo, we, ws, gp_scr, sems) = refs[len(REST_PARTS) :]
    step = pl.program_id(0)
    half_d = wo.shape[1] // 2
    half_f = we.shape[1] // 2

    we_rows = half_f // half_d * SLAB

    def copies_wo():
        return slab_copies(meta, REST_PARTS, sources, wo, sems, we_rows, SLAB, half_d, lambda h: h * half_d, 0)

    def copies_we():
        copies = []
        for k in range(half_f // half_d):
            copies += slab_copies(
                meta, REST_PARTS, sources, we, sems, k * SLAB, SLAB, half_d,
                lambda h, k=k: h * half_f + k * half_d, 2 * CHIPS + len(copies)
            )
        return copies

    def copies_ws():
        return slab_copies(
            meta, REST_PARTS, sources, ws, sems, we_rows + SLAB, ws.shape[0] // CHIPS, half_d,
            lambda h: h * half_d, 2 * CHIPS * (1 + half_f // half_d)
        )

    @pl.when(step == 0)
    def _():
        start_all(copies_wo() + copies_we() + copies_ws())
        gvec_ref[...] = jnp.zeros(gvec_ref.shape, F32)
        gbias_ref[...] = jnp.zeros(gbias_ref.shape, F32)
        wait_all(copies_wo())

    base = 3 + ws.shape[0] // wo.shape[0]
    bias_out = vec[2:3]
    bias_shrink, gain1, shift1, gain2, shift2 = (vec[base + i : base + i + 1] for i in range(5))
    chunk = wo.shape[0]
    chunks = ws.shape[0] // chunk

    branch = dot(o_ref[...], wo[...]) + bias_out
    normed1, inverse1 = norm(x_ref[...].astype(F32) + branch)
    hidden = normed1 * gain1 + shift1
    hidden_low = hidden.astype(BF16)
    h1_ref[...] = hidden_low
    pl.when(step == 0)(lambda: wait_all(copies_we()))
    pl.when(step == 0)(lambda: wait_all(copies_ws()))
    spans = [slice(c * chunk, (c + 1) * chunk) for c in range(chunks)]
    z = None
    for cols in spans:
        u = dot(hidden_low, we[:, cols]) + fbias[0:1, cols]
        phi = 0.5 + 0.5 * lax.erf(u * INV_SQRT2)
        gp_scr[:, cols] = phi + u * (jnp.exp(-0.5 * u * u) * INV_SQRT_2PI)
        gl = (u * phi).astype(BF16)
        gl_ref[:, cols] = gl
        part = dot(gl, ws[cols, :])
        z = part if z is None else z + part
    normed2, inverse2 = norm(hidden + z + bias_shrink)
    out_ref[...] = (normed2 * gain2 + shift2).astype(BF16)
    cot = cot_ref[...].astype(F32)
    gvec_ref[6:7] += colsum(cot * normed2)
    gvec_ref[7:8] += colsum(cot)
    df2 = norm_back(cot, normed2, inverse2, gain2)
    dz = df2.astype(BF16)
    dz_ref[...] = dz
    gvec_ref[3:4] += colsum(df2)
    dh = df2
    for cols in spans:
        du = dot_nt(dz, ws[cols, :]) * gp_scr[:, cols]
        du_low = du.astype(BF16)
        du_ref[:, cols] = du_low
        gbias_ref[0:1, cols] += colsum(du)
        dh = dh + dot_nt(du_low, we[:, cols])
    gvec_ref[4:5] += colsum(dh * normed1)
    gvec_ref[5:6] += colsum(dh)
    df1 = norm_back(dh, normed1, inverse1, gain1)
    df1_ref[...] = df1
    da = df1.astype(BF16)
    da_ref[...] = da
    gvec_ref[2:3] += colsum(df1)
    do_ref[...] = dot_nt(da, wo[...]).astype(BF16)


def feed(meta, x, o, cot, vec, fbias, slabs):
    tokens, width = x.shape
    hidden = fbias.shape[1]
    size = tokens // 4
    tok = pl.BlockSpec((size, width), lambda i, *_: (i, 0))
    wide = pl.BlockSpec((size, hidden), lambda i, *_: (i, 0))
    full = lambda shape: pl.BlockSpec(shape, lambda i, *_: (0, 0))
    hbm = pl.BlockSpec(memory_space=pl.ANY)
    low = jax.ShapeDtypeStruct(x.shape, BF16)
    wide_low = jax.ShapeDtypeStruct((tokens, hidden), BF16)
    return pl.pallas_call(
        feed_kernel,
        grid_spec=pltpu.PrefetchScalarGridSpec(
            num_scalar_prefetch=1,
            grid=(tokens // size,),
            in_specs=[tok, tok, tok, full(vec.shape), full(fbias.shape)] + [hbm] * len(slabs),
            out_specs=[tok, tok, tok, wide, wide, tok, tok, tok, full((8, width)), full((8, hidden))],
            scratch_shapes=[
                pltpu.VMEM((width, width), BF16),
                pltpu.VMEM((width, hidden), BF16),
                pltpu.VMEM((hidden, width), BF16),
                pltpu.VMEM((size, hidden), F32),
                pltpu.SemaphoreType.DMA((32 * (hidden // width + 2),)),
            ],
        ),
        out_shape=[
            low,
            jax.ShapeDtypeStruct(x.shape, F32),
            low,
            wide_low,
            wide_low,
            low,
            low,
            low,
            jax.ShapeDtypeStruct((8, width), F32),
            jax.ShapeDtypeStruct((8, hidden), F32),
        ],
        compiler_params=params(1),
        cost_estimate=cost(
            4 * tokens * width * (width + 2 * hidden), 4 * tokens * (5 * width + hidden)
        ),
        name="feed",
    )(meta, x, o, cot, vec, fbias, *slabs)


def chip_of(meta, x, y, z):
    far_z, far_x, far_y = (jnp.bitwise_xor(meta[20 + i], v) for i, v in enumerate((z, x, y)))
    return (far_z * 2 + far_x) * 2 + far_y


def feed_grad_kernel(added, meta, h1_ref, du_ref, gl_ref, dz_ref, ol_ref, da_ref, *refs):
    got_ref = refs[0] if added else None
    scr = refs[-1]
    step = pl.program_id(0)
    half = dz_ref.shape[1]
    width = 2 * half
    we_rows = 4 * SLAB

    def put(x, y, z, at, rows, part):
        at = pl.ds(at, rows)
        if not added:
            refs[0][x, y, z, at] = part.astype(BF16)
            return
        near, next_x, next_y, over_x, over_y = refs[1:6]
        total = part + got_ref[x, y, z, at].astype(F32)

        def first_half():
            if x == 1:
                over_x[1 - y, z % 2, at] = total.astype(BF16)
            elif y == 1:
                next_y[z % 2, at] = total

        def last_half():
            if y == 1:
                over_y[1 - x, z % 2, at] = total.astype(BF16)
            elif x == 1:
                next_x[z % 2, at] = total

        if x == 0 and y == 0:
            near[z, at] = total
        elif isinstance(z, int):
            first_half() if z < 2 else last_half()
        else:
            pl.when(z < 2)(first_half)
            pl.when(z >= 2)(last_half)

    def put_all(at, cols):
        for x in range(2):
            for y in range(2):
                for z in range(4):
                    first = pl.multiple_of(chip_of(meta, x, y, z) * SLAB, 8)
                    put(x, y, z, at, SLAB, scr[pl.ds(first, SLAB), cols])

    @pl.when(step == 0)
    def _():
        scr[:, :half] = dot_tn(ol_ref[...], da_ref[...])
        put_all(we_rows, slice(0, half))

    for u in range(2):

        @pl.when(step == u)
        def _(u=u):
            scr[...] = dot_tn(h1_ref[...], du_ref[...])
            for k in range(width // half):
                put_all((2 * u + k) * SLAB, slice(k * half, (k + 1) * half))

    @pl.when(step >= 2)
    def _():
        scr[:, :half] = dot_tn(gl_ref[...], dz_ref[...])
        z = jnp.bitwise_xor(meta[20], step - 2)
        for x in range(2):
            for y in range(2):
                chip = jnp.bitwise_xor(meta[21], x) * 2 + jnp.bitwise_xor(meta[22], y)
                first = pl.multiple_of(chip * 4 * SLAB, 8)
                put(x, y, z, we_rows + SLAB, 4 * SLAB, scr[pl.ds(first, 4 * SLAB), :half])


def feed_grad(meta, h1, du, gl, dz, ol, da, got):
    tokens, width = h1.shape
    half = width // 2
    wide = lambda index: pl.BlockSpec((tokens, width), index)
    added = got is not None
    slab = (9 * SLAB, half)
    every = (2, 2, 4)
    if added:
        outs = [((4,), F32), ((2,), F32), ((2,), F32), ((2, 2), BF16), ((2, 2), BF16)]
    else:
        outs = [(every, BF16)]
    slab_spec = lambda lead: pl.BlockSpec(lead + slab, lambda u, m: (0,) * (len(lead) + 2))
    return pl.pallas_call(
        functools.partial(feed_grad_kernel, added),
        grid_spec=pltpu.PrefetchScalarGridSpec(
            num_scalar_prefetch=1,
            grid=(6,),
            in_specs=[
                wide(lambda u, m: (0, 0)),
                wide(lambda u, m: (0, 2 * m[0] + jnp.minimum(u, 1))),
                wide(lambda u, m: (0, jnp.clip(u - 2, 0, 3))),
                pl.BlockSpec((tokens, half), lambda u, m: (0, m[0])),
                wide(lambda u, m: (0, 0)),
                pl.BlockSpec((tokens, half), lambda u, m: (0, m[0])),
            ]
            + [slab_spec(every)] * added,
            out_specs=[slab_spec(lead) for lead, _ in outs],
            scratch_shapes=[pltpu.VMEM((width, width), F32)],
        ),
        out_shape=[jax.ShapeDtypeStruct(lead + slab, dtype) for lead, dtype in outs],
        compiler_params=params(1),
        cost_estimate=cost(9 * tokens * width * width, 16 * tokens * width),
        name="feed_grad",
    )(meta, h1, du, gl, dz, ol, da, *((got,) if added else ()))


def token_grad_kernel(steps, sent, kept, meta, need, dk_ref, dv_ref, w_ref, *refs):
    step = pl.program_id(0)
    row = step % steps * 2
    width = w_ref.shape[0]
    blocks = sent + kept
    for i, d in enumerate(blocks):
        out_ref = refs[-2] if i < len(sent) and kept else refs[-1]
        wanted = need[row, d] + need[row + 1, d]

        @pl.when((step // steps == i) & (wanted > 0))
        def _(d=d, out_ref=out_ref):
            out = dot_nt(dk_ref[0], w_ref[:, width : 2 * width])
            out = out + dot_nt(dv_ref[0], w_ref[:, 2 * width :])
            if d == 0:
                dq_ref, df1_ref = refs[:2]
                out = out + dot_nt(dq_ref[...], w_ref[:, :width]) + df1_ref[...]
            out_ref[0] = out.astype(out_ref.dtype)

        if d > 0:

            @pl.when((step // steps == i) & (wanted == 0))
            def _(out_ref=out_ref):
                out_ref[0] = jnp.zeros(out_ref.shape[1:], out_ref.dtype)


def token_grad(meta, need, dk, dv, w, sent, kept, extra, dtype, deps=()):
    _, tokens, width = dk.shape
    steps = need.shape[0] // 2
    size = tokens // steps
    blocks = sent + kept

    def block_of(i):
        d = jnp.int32(blocks[0])
        for at, b in enumerate(blocks):
            d = jnp.where(i // steps == at, b, d)
        return d

    kv_spec = pl.BlockSpec((1, size, width), lambda i, *_: (block_of(i), i % steps, 0))

    def out_spec(first, count):
        def index(i, *_):
            at = jnp.clip(i - first * steps, 0, count * steps - 1)
            return (at // steps, at % steps, 0)

        return pl.BlockSpec((1, size, width), index)

    groups = [(0, len(sent))] + ([(len(sent), len(kept))] if kept else [])
    return pl.pallas_call(
        skipping(
            functools.partial(token_grad_kernel, steps, sent, kept), 5 + len(extra), len(deps)
        ),
        grid_spec=pltpu.PrefetchScalarGridSpec(
            num_scalar_prefetch=2,
            grid=(len(blocks) * steps,),
            in_specs=[kv_spec, kv_spec, pl.BlockSpec(w.shape, lambda i, *_: (0, 0))]
            + [pl.BlockSpec((size, width), lambda i, *_: (i, 0)) for _ in extra]
            + [pl.BlockSpec(memory_space=pl.ANY)] * len(deps),
            out_specs=[out_spec(*g) for g in groups],
        ),
        out_shape=[jax.ShapeDtypeStruct((n, tokens, width), dtype) for _, n in groups],
        compiler_params=params(1),
        cost_estimate=cost(
            4 * len(blocks) * tokens * width * width, 6 * len(blocks) * tokens * width
        ),
        name="token_grad",
    )(meta, need, dk, dv, w, *extra, *deps)


def joint_grad_kernel(counts, meta, *refs):
    blocks = len(counts)
    starts = np.cumsum((0,) + counts)
    dq_ref, dk_ref, dv_ref, mine_ref, theirs_ref, sum_ref, acc = refs[starts[-1] :]
    step = pl.program_id(0)
    width = acc.shape[0]
    half = acc.shape[1] // 2

    for d in range(blocks):

        @pl.when(step == d)
        def _(d=d):
            x = [ref[...].T for ref in refs[starts[d] : starts[d + 1]]]
            x = x[0] if len(x) == 1 else jnp.concatenate(x, axis=1)
            k_part = dot(x, dk_ref[0])
            v_part = dot(x, dv_ref[0])
            v_sum = colsum(dv_ref[0].astype(F32))
            if d == 0:
                acc[:, :width] = dot(x, dq_ref[...])
                acc[:, width : 2 * width] = k_part
                acc[:, 2 * width :] = v_part
                sum_ref[0:1] = colsum(dq_ref[...].astype(F32))
                sum_ref[1:2] = v_sum
            else:
                acc[:, width : 2 * width] += k_part
                acc[:, 2 * width :] += v_part
                sum_ref[1:2] += v_sum

    @pl.when(step == blocks - 1)
    def _():
        mine = pl.ds(pl.multiple_of(meta[0] * half, LANES), half)
        theirs = pl.ds(pl.multiple_of((1 - meta[0]) * half, LANES), half)
        for x in range(2):
            for y in range(2):
                for z in range(4):
                    part = pl.ds(pl.multiple_of(chip_of(meta, x, y, z) * SLAB, 8), SLAB)
                    mine_ref[x, y, z] = acc[part, mine]
                    theirs_ref[x, y, z] = acc[part, theirs].astype(BF16)


def joint_grad(meta, xs, dq, dk, dv, deps):
    blocks = len(xs)
    counts = tuple(len(x) for x in xs)
    pieces = [piece for x in xs for piece in x]
    tokens, width = dq.shape
    half = 3 * width // 2
    full = pl.BlockSpec((tokens, width), lambda i, *_: (0, 0))
    kv_spec = pl.BlockSpec((1, tokens, width), lambda i, *_: (i, 0, 0))
    shape = (2, 2, 4, SLAB, half)
    slab_spec = pl.BlockSpec(shape, lambda i, *_: (0, 0, 0, 0, 0))
    return pl.pallas_call(
        skipping(functools.partial(joint_grad_kernel, counts), len(pieces) + 4, len(deps)),
        grid_spec=pltpu.PrefetchScalarGridSpec(
            num_scalar_prefetch=1,
            grid=(blocks,),
            in_specs=[pl.BlockSpec(x.shape, lambda i, *_: (0, 0)) for x in pieces]
            + [full, kv_spec, kv_spec]
            + [pl.BlockSpec(memory_space=pl.ANY)] * len(deps),
            out_specs=[slab_spec, slab_spec, pl.BlockSpec((8, width), lambda i, *_: (0, 0))],
            scratch_shapes=[pltpu.VMEM((width, 3 * width), F32)],
        ),
        out_shape=[
            jax.ShapeDtypeStruct(shape, F32),
            jax.ShapeDtypeStruct(shape, BF16),
            jax.ShapeDtypeStruct((8, width), F32),
        ],
        compiler_params=params(1),
        cost_estimate=cost(
            2 * tokens * width * width * (2 * blocks + 1), 8 * blocks * tokens * width
        ),
        name="joint_grad",
    )(meta, *pieces, dq, dk, dv, *deps)


def segment_ids(doc_lengths, total):
    doc_ends = jnp.cumsum(doc_lengths, axis=-1, dtype=jnp.int32)
    places = jnp.arange(total, dtype=jnp.int32)
    return jnp.sum(
        (doc_ends[:, None, :] <= places[None, :, None]).astype(jnp.int32), axis=-1, dtype=jnp.int32
    )


def adam_step(gradient, master, mean_old, square_old, rate, decay):
    momentum = BETA_ONE * mean_old + (1.0 - BETA_ONE) * gradient
    variance = BETA_TWO * square_old + (1.0 - BETA_TWO) * gradient * gradient
    update = (
        momentum / (1.0 - BETA_ONE**STEP) / (jnp.sqrt(variance / (1.0 - BETA_TWO**STEP)) + ADAM_EPS)
    )
    return (master - rate * (update + decay * master), momentum, variance)


def documents(doc_lengths, seq_rank, seq_count, rows, length):
    segments = segment_ids(doc_lengths, length * seq_count).reshape(rows, seq_count, length)
    seg_rel = jnp.take(segments, jnp.arange(seq_count) ^ seq_rank, axis=1)
    need = (
        (seg_rel[:, :, 0] <= seg_rel[:, :1, -1]) & (seg_rel[:, :, -1] >= seg_rel[:, :1, 0])
    ).astype(jnp.int32)
    segq = jnp.broadcast_to(seg_rel[:, 0, :, None], (rows, length, LANES))
    segk = jnp.broadcast_to(
        seg_rel.transpose(1, 0, 2)[:, :, None, :], (seq_count, rows, 8, length)
    )
    seg_row = jnp.broadcast_to(segments.reshape(rows, 1, -1), (rows, 8, length * seq_count))
    rank_in = jnp.cumsum(need, axis=1)
    slots = jnp.where(need > 0, rank_in - 1, rank_in[:, -1:] + jnp.cumsum(1 - need, axis=1) - 1)
    spots = slots[:, None, :] == jnp.arange(seq_count)[None, :, None]
    order = jnp.sum(spots * jnp.arange(seq_count)[None, None, :], axis=2)
    plan = jnp.concatenate([rank_in[:, -1:], order], axis=1).astype(jnp.int32)
    return seg_row, need, plan, segq, segk


def own_part(x, index, axis):
    return lax.dynamic_index_in_dim(x, index, axis, keepdims=False)


def both_halves(own, other, core, axis=-1):
    first = jnp.where(core == 0, own, other)
    second = jnp.where(core == 0, other, own)
    return jnp.concatenate([first, second], axis=axis)


def full_slabs(w, row_groups):
    rows, cols = w.shape
    half = cols // 2
    out = []
    for h in range(2):
        s = w[:, h * half : (h + 1) * half].reshape(4, 2, 2, rows // CHIPS, half)
        s = s.transpose(1, 2, 0, 3, 4)
        if row_groups > 1:
            s = s.reshape(2, 2, 4, rows // CHIPS, row_groups, half // row_groups)
            s = s.transpose(0, 1, 2, 4, 3, 5).reshape(2, 2, 4, -1, half // row_groups)
        out.append(s)
    return out


def slab_list(halves, parts):
    order = np.asarray(GATHER_Z)
    every = [jnp.concatenate([h[x, y][order] for x in range(2) for y in range(2)]) for h in halves]
    return [every[other][first : first + count] for first, count, other in parts]


def full_weight(halves, row_groups):
    out = []
    for s in halves:
        _, _, _, rows, cols = s.shape
        s = s.reshape(2, 2, 4, row_groups, rows // row_groups, cols)
        s = s.transpose(2, 0, 1, 4, 3, 5)
        out.append(s.reshape(CHIPS * rows // row_groups, row_groups * cols))
    return jnp.concatenate(out, axis=1)


def local(
    tokens,
    doc_lengths,
    teacher,
    cotangent,
    joint_weight,
    output_weight,
    expand_weight,
    shrink_weight,
    vectors,
    joint_mean,
    output_mean,
    expand_mean,
    shrink_mean,
    vector_mean,
    joint_square,
    output_square,
    expand_square,
    shrink_square,
    vector_square,
):
    seq_count = lax.axis_size("seq")
    dp_count = lax.axis_size("dp")
    seq_rank = lax.axis_index("seq")
    dp_rank = lax.axis_index("dp")
    rows, length, width = tokens.shape
    hidden = expand_weight.shape[1]
    spare = hidden // width
    token_total = rows * length
    shard_rows = joint_weight.shape[0]
    half = width // 2
    by_slabs = dp_count == 8 and seq_count == 4 and 2 * shard_rows == SLAB
    core = seq_rank % 2

    if by_slabs:
        me_z, me_x, me_y, my_half = dp_rank // 2, dp_rank % 2, seq_rank // 2, core
    else:
        me_z = me_x = me_y = my_half = jnp.zeros((), jnp.int32)
    places = [
        ((me_z ^ z) * 2 + (me_x ^ x)) * 2 + (me_y ^ y) for (x, y, z) in PLACES
    ]
    zero = jnp.zeros((), jnp.int32)
    meta = jnp.stack(
        [my_half, zero, zero, seq_rank, *places, me_z, me_x, me_y]
    ).astype(jnp.int32)
    meta_other = meta.at[0].set(1 - my_half)
    if by_slabs:
        low = joint_weight.astype(BF16)
        vec_low = jnp.pad(vectors.astype(BF16).T, ((0, 0), (0, LANES - vectors.shape[0])))
        joint_halves = low.reshape(shard_rows, 2, -1).transpose(1, 0, 2)
        joint_own = jnp.concatenate([own_part(joint_halves, core, 0), vec_low], axis=1)
        joint_send = jnp.concatenate([own_part(joint_halves, 1 - core, 0), vec_low], axis=1)
        joint_got = swap(joint_send, "seq", 1)
        joint_piece = jnp.where(
            core == 0,
            jnp.concatenate([joint_own, joint_got]),
            jnp.concatenate([joint_got, joint_own]),
        )
        lengths = after(doc_lengths, joint_piece)
        docs = documents(lengths, seq_rank, seq_count, rows, length)
        seg_row, need, plan, segq, segk = docs
        lot = rows // 2
        tokens_y = [swap(after(tokens[:lot], joint_piece), "seq", 2)]
        tokens_core = swap(after(tokens, joint_piece), "seq", 1)
        joint_pair = jnp.stack([joint_piece, swap(joint_piece, "dp", 4)])
        rest_weights = after((expand_weight, output_weight, shrink_weight), joint_piece)
        expand_low, output_low, shrink_low = (w.astype(BF16) for w in rest_weights)
        expand_halves = expand_low.reshape(shard_rows, 2, spare, half)
        expand_halves = expand_halves.transpose(1, 2, 0, 3).reshape(2, spare * shard_rows, half)
        output_halves = output_low.reshape(shard_rows, 2, half).transpose(1, 0, 2)
        shrink_halves = shrink_low.reshape(-1, 2, half).transpose(1, 0, 2)
        rest = jnp.concatenate([expand_halves, output_halves, shrink_halves], axis=1)
        rest_own = own_part(rest, core, 0)
        rest_got = swap(own_part(rest, 1 - core, 0), "seq", 1)
        pair = jnp.where(
            core == 0, jnp.stack([rest_own, rest_got]), jnp.stack([rest_got, rest_own])
        )
        cut = spare * shard_rows
        expand_piece = pair[:, :cut].reshape(2, spare, shard_rows, half)
        rest_piece = jnp.concatenate(
            [
                expand_piece.transpose(1, 0, 2, 3).reshape(-1, half),
                pair[:, cut : cut + shard_rows].reshape(-1, half),
                pair[:, cut + shard_rows :].reshape(-1, half),
            ]
        )
        joint_z = jnp.concatenate([joint_pair, swap(joint_pair, "dp", 2)])
        joint_z, rest_piece, tokens_core, tokens_y[0] = stage(
            joint_z, rest_piece, tokens_core, tokens_y[0]
        )
        shares = [share(teacher, segq, seg_row, 0, 2, (joint_z,))]
        joint_y, joint_x, rest_got, shares[0] = stage(
            swap(joint_z, "seq", 2),
            swap(joint_z, "dp", 1),
            swap(rest_piece, "dp", 4),
            shares[0],
        )
        rest_pair = jnp.stack([rest_piece, rest_got])
        shares.append(share(teacher, segq, seg_row, 2, 2, (joint_x, joint_y, shares[0])))
        tokens_far = [swap(after(tokens_y[0], joint_x), "seq", 1)]
        tokens_y.append(swap(after(tokens[lot:], joint_y), "seq", 2))
        rest_got = swap(rest_pair, "dp", 2)
        joint_xy, tokens_far[0], core_zyx, shares[1] = stage(
            swap(joint_y, "dp", 1),
            tokens_far[0],
            swap(jnp.concatenate([joint_z, joint_y, joint_x]), "seq", 1),
            shares[1],
        )
        core_xy, rest_got, tokens_y[1] = stage(
            swap(joint_xy, "seq", 1), rest_got, tokens_y[1]
        )
        tokens_far.append(swap(tokens_y[1], "seq", 1))
        got = {0: [tokens], 1: [tokens_core], 2: tokens_y, 3: tokens_far}
        joint_slabs = [joint_z, joint_y, joint_x, joint_xy, core_zyx, core_xy]
        rest_z = jnp.concatenate([rest_pair, rest_got])
        rest_y = swap(rest_z, "seq", 2)
        rest_x = swap(rest_z, "dp", 1)
        vec_slabs = jnp.stack([t[..., -LANES:] for t in joint_slabs[:4]])
        vec_slabs = vec_slabs.reshape(CHIPS, SLAB, LANES)
        spots = np.argsort([(z * 2 + x) * 2 + y for (x, y, z) in PLACES])
        me_chip = (me_z * 2 + me_x) * 2 + me_y
        order = jnp.asarray(spots, jnp.int32)[jnp.arange(CHIPS, dtype=jnp.int32) ^ me_chip]
        vec_f = jnp.take(vec_slabs, order, axis=0).reshape(width, LANES).T[: vectors.shape[0]]
    else:
        joint_full, output_full, expand_full, shrink_full = (
            lax.all_gather(w.astype(BF16), ("dp", "seq"), axis=0, tiled=True)
            for w in (joint_weight, output_weight, expand_weight, shrink_weight)
        )
        vec_f = lax.all_gather(vectors.astype(BF16), ("dp", "seq"), axis=1, tiled=True)
        joint_parts = full_slabs(joint_full, 1)
        joint_slabs = slab_list(joint_parts, JOINT_PARTS)
        rest_parts = [
            jnp.concatenate(p, axis=3)
            for p in zip(
                full_slabs(expand_full, spare), full_slabs(output_full, 1), full_slabs(shrink_full, 1)
            )
        ]
        rest_slabs = slab_list(rest_parts, REST_PARTS)
    vec_f = vec_f.astype(F32)
    vec_pad = jnp.pad(vec_f, ((0, -vec_f.shape[0] % 8), (0, 0)))
    fbias = jnp.broadcast_to(vec_f[3 : 3 + spare].reshape(1, hidden), (8, hidden))

    bits = [1 << i for i in range(seq_count.bit_length() - 1)]
    if not by_slabs:
        docs = documents(doc_lengths, seq_rank, seq_count, rows, length)
        seg_row, need, plan, segq, segk = docs
        got = {0: [tokens]}
        for bit in reversed(bits):
            for d, block in list(got.items()):
                got[d | bit] = [swap(block[0], "seq", bit)]
    flat = lambda t: t.reshape(-1, t.shape[-1])
    xs = [[flat(x) for x in got[d]] for d in range(seq_count)]

    bias_qv = jnp.pad(vec_f[:2], ((0, 6), (0, 0)))
    by_rows = lambda t: t.reshape(*t.shape[:-2], rows, length, width)
    if not by_slabs:
        shares = [share(teacher, segq, seg_row, r, 1, ()) for r in range(rows)]
    q_flat, k_flat, v_flat, joint_w = project(
        meta, need, xs, joint_slabs, bias_qv, tuple(shares[-1:])
    )
    q, k, v = by_rows(q_flat), by_rows(k_flat), by_rows(v_flat)
    cut = rows // 2
    front = attend(plan, q, k, v, segq, segk, 0, cut, (), ())
    if by_slabs:
        rest_y, rest_x, _ = stage(rest_y, rest_x, front[0])
        rest_slabs = [rest_z, rest_y, rest_x]
        far = [swap(rest_y[:2], "dp", 1), swap(rest_x[2:], "seq", 2)]
        rest_other = [swap(t, "seq", 1) for t in rest_slabs]
    attended, lse = attend(
        plan, q, k, v, segq, segk, cut, rows - cut, front, (rest_slabs[1], rest_slabs[2])
    )
    if by_slabs:
        far = stage(*far, attended)[:2]
        rest_slabs = rest_slabs + far + rest_other + [swap(t, "seq", 1) for t in far]
    layer_output, d_first, d_att, gl, du, h1, dz, da, gvec, gbias = feed(
        meta, flat(tokens), flat(attended), flat(cotangent), vec_pad, fbias, rest_slabs
    )
    layer_output = by_rows(layer_output)
    grad_args = (h1, du, gl, dz, flat(attended), da)
    rest_theirs = feed_grad(meta_other, *grad_args, None)[0]
    back_args = (
        meta, plan, q, k, v, by_rows(d_att), attended, lse, shares, teacher, segq, segk
    )
    deps = (rest_theirs,)
    if by_slabs:
        rest_got = swap(rest_theirs, "seq", 1)
    grads = tuple(attend_back(*back_args, 0, cut, (), deps))
    deps = ()
    if by_slabs:
        near, next_x, next_y, over_x, over_y = feed_grad(
            meta, *grad_args, after(rest_got, grads[0])
        )
        got_x, got_y = swap(over_x, "dp", 1), swap(over_y, "seq", 2)
        deps = (over_x, over_y)
    grads = tuple(attend_back(*back_args, cut, rows - cut, grads, deps))
    dq, dk, dv = grads
    if not by_slabs:
        nothing = jnp.zeros(rest_theirs.shape, BF16)
        near, next_x, next_y, over_x, over_y = feed_grad(meta, *grad_args, nothing)
        over_x, over_y = over_x.astype(F32), over_y.astype(F32)
        rest_mine = jnp.stack(
            [
                jnp.stack([near, jnp.concatenate([next_y, over_y[1]])]),
                jnp.stack(
                    [jnp.concatenate([over_x[1], next_x]), jnp.concatenate([over_x[0], over_y[0]])]
                ),
            ]
        )
    deps = ()
    if by_slabs:
        got_x, got_y, _ = stage(got_x, got_y, dq)
        rest_near, over_x, over_y = add_first((near, next_x, next_y), got_x, got_y)
        got_x, got_y = swap(over_x, "dp", 1), swap(over_y, "seq", 2)
        deps = (over_x, over_y)
    flat_kv = lambda t: t.reshape(seq_count, token_total, width)
    dq, dk, dv = flat(dq), flat_kv(dk), flat_kv(dv)
    joint_mine, joint_theirs, sums = joint_grad(meta, xs, dq, dk, dv, deps)
    grad_vector = jnp.concatenate(
        [sums[:2], gvec[2:3], gbias[0:1].reshape(spare, width), gvec[3:8]], axis=0
    )
    if by_slabs:
        got_x, got_y, _ = stage(got_x, got_y, sums)
        rest_near, rest_far = add_second(rest_near, got_x, got_y)
        rest_got = swap(rest_far, "dp", 2)
        joint_got = swap(joint_theirs, "seq", 1)
        vector_got = swap(grad_vector, "dp", 1)
    odd = tuple(range(1, seq_count, 2))
    even = tuple(range(2, seq_count, 2))
    deps = (rest_far,) if by_slabs else ()
    sent, kept = token_grad(meta, need, dk, dv, joint_w, odd, even, (), BF16, deps)
    deps = ()
    if by_slabs:
        rest_got, joint_got, vector_got, _ = stage(rest_got, joint_got, vector_got, sent)
        joint_kept, over_x, over_y = split_core(joint_mine, joint_got)
        got_x, got_y = swap(over_x, "dp", 1), swap(over_y, "seq", 2)
        grad_vector = grad_vector + vector_got
        vector_got = swap(grad_vector, "seq", 1)
        rest_near, rest_far = add_z(rest_near, rest_got)
        rest_got = swap(rest_far, "dp", 4)
        deps = (over_x, over_y)
    arrived = swap(sent, "seq", 1)
    own_grad = token_grad(meta, need, dk, dv, joint_w, (0,), (), (dq, d_first), F32, deps)[0]
    if by_slabs:
        arrived, got_x, got_y, vector_got, _ = stage(arrived, got_x, got_y, vector_got, own_grad)
        grad_vector = grad_vector + vector_got
    held = {0: own_grad[0] + arrived[0].astype(F32)}
    for i, d in enumerate(even):
        held[d] = (kept[i].astype(F32) + arrived[i + 1].astype(F32)).astype(BF16)
    if by_slabs:
        joint_near, over_x, over_y = add_first(joint_kept, got_x, got_y)
        got_x, got_y, rest_got, vector_got, held[2] = stage(
            swap(over_x, "dp", 1), swap(over_y, "seq", 2), rest_got, swap(grad_vector, "seq", 2),
            held[2],
        )
        joint_near, joint_far = add_second(joint_near, got_x, got_y)
        rest_sum = rest_near + rest_got.astype(F32)
        grad_vector = grad_vector + vector_got
        tokens_got = swap(held.pop(2), "seq", 2)
        cut = spare * SLAB
        expand_sum = rest_sum[:cut].reshape(spare, 2, shard_rows, half).transpose(1, 0, 2, 3)
        rest_cores = jnp.concatenate(
            [
                expand_sum.reshape(2, spare * shard_rows, half),
                rest_sum[cut : cut + SLAB].reshape(2, shard_rows, half),
                rest_sum[cut + SLAB :].reshape(2, -1, half),
            ],
            axis=1,
        )
        joint_got, vector_got, rest_other = stage(
            swap(joint_far, "dp", 2),
            swap(grad_vector, "dp", 2),
            swap(own_part(rest_cores, 1 - core, 0), "seq", 1),
        )
        rest_two = both_halves(own_part(rest_cores, core, 0)[None], rest_other[None], core, axis=0)
        joint_near, joint_far = add_z(joint_near, joint_got)
        grad_vector = grad_vector + vector_got
        joint_got, vector_got, rest_two = stage(
            swap(joint_far, "dp", 4), swap(grad_vector, "dp", 4), rest_two
        )
        joint_sum = joint_near + joint_got.astype(F32)
        vector_sum = grad_vector + vector_got
    for bit in bits[1:]:
        for d in [d for d in held if d & bit]:
            arrived = swap(held.pop(d).astype(BF16), "seq", bit).astype(F32)
            held[d ^ bit] = held[d ^ bit].astype(F32) + arrived

    cut = spare * SLAB
    if by_slabs:
        rank = dp_rank * seq_count + seq_rank
        shard_cols = vectors.shape[1]
        shard_vector = lax.dynamic_slice_in_dim(vector_sum, rank * shard_cols, shard_cols, 1)
        local_squares = (
            jnp.sum(rest_sum * rest_sum)
            + jnp.sum(joint_sum * joint_sum)
            + jnp.sum(shard_vector * shard_vector)
        )
        joint_cores = joint_sum.reshape(2, shard_rows, -1)
        shard_joint = both_halves(
            own_part(joint_cores, core, 0),
            swap(own_part(joint_cores, 1 - core, 0), "seq", 1),
            core,
        )
        cut = spare * shard_rows
        shard_expand = rest_two[:, :cut].reshape(2, spare, shard_rows, half)
        shard_expand = shard_expand.transpose(2, 0, 1, 3).reshape(shard_rows, hidden)
        shard_output = rest_two[:, cut : cut + shard_rows].transpose(1, 0, 2)
        shard_output = shard_output.reshape(shard_rows, width)
        shard_shrink = rest_two[:, cut + shard_rows :].transpose(1, 0, 2).reshape(-1, width)
        square_total = local_squares.reshape(1, 1)
        for axis, bit in (("seq", 1), ("dp", 1), ("dp", 2)):
            square_total = square_total + swap(square_total, axis, bit)
        square_total, tokens_got = stage(square_total, tokens_got)
        held[0] = held[0] + tokens_got.astype(F32)
        for axis, bit in (("dp", 4), ("seq", 2)):
            square_total = square_total + swap(square_total, axis, bit)
        square_total = square_total[0, 0]
    else:
        rest_other = rest_theirs.astype(F32)
        grads = (
            full_weight((joint_mine, joint_theirs.astype(F32)), 1),
            full_weight((rest_mine[..., cut : cut + SLAB, :], rest_other[..., cut : cut + SLAB, :]), 1),
            full_weight((rest_mine[..., :cut, :], rest_other[..., :cut, :]), spare),
            full_weight((rest_mine[..., cut + SLAB :, :], rest_other[..., cut + SLAB :, :]), 1),
        )
        shard_joint, shard_output, shard_expand, shard_shrink = (
            lax.psum_scatter(g, ("dp", "seq"), scatter_dimension=0, tiled=True) for g in grads
        )
        shard_vector = lax.psum_scatter(
            grad_vector, ("dp", "seq"), scatter_dimension=1, tiled=True
        )
        local_squares = sum(
            jnp.sum(g * g)
            for g in (shard_joint, shard_output, shard_expand, shard_shrink, shard_vector)
        )
        square_total = lax.psum(local_squares, ("dp", "seq"))
    token_gradient = held[0].reshape(rows, length, width)
    gradient_norm = jnp.sqrt(square_total)
    clip_scale = CLIP_LEVEL / (gradient_norm + 1e-06)
    joint_master, joint_momentum, joint_variance = adam_step(
        shard_joint * clip_scale, joint_weight, joint_mean, joint_square, RATE_MATRIX, DECAY
    )
    output_master, output_momentum, output_variance = adam_step(
        shard_output * clip_scale, output_weight, output_mean, output_square, RATE_MATRIX, DECAY
    )
    expand_master, expand_momentum, expand_variance = adam_step(
        shard_expand * clip_scale, expand_weight, expand_mean, expand_square, RATE_MATRIX, DECAY
    )
    shrink_master, shrink_momentum, shrink_variance = adam_step(
        shard_shrink * clip_scale, shrink_weight, shrink_mean, shrink_square, RATE_MATRIX, DECAY
    )
    vector_master, vector_momentum, vector_variance = adam_step(
        shard_vector * clip_scale, vectors, vector_mean, vector_square, RATE_VECTOR, 0.0
    )
    return (
        layer_output,
        token_gradient,
        gradient_norm,
        joint_master,
        output_master,
        expand_master,
        shrink_master,
        vector_master,
        joint_momentum,
        output_momentum,
        expand_momentum,
        shrink_momentum,
        vector_momentum,
        joint_variance,
        output_variance,
        expand_variance,
        shrink_variance,
        vector_variance,
    )


def solution(mesh):
    rows = P(("dp", "seq"), None)
    cols = P(None, ("dp", "seq"))
    state = (rows, rows, rows, rows, cols)
    tokens = P("dp", "seq", None)
    return jax.shard_map(
        local,
        mesh=mesh,
        in_specs=(tokens, P("dp", None), P("dp", None, "seq", None), tokens) + state * 3,
        out_specs=(tokens, tokens, P()) + state * 3,
        check_vma=False,
    )
```

profile of v0, /device:TPU:0, one launch (start us, length us, event | category | flops | bytes accessed | tf_op | source)
XLA Modules:
  0.0 433.8 jit_solution(9282773658749096407)
XLA Ops:
  4.4 1.2 fusion.46
  6.3 3.7 collective-permute-start.1
  11.0 1.5 collective-permute-start.5
  13.3 3.3 collective-permute-done.1
  17.7 6.7 %collective-permute-done.2 = bf16[2,48,1280]{2,1,0:T(8,128)(2,1)S(1)} collective-permute-done((bf16[2,48,1280]{2,1,0:T(8,128)(2,1)S(1)}, bf16[2,48,1280]{2,1,0:T(8,128)(2,1)S(1)}, u32[]{:S(2)}, u32[]{:S(2)}) %collective-permute-start.2) | collective-permute-done | bytes 245792 | tf_op jit(solution)/shard_map/ppermute | solution.py:60
  25.2 5.9 %collective-permute-done.5 = bf16[2,256,768]{2,1,0:T(8,128)(2,1)} collective-permute-done((bf16[2,256,768]{2,1,0:T(8,128)(2,1)}, bf16[2,256,768]{2,1,0:T(8,128)(2,1)}, u32[]{:S(2)}, u32[]{:S(2)}) %collective-permute-start.5) | collective-permute-done | bytes 786464 | tf_op jit(solution)/shard_map/ppermute | solution.py:60
  31.1 1.5 collective-permute-start.7
  32.6 1.5 collective-permute-start.6
  37.0 8.6 %share.2.refs_5_.refs_8_ = f32[2,6,256,128]{3,2,1,0:T(8,128)} custom-call(bf16[4,12,256,1024]{3,2,1,0:T(8,128)(2,1)} %refs_9_.3, s32[4,256,128]{2,1,0:T(8,128)} %broadcast_in_dim.62.refs_1_.refs_4_.refs_10_, s32[4,8,1024]{2,1,0:T(8,128)} %broadcast_in_dim.63.refs_2_, bf16[4,48,1280]{2,1,0:T(8,128)(2,1)} %pad_maximum_fusion.6.refs_3_.refs_8_), custom_call_target="tpu_custom_call" | custom-call | flops 25165824 | bytes 12582912 | tf_op jit(solution)/shard_map/share/pallas_call | solution.py:228
  45.6 5.6 %collective-permute-done.8 = bf16[432,384]{1,0:T(8,128)(2,1)S(1)} collective-permute-done((bf16[432,384]{1,0:T(8,128)(2,1)S(1)}, bf16[432,384]{1,0:T(8,128)(2,1)S(1)}, u32[]{:S(2)}, u32[]{:S(2)}) %collective-permute-start.8) | collective-permute-done | bytes 331808 | tf_op jit(solution)/shard_map/ppermute | solution.py:60
  51.3 1.5 pad_maximum_fusion
  57.3 8.2 %share.3.refs_15_.refs_8_ = f32[2,6,256,128]{3,2,1,0:T(8,128)} custom-call(bf16[4,12,256,1024]{3,2,1,0:T(8,128)(2,1)} %refs_9_.3, s32[4,256,128]{2,1,0:T(8,128)} %broadcast_in_dim.62.refs_1_.refs_4_.refs_10_, s32[4,8,1024]{2,1,0:T(8,128)} %broadcast_in_dim.63.refs_2_, bf16[4,48,1280]{2,1,0:T(8,128)(2,1)} %copy-done.8, bf16[4,48,1280]{2,1,0:T(8,128)(2,1)} %copy-done.9, ...), custom_call_target="tpu_custom_call" | custom-call | flops 25165824 | bytes 12582912 | tf_op jit(solution)/shard_map/share/pallas_call | solution.py:228
  65.5 2.3 collective-permute-done.9.refs_11_
  70.2 3.5 collective-permute-done.13
  73.6 2.6 collective-permute-done.14
  77.1 1.3 pad_maximum_fusion.1.refs_0_
  78.3 1.6 collective-permute-start.17
  80.4 19.9 %project.1 = (bf16[1024,768]{1,0:T(8,128)(2,1)}, bf16[4,1024,768]{2,1,0:T(8,128)(2,1)}, bf16[4,1024,768]{2,1,0:T(8,128)(2,1)}, bf16[768,2304]{1,0:T(8,128)(2,1)}) custom-call(s32[23]{0:T(128)} %stack.146.refs_0_.meta, s32[4,4]{1,0:T(4,128)} %copy-done.42, bf16[1024,768]{1,0:T(8,128)(2,1)} %bitcast.255, bf16[1024,768]{1,0:T(8,128)(2,1)} %bitcast.44.refs_3_.refs_2_, ...), custom_call_target="tpu_custom_call" | custom-call | flops 10871635968 | bytes 12582912 | tf_op jit(solution)/shard_map/project/pallas_call | solution.py:179
  100.9 16.2 %attend.2 = (bf16[4,256,768]{2,1,0:T(8,128)(2,1)}, f32[4,6,256,128]{3,2,1,0:T(8,128)}) custom-call(s32[4,5]{1,0:T(4,128)} %pad_add_fusion.refs_0_.refs_1_, bf16[4,256,768]{2,1,0:T(8,128)(2,1)} %bitcast.258, bf16[4,4,256,768]{3,2,1,0:T(8,128)(2,1)} %bitcast.244, bf16[4,4,256,768]{3,2,1,0:T(8,128)(2,1)} %bitcast.248, ...), custom_call_target="tpu_custom_call" | custom-call | flops 6442450944 | bytes 3145728 | tf_op jit(solution)/shard_map/attend/pallas_call | solution.py:337
  119.5 2.7 collective-permute-start.19
  122.9 12.2 %attend.3 = (bf16[4,256,768]{2,1,0:T(8,128)(2,1)}, f32[4,6,256,128]{3,2,1,0:T(8,128)}) custom-call(s32[4,5]{1,0:T(4,128)} %pad_add_fusion.refs_0_.refs_1_, bf16[4,256,768]{2,1,0:T(8,128)(2,1)} %bitcast.259, bf16[4,4,256,768]{3,2,1,0:T(8,128)(2,1)} %bitcast.245, bf16[4,4,256,768]{3,2,1,0:T(8,128)(2,1)} %bitcast.249, ...), custom_call_target="tpu_custom_call", output_to_operand_aliasing={{0}: (6, {}), {1}: (7, {})} | custom-call | flops 6442450944 | bytes 3145728 | tf_op jit(solution)/shard_map/attend/pallas_call | solution.py:337
  135.1 2.8 collective-permute-done.19.refs_4_
  138.2 1.7 collective-permute-start.23
  140.7 1.3 collective-permute-done.23.refs_8_
  143.4 40.9 %feed.1 = (bf16[1024,768]{1,0:T(8,128)(2,1)}, f32[1024,768]{1,0:T(8,128)}, bf16[1024,768]{1,0:T(8,128)(2,1)}, bf16[1024,3072]{1,0:T(8,128)(2,1)}, bf16[1024,3072...) custom-call(s32[23]{0:T(128)} %stack.146.refs_0_.meta, ...), custom_call_target="tpu_custom_call" | custom-call | flops 21743271936 | bytes 28311552 | tf_op jit(solution)/shard_map/feed/pallas_call | solution.py:587
  184.3 15.8 %feed_grad.2.refs_12_ = bf16[2,2,4,432,384]{4,3,2,1,0:T(8,128)(2,1)} custom-call(s32[23]{0:T(128)} %copy-done.51, bf16[1024,768]{1,0:T(8,128)(2,1)} %get-tuple-element.152.h1_ref, bf16[1024,3072]{1,0:T(8,128)(2,1)} %get-tuple-element.153.du_ref, bf16[1024,3072]{1,0:T(8,128)(2,1)} %get-tuple-element.154.gl_ref, bf16[1024,768]{1,0:T(8,128)(2,1)} %get-tuple-element.155.dz_ref, ...), custom_call_target="tpu_custom_call" | custom-call | flops 5435817984 | bytes 12582912 | tf_op jit(solution)/shard_map/feed_grad/pallas_call | solution.py:706
  200.4 34.2 %attend_back.2 = (bf16[4,256,768]{2,1,0:T(8,128)(2,1)}, bf16[4,4,256,768]{3,2,1,0:T(8,128)(2,1)}, bf16[4,4,256,768]{3,2,1,0:T(8,128)(2,1)}) custom-call(s32[23]{0:T(128)} %stack.146.refs_0_.meta, s32[4,5]{1,0:T(4,128)} %pad_add_fusion.refs_0_.refs_1_, bf16[4,256,768]{2,1,0:T(8,128)(2,1)} %bitcast.260, bf16[4,4,256,768]{3,2,1,0:T(8,128)(2,1)} %bitcast.246, ...), custom_call_target="tpu_custom_call" | custom-call | flops 16106127360 | bytes 6291456 | tf_op jit(solution)/shard_map/attend_back/pallas_call | solution.py:438
  234.6 18.5 %feed_grad.3 = (f32[4,432,384]{2,1,0:T(8,128)}, f32[2,432,384]{2,1,0:T(8,128)}, f32[2,432,384]{2,1,0:T(8,128)}, bf16[2,2,432,384]{3,2,1,0:T(8,128)(2,1)}, bf16[2,2,432,384]{3,2,1,0:T(8,128)(2,1)}) custom-call(s32[23]{0:T(128)} %stack.146.refs_0_.meta, bf16[1024,768]{1,0:T(8,128)(2,1)} %get-tuple-element.152.h1_ref, ...), custom_call_target="tpu_custom_call" | custom-call | flops 5435817984 | bytes 12582912 | tf_op jit(solution)/shard_map/feed_grad/pallas_call | solution.py:706
  253.4 22.4 %attend_back.3 = (bf16[4,256,768]{2,1,0:T(8,128)(2,1)}, bf16[4,4,256,768]{3,2,1,0:T(8,128)(2,1)}, bf16[4,4,256,768]{3,2,1,0:T(8,128)(2,1)}) custom-call(s32[23]{0:T(128)} %stack.146.refs_0_.meta, s32[4,5]{1,0:T(4,128)} %pad_add_fusion.refs_0_.refs_1_, bf16[4,256,768]{2,1,0:T(8,128)(2,1)} %bitcast.261, ...), custom_call_target="tpu_custom_call", output_to_operand_aliasing={{0}: (12, {}), {1}: (13, {}), {2}: (14, {})} | custom-call | flops 16106127360 | bytes 6291456 | tf_op jit(solution)/shard_map/attend_back/pallas_call | solution.py:438
  275.7 8.8 %collective-permute-done.26 = bf16[2,2,432,384]{3,2,1,0:T(8,128)(2,1)S(1)} collective-permute-done((bf16[2,2,432,384]{3,2,1,0:T(8,128)(2,1)}, bf16[2,2,432,384]{3,2,1,0:T(8,128)(2,1)S(1)}, u32[]{:S(2)}, u32[]{:S(2)}) %collective-permute-start.26) | collective-permute-done | bytes 1327136 | tf_op jit(solution)/shard_map/ppermute | solution.py:60
  285.7 1.6 convert_element_type.137
  288.4 2.0 collective-permute-start.28
  290.8 1.3 copy-done.2
  292.1 4.8 %collective-permute-start.29 = (bf16[2,432,384]{2,1,0:T(8,128)(2,1)S(1)}, bf16[2,432,384]{2,1,0:T(8,128)(2,1)S(1)}, u32[]{:S(2)}, u32[]{:S(2)}) collective-permute-start(bf16[2,432,384]{2,1,0:T(8,128)(2,1)S(1)} %fusion.6.refs_11_), channel_id=1, source_target_pairs={{0,2},{1,3},{2,0},{3,1},{4,6},{5,7},{6,4},{7,5},{8,10},{9,11},{10,... | collective-permute-start | bytes 1990664 | tf_op jit(solution)/shard_map/ppermute | solution.py:60
  296.9 19.8 %joint_grad.1 = (f32[2,2,4,48,1152]{4,3,2,1,0:T(8,128)}, bf16[2,2,4,48,1152]{4,3,2,1,0:T(8,128)(2,1)}, f32[8,768]{1,0:T(8,128)}) custom-call(s32[23]{0:T(128)} %stack.146.refs_0_.meta, bf16[1024,768]{1,0:T(8,128)(2,1)} %bitcast.257, bf16[1024,768]{1,0:T(8,128)(2,1)} %bitcast.44.refs_3_.refs_2_, bf16[512,768]{1,0:T(8,128)(2,1)} %bitcast.45.refs_4_.refs_3_, ...), custom_call_target="tpu_custom_call" | custom-call | flops 10871635968 | bytes 25165824 | tf_op jit(solution)/shard_map/joint_grad/pallas_call | solution.py:848
  316.7 2.7 fusion.4
  321.8 12.7 %token_grad.2 = (bf16[2,1024,768]{2,1,0:T(8,128)(2,1)}, bf16[1,1024,768]{2,1,0:T(8,128)(2,1)}) custom-call(s32[23]{0:T(128)} %stack.146.refs_0_.meta, s32[4,4]{1,0:T(4,128)} %copy-done.42, bf16[4,1024,768]{2,1,0:T(8,128)(2,1)} %bitcast.234, bf16[4,1024,768]{2,1,0:T(8,128)(2,1)} %bitcast.237, bf16[768,2304]{1,0:T(8,128)(2,1)} %get-tuple-element.165.refs_4_, ...), custom_call_target="tpu_custom_call" | custom-call | flops 7247757312 | bytes 14155776 | tf_op jit(solution)/shard_map/token_grad/pallas_call | solution.py:777
  334.6 1.8 collective-permute-start.33
  339.0 3.3 collective-permute-done.32
  343.1 3.0 fusion.44
  349.8 9.6 %token_grad.3 = f32[1,1024,768]{2,1,0:T(8,128)} custom-call(s32[23]{0:T(128)} %stack.146.refs_0_.meta, s32[4,4]{1,0:T(4,128)} %copy-done.42, bf16[4,1024,768]{2,1,0:T(8,128)(2,1)} %bitcast.235, bf16[4,1024,768]{2,1,0:T(8,128)(2,1)} %bitcast.238, bf16[768,2304]{1,0:T(8,128)(2,1)} %get-tuple-element.165.refs_4_, bf16[1024,768]{1,0:T(8,128)(2,1)} %bitcast.243, ...), custom_call_target="tpu_custom_call" | custom-call | flops 2415919104 | bytes 4718592 | tf_op jit(solution)/shard_map/token_grad/pallas_call | solution.py:777
  361.6 1.2 convert_element_type.148
  363.0 1.5 collective-permute-start.38
  365.6 3.2 fusion
  370.4 1.8 multiply_reduce_fusion
  374.3 1.3 collective-permute-start.42
  376.3 6.2 %collective-permute-done.42 = f32[12,768]{1,0:T(8,128)S(1)} collective-permute-done((f32[12,768]{1,0:T(8,128)S(1)}, f32[12,768]{1,0:T(8,128)S(1)}, u32[]{:S(2)}, u32[]{:S(2)}) %collective-permute-start.42) | collective-permute-done | bytes 36896 | tf_op jit(solution)/shard_map/ppermute | solution.py:60
  382.6 2.1 collective-permute-start.45
  385.6 1.3 bitcast_select_fusion.1
  387.7 3.1 collective-permute-done.45
  391.4 1.5 collective-permute-done.44
  392.9 1.6 multiply_reduce_fusion.1
  395.8 1.4 multiply_reduce_fusion.2
  397.9 1.4 collective-permute-start.46
  399.9 2.5 collective-permute-start.47
  404.1 1.4 collective-permute-start.48
  405.4 2.2 collective-permute-done.48
  408.3 1.6 bitcast_select_fusion.3
  409.8 2.4 collective-permute-done.49
  412.2 4.0 bitcast_add_fusion
  416.2 3.4 collective-permute-start.50
  421.2 2.0 collective-permute-start.51
  423.1 1.6 collective-permute-done.51
  426.4 1.2 multiply_bitcast_fusion
  (302 shorter events, 55.6 us)
Async XLA Ops:
  2.9 3.4 collective-permute-start
  4.4 6.1 %copy-start.31 = (f32[24,768]{1,0:T(8,128)S(1)}, f32[24,768]{1,0:T(8,128)}, u32[]{:S(2)}) copy-start(f32[24,768]{1,0:T(8,128)} %param.27) | copy-start | bytes 221188
  4.4 6.1 %copy-start.19 = (f32[24,3072]{1,0:T(8,128)S(1)}, f32[24,3072]{1,0:T(8,128)}, u32[]{:S(2)}) copy-start(f32[24,3072]{1,0:T(8,128)} %param.28) | copy-start | bytes 884740
  4.4 6.2 %copy-start.21 = (f32[96,768]{1,0:T(8,128)S(1)}, f32[96,768]{1,0:T(8,128)}, u32[]{:S(2)}) copy-start(f32[96,768]{1,0:T(8,128)} %param.29) | copy-start | bytes 884740
  6.3 10.3 %collective-permute-start.1 = (bf16[48,1280]{1,0:T(8,128)(2,1)S(1)}, bf16[48,1280]{1,0:T(8,128)(2,1)S(1)}, u32[]{:S(2)}, u32[]{:S(2)}) collective-permute-start(bf16[48,1280]{1,0:T(8,128)(2,1)S(1)} %maximum_select_fusion.1), channel_id=1, source_target_pairs={{0,16},{4,20},{8,24},{12,28},{16,0},{20,4},{24,8},{28,12},{1,17},{... | collective-permute-start | bytes 368648 | tf_op jit(solution)/shard_map/ppermute | solution.py:60
  10.8 6.7 %collective-permute-start.3 = (bf16[216,384]{1,0:T(8,128)(2,1)S(1)}, bf16[216,384]{1,0:T(8,128)(2,1)S(1)}, u32[]{:S(2)}, u32[]{:S(2)}) collective-permute-start(bf16[216,384]{1,0:T(8,128)(2,1)S(1)} %get-tuple-element.252), channel_id=1, source_target_pairs={{0,1},{1,0},{2,3},{3,2},{4,5},{5,4},{6,7},{7,6},{8,9},{9,8},{10,11... | collective-permute-start | bytes 497672 | tf_op jit(solution)/shard_map/ppermute | solution.py:60
  11.0 20.1 %collective-permute-start.5 = (bf16[2,256,768]{2,1,0:T(8,128)(2,1)}, bf16[2,256,768]{2,1,0:T(8,128)(2,1)}, u32[]{:S(2)}, u32[]{:S(2)}) collective-permute-start(bf16[2,256,768]{2,1,0:T(8,128)(2,1)} %get-tuple-element.121), channel_id=1, source_target_pairs={{0,2},{1,3},{2,0},{3,1},{4,6},{5,7},{6,4},{7,5},{8,10},{9,11},{10,... | collective-permute-start | bytes 2359304 | tf_op jit(solution)/shard_map/ppermute | solution.py:60
  12.5 18.6 %collective-permute-start.4 = (bf16[4,256,768]{2,1,0:T(8,128)(2,1)S(1)}, bf16[4,256,768]{2,1,0:T(8,128)(2,1)}, u32[]{:S(2)}, u32[]{:S(2)}) collective-permute-start(bf16[4,256,768]{2,1,0:T(8,128)(2,1)S(1)} %copy-done.11), channel_id=1, source_target_pairs={{0,1},{1,0},{2,3},{3,2},{4,5},{5,4},{6,7},{7,6},{8,9},{9,8},{10,11... | collective-permute-start | bytes 4718600 | tf_op jit(solution)/shard_map/ppermute | solution.py:60
  16.6 7.8 %collective-permute-start.2 = (bf16[2,48,1280]{2,1,0:T(8,128)(2,1)S(1)}, bf16[2,48,1280]{2,1,0:T(8,128)(2,1)S(1)}, u32[]{:S(2)}, u32[]{:S(2)}) collective-permute-start(bf16[2,48,1280]{2,1,0:T(8,128)(2,1)S(1)} %pad_maximum_fusion.11), channel_id=1, source_target_pairs={{0,8},{4,12},{8,0},{12,4},{16,24},{20,28},{24,16},{28,20},{1,9},{5... | collective-permute-start | bytes 737288 | tf_op jit(solution)/shard_map/ppermute | solution.py:60
  31.1 20.1 %collective-permute-start.7 = (bf16[4,48,1280]{2,1,0:T(8,128)(2,1)}, bf16[4,48,1280]{2,1,0:T(8,128)(2,1)S(1)}, u32[]{:S(2)}, u32[]{:S(2)}) collective-permute-start(bf16[4,48,1280]{2,1,0:T(8,128)(2,1)} %pad_maximum_fusion.6.refs_3_.refs_8_), channel_id=1, source_target_pairs={{0,4},{4,0},{8,12},{12,8},{16,20},{20,16},{24,28},{28,24},{1,5},{5... | collective-permute-start | bytes 1474568 | tf_op jit(solution)/shard_map/ppermute | solution.py:60
  32.6 18.6 %collective-permute-start.6 = (bf16[4,48,1280]{2,1,0:T(8,128)(2,1)}, bf16[4,48,1280]{2,1,0:T(8,128)(2,1)S(1)}, u32[]{:S(2)}, u32[]{:S(2)}) collective-permute-start(bf16[4,48,1280]{2,1,0:T(8,128)(2,1)} %pad_maximum_fusion.6.refs_3_.refs_8_), channel_id=1, source_target_pairs={{0,2},{1,3},{2,0},{3,1},{4,6},{5,7},{6,4},{7,5},{8,10},{9,11},{10,... | collective-permute-start | bytes 1474568 | tf_op jit(solution)/shard_map/ppermute | solution.py:60
  34.5 16.7 %collective-permute-start.8 = (bf16[432,384]{1,0:T(8,128)(2,1)S(1)}, bf16[432,384]{1,0:T(8,128)(2,1)S(1)}, u32[]{:S(2)}, u32[]{:S(2)}) collective-permute-start(bf16[432,384]{1,0:T(8,128)(2,1)S(1)} %pad_maximum_fusion.10), channel_id=1, source_target_pairs={{0,16},{4,20},{8,24},{12,28},{16,0},{20,4},{24,8},{28,12},{1,17},{... | collective-permute-start | bytes 995336 | tf_op jit(solution)/shard_map/ppermute | solution.py:60
  34.9 18.1 %copy-start.42 = (s32[4,4]{1,0:T(4,128)}, s32[4,4]{1,0:T(4,128)S(1)}, u32[]{:S(2)}) copy-start(s32[4,4]{1,0:T(4,128)S(1)} %get-tuple-element.228.refs_1_) | copy-start | bytes 196
  52.8 15.0 %collective-permute-start.11 = (bf16[12,48,1280]{2,1,0:T(8,128)(2,1)S(1)}, bf16[12,48,1280]{2,1,0:T(8,128)(2,1)}, u32[]{:S(2)}, u32[]{:S(2)}) collective-permute-start(bf16[12,48,1280]{2,1,0:T(8,128)(2,1)S(1)} %pad_maximum_fusion), channel_id=1, source_target_pairs={{0,1},{1,0},{2,3},{3,2},{4,5},{5,4},{6,7},{7,6},{8,9},{9,8},{10,11... | collective-permute-start | bytes 4423688 | tf_op jit(solution)/shard_map/ppermute | solution.py:60
  54.0 13.8 %collective-permute-start.10 = (bf16[2,256,768]{2,1,0:T(8,128)(2,1)}, bf16[2,256,768]{2,1,0:T(8,128)(2,1)}, u32[]{:S(2)}, u32[]{:S(2)}) collective-permute-start(bf16[2,256,768]{2,1,0:T(8,128)(2,1)} %collective-permute-done.5), channel_id=1, source_target_pairs={{0,1},{1,0},{2,3},{3,2},{4,5},{5,4},{6,7},{7,6},{8,9},{9,8},{10,11... | collective-permute-start | bytes 2359304 | tf_op jit(solution)/shard_map/ppermute | solution.py:60
  54.5 13.3 %collective-permute-start.9 = (bf16[4,48,1280]{2,1,0:T(8,128)(2,1)S(1)}, bf16[4,48,1280]{2,1,0:T(8,128)(2,1)}, u32[]{:S(2)}, u32[]{:S(2)}) collective-permute-start(bf16[4,48,1280]{2,1,0:T(8,128)(2,1)S(1)} %collective-permute-done.6.refs_4_.refs_9_), channel_id=1, source_target_pairs={{0,4},{4,0},{8,12},{12,8},{16,20},{20,16},{24,28},{28,24},{1,5},{5... | collective-permute-start | bytes 1474568 | tf_op jit(solution)/shard_map/ppermute | solution.py:60
  56.8 16.9 %collective-permute-start.13 = (bf16[2,432,384]{2,1,0:T(8,128)(2,1)}, bf16[2,432,384]{2,1,0:T(8,128)(2,1)}, u32[]{:S(2)}, u32[]{:S(2)}) collective-permute-start(bf16[2,432,384]{2,1,0:T(8,128)(2,1)} %pad_maximum_fusion.2), channel_id=1, source_target_pairs={{0,8},{4,12},{8,0},{12,4},{16,24},{20,28},{24,16},{28,20},{1,9},{5... | collective-permute-start | bytes 1990664 | tf_op jit(solution)/shard_map/ppermute | solution.py:60
  56.8 19.5 %collective-permute-start.14 = (bf16[2,256,768]{2,1,0:T(8,128)(2,1)}, bf16[2,256,768]{2,1,0:T(8,128)(2,1)}, u32[]{:S(2)}, u32[]{:S(2)}) collective-permute-start(bf16[2,256,768]{2,1,0:T(8,128)(2,1)} %get-tuple-element.132), channel_id=1, source_target_pairs={{0,2},{1,3},{2,0},{3,1},{4,6},{5,7},{6,4},{7,5},{8,10},{9,11},{10,... | collective-permute-start | bytes 2359304 | tf_op jit(solution)/shard_map/ppermute | solution.py:60
  65.5 10.8 %copy-start.50 = (pred[8]{0:T(512)(128)(4,1)S(1)}, pred[8]{0:T(512)(128)(4,1)}, u32[]{:S(2)}) copy-start(pred[8]{0:T(512)(128)(4,1)} %constant.203.clone.1) | copy-start | bytes 28
  67.8 8.5 %collective-permute-start.12 = (bf16[4,48,1280]{2,1,0:T(8,128)(2,1)}, bf16[4,48,1280]{2,1,0:T(8,128)(2,1)S(1)}, u32[]{:S(2)}, u32[]{:S(2)}) collective-permute-start(bf16[4,48,1280]{2,1,0:T(8,128)(2,1)} %collective-permute-done.9.refs_11_), channel_id=1, source_target_pairs={{0,1},{1,0},{2,3},{3,2},{4,5},{5,4},{6,7},{7,6},{8,9},{9,8},{10,11... | collective-permute-start | bytes 1474568 | tf_op jit(solution)/shard_map/ppermute | solution.py:60
  76.3 4.1 collective-permute-start.15
  78.3 44.0 %copy-start.17 = (bf16[4,432,384]{2,1,0:T(8,128)(2,1)}, bf16[4,432,384]{2,1,0:T(8,128)(2,1)S(1)}, u32[]{:S(2)}) copy-start(bf16[4,432,384]{2,1,0:T(8,128)(2,1)S(1)} %pad_maximum_fusion.1.refs_0_) | copy-start | bytes 3981316
  78.3 38.8 %collective-permute-start.17 = (bf16[4,432,384]{2,1,0:T(8,128)(2,1)S(1)}, bf16[4,432,384]{2,1,0:T(8,128)(2,1)}, u32[]{:S(2)}, u32[]{:S(2)}) collective-permute-start(bf16[4,432,384]{2,1,0:T(8,128)(2,1)S(1)} %pad_maximum_fusion.1.refs_0_), channel_id=1, source_target_pairs={{0,4},{4,0},{8,12},{12,8},{16,20},{20,16},{24,28},{28,24},{1,5},{5... | collective-permute-start | bytes 3981320 | tf_op jit(solution)/shard_map/ppermute | solution.py:60
  79.9 37.3 %collective-permute-start.16 = (bf16[4,432,384]{2,1,0:T(8,128)(2,1)S(1)}, bf16[4,432,384]{2,1,0:T(8,128)(2,1)}, u32[]{:S(2)}, u32[]{:S(2)}) collective-permute-start(bf16[4,432,384]{2,1,0:T(8,128)(2,1)S(1)} %pad_maximum_fusion.1.refs_0_), channel_id=1, source_target_pairs={{0,2},{1,3},{2,0},{3,1},{4,6},{5,7},{6,4},{7,5},{8,10},{9,11},{10,... | collective-permute-start | bytes 3981320 | tf_op jit(solution)/shard_map/ppermute | solution.py:60
  119.5 18.4 %collective-permute-start.19 = (bf16[2,432,384]{2,1,0:T(8,128)(2,1)S(1)}, bf16[2,432,384]{2,1,0:T(8,128)(2,1)S(1)}, u32[]{:S(2)}, u32[]{:S(2)}) collective-permute-start(bf16[2,432,384]{2,1,0:T(8,128)(2,1)S(1)} %slice.234), channel_id=1, source_target_pairs={{0,2},{1,3},{2,0},{3,1},{4,6},{5,7},{6,4},{7,5},{8,10},{9,11},{10,... | collective-permute-start | bytes 1990664 | tf_op jit(solution)/shard_map/ppermute | solution.py:60
  122.2 16.0 %collective-permute-start.18 = (bf16[2,432,384]{2,1,0:T(8,128)(2,1)S(1)}, bf16[2,432,384]{2,1,0:T(8,128)(2,1)}, u32[]{:S(2)}, u32[]{:S(2)}) collective-permute-start(bf16[2,432,384]{2,1,0:T(8,128)(2,1)S(1)} %slice.233), channel_id=1, source_target_pairs={{0,4},{4,0},{8,12},{12,8},{16,20},{20,16},{24,28},{28,24},{1,5},{5... | collective-permute-start | bytes 1990664 | tf_op jit(solution)/shard_map/ppermute | solution.py:60
  122.4 18.3 %collective-permute-start.20 = (bf16[4,432,384]{2,1,0:T(8,128)(2,1)S(1)}, bf16[4,432,384]{2,1,0:T(8,128)(2,1)}, u32[]{:S(2)}, u32[]{:S(2)}) collective-permute-start(bf16[4,432,384]{2,1,0:T(8,128)(2,1)S(1)} %pad_maximum_fusion.1.refs_0_), channel_id=1, source_target_pairs={{0,1},{1,0},{2,3},{3,2},{4,5},{5,4},{6,7},{7,6},{8,9},{9,8},{10,11... | collective-permute-start | bytes 3981320 | tf_op jit(solution)/shard_map/ppermute | solution.py:60
  122.4 20.3 %collective-permute-start.21 = (bf16[4,432,384]{2,1,0:T(8,128)(2,1)}, bf16[4,432,384]{2,1,0:T(8,128)(2,1)}, u32[]{:S(2)}, u32[]{:S(2)}) collective-permute-start(bf16[4,432,384]{2,1,0:T(8,128)(2,1)} %collective-permute-done.16.refs_8_.refs_1_), channel_id=1, source_target_pairs={{0,1},{1,0},{2,3},{3,2},{4,5},{5,4},{6,7},{7,6},{8,9},{9,8},{10,11... | collective-permute-start | bytes 3981320 | tf_op jit(solution)/shard_map/ppermute | solution.py:60
  122.9 19.8 %collective-permute-start.22 = (bf16[4,432,384]{2,1,0:T(8,128)(2,1)}, bf16[4,432,384]{2,1,0:T(8,128)(2,1)}, u32[]{:S(2)}, u32[]{:S(2)}) collective-permute-start(bf16[4,432,384]{2,1,0:T(8,128)(2,1)} %collective-permute-done.17.refs_9_.refs_2_), channel_id=1, source_target_pairs={{0,1},{1,0},{2,3},{3,2},{4,5},{5,4},{6,7},{7,6},{8,9},{9,8},{10,11... | collective-permute-start | bytes 3981320 | tf_op jit(solution)/shard_map/ppermute | solution.py:60
  122.9 17.1 %copy-start.47 = (s32[23]{0:T(128)S(1)}, s32[23]{0:T(128)}, u32[]{:S(2)}) copy-start(s32[23]{0:T(128)} %stack.146.refs_0_.meta) | copy-start | bytes 280
  138.2 3.8 collective-permute-start.23
  139.9 2.8 collective-permute-start.24
  140.0 44.2 %copy-start.51 = (s32[23]{0:T(128)}, s32[23]{0:T(128)S(1)}, u32[]{:S(2)}) copy-start(s32[23]{0:T(128)S(1)} %constant_dynamic-update-slice_fusion.meta) | copy-start | bytes 280
  200.0 34.6 %collective-permute-start.25 = (bf16[2,2,4,432,384]{4,3,2,1,0:T(8,128)(2,1)}, bf16[2,2,4,432,384]{4,3,2,1,0:T(8,128)(2,1)}, u32[]{:S(2)}, u32[]{:S(2)}) collective-permute-start(bf16[2,2,4,432,384]{4,3,2,1,0:T(8,128)(2,1)} %feed_grad.2.refs_12_), channel_id=1, source_target_pairs={{0,1},{1,0},{2,3},{3,2},{4,5},{5,4},{6,7},{7,6},{8,9},{9,8},{10,11... | collective-permute-start | bytes 15925256 | tf_op jit(solution)/shard_map/ppermute | solution.py:60
  253.1 31.4 %collective-permute-start.26 = (bf16[2,2,432,384]{3,2,1,0:T(8,128)(2,1)}, bf16[2,2,432,384]{3,2,1,0:T(8,128)(2,1)S(1)}, u32[]{:S(2)}, u32[]{:S(2)}) collective-permute-start(bf16[2,2,432,384]{3,2,1,0:T(8,128)(2,1)} %get-tuple-element.161.refs_15_), channel_id=1, source_target_pairs={{0,4},{4,0},{8,12},{12,8},{16,20},{20,16},{24,28},{28,24},{1,5},{5... | collective-permute-start | bytes 3981320 | tf_op jit(solution)/shard_map/ppermute | solution.py:60
  253.2 31.4 %collective-permute-start.27 = (bf16[2,2,432,384]{3,2,1,0:T(8,128)(2,1)}, bf16[2,2,432,384]{3,2,1,0:T(8,128)(2,1)S(1)}, u32[]{:S(2)}, u32[]{:S(2)}) collective-permute-start(bf16[2,2,432,384]{3,2,1,0:T(8,128)(2,1)} %get-tuple-element.162.refs_16_), channel_id=1, source_target_pairs={{0,2},{1,3},{2,0},{3,1},{4,6},{5,7},{6,4},{7,5},{8,10},{9,11},{10,... | collective-permute-start | bytes 3981320 | tf_op jit(solution)/shard_map/ppermute | solution.py:60
  288.4 28.3 %collective-permute-start.28 = (bf16[2,432,384]{2,1,0:T(8,128)(2,1)}, bf16[2,432,384]{2,1,0:T(8,128)(2,1)}, u32[]{:S(2)}, u32[]{:S(2)}) collective-permute-start(bf16[2,432,384]{2,1,0:T(8,128)(2,1)} %fusion.8.refs_10_), channel_id=1, source_target_pairs={{0,4},{4,0},{8,12},{12,8},{16,20},{20,16},{24,28},{28,24},{1,5},{5... | collective-permute-start | bytes 1990664 | tf_op jit(solution)/shard_map/ppermute | solution.py:60
  292.1 24.5 %collective-permute-start.29 = (bf16[2,432,384]{2,1,0:T(8,128)(2,1)S(1)}, bf16[2,432,384]{2,1,0:T(8,128)(2,1)S(1)}, u32[]{:S(2)}, u32[]{:S(2)}) collective-permute-start(bf16[2,432,384]{2,1,0:T(8,128)(2,1)S(1)} %fusion.6.refs_11_), channel_id=1, source_target_pairs={{0,2},{1,3},{2,0},{3,1},{4,6},{5,7},{6,4},{7,5},{8,10},{9,11},{10,... | collective-permute-start | bytes 1990664 | tf_op jit(solution)/shard_map/ppermute | solution.py:60
  316.7 25.6 %collective-permute-start.31 = (bf16[2,2,4,48,1152]{4,3,2,1,0:T(8,128)(2,1)}, bf16[2,2,4,48,1152]{4,3,2,1,0:T(8,128)(2,1)}, u32[]{:S(2)}, u32[]{:S(2)}) collective-permute-start(bf16[2,2,4,48,1152]{4,3,2,1,0:T(8,128)(2,1)} %get-tuple-element.177), channel_id=1, source_target_pairs={{0,1},{1,0},{2,3},{3,2},{4,5},{5,4},{6,7},{7,6},{8,9},{9,8},{10,11... | collective-permute-start | bytes 5308424 | tf_op jit(solution)/shard_map/ppermute | solution.py:60
  321.0 21.3 %collective-permute-start.30 = (bf16[2,432,384]{2,1,0:T(8,128)(2,1)S(1)}, bf16[2,432,384]{2,1,0:T(8,128)(2,1)S(1)}, u32[]{:S(2)}, u32[]{:S(2)}) collective-permute-start(bf16[2,432,384]{2,1,0:T(8,128)(2,1)S(1)} %pad_maximum_fusion.3.refs_5_), channel_id=1, source_target_pairs={{0,8},{4,12},{8,0},{12,4},{16,24},{20,28},{24,16},{28,20},{1,9},{5... | collective-permute-start | bytes 1990664 | tf_op jit(solution)/shard_map/ppermute | solution.py:60
  321.8 14.5 %copy-start.44 = (f32[8,768]{1,0:T(8,128)S(1)}, f32[8,768]{1,0:T(8,128)}, u32[]{:S(2)}) copy-start(f32[8,768]{1,0:T(8,128)} %get-tuple-element.178) | copy-start | bytes 73732
  334.6 25.3 %collective-permute-start.33 = (bf16[2,1024,768]{2,1,0:T(8,128)(2,1)}, bf16[2,1024,768]{2,1,0:T(8,128)(2,1)}, u32[]{:S(2)}, u32[]{:S(2)}) collective-permute-start(bf16[2,1024,768]{2,1,0:T(8,128)(2,1)} %get-tuple-element.180), channel_id=1, source_target_pairs={{0,1},{1,0},{2,3},{3,2},{4,5},{5,4},{6,7},{7,6},{8,9},{9,8},{10,11... | collective-permute-start | bytes 9437192 | tf_op jit(solution)/shard_map/ppermute | solution.py:60
  338.1 4.2 collective-permute-start.32
  342.3 17.0 %collective-permute-start.36 = (f32[12,768]{1,0:T(8,128)S(1)}, f32[12,768]{1,0:T(8,128)S(1)}, u32[]{:S(2)}, u32[]{:S(2)}) collective-permute-start(f32[12,768]{1,0:T(8,128)S(1)} %fusion.36), channel_id=1, source_target_pairs={{0,1},{1,0},{2,3},{3,2},{4,5},{5,4},{6,7},{7,6},{8,9},{9,8},{10,11... | collective-permute-start | bytes 110600 | tf_op jit(solution)/shard_map/ppermute | solution.py:60
  346.3 13.0 %collective-permute-start.34 = (bf16[2,2,48,1152]{3,2,1,0:T(8,128)(2,1)S(1)}, bf16[2,2,48,1152]{3,2,1,0:T(8,128)(2,1)}, u32[]{:S(2)}, u32[]{:S(2)}) collective-permute-start(bf16[2,2,48,1152]{3,2,1,0:T(8,128)(2,1)S(1)} %pad_maximum_fusion.7.refs_7_), channel_id=1, source_target_pairs={{0,4},{4,0},{8,12},{12,8},{16,20},{20,16},{24,28},{28,24},{1,5},{5... | collective-permute-start | bytes 1327112 | tf_op jit(solution)/shard_map/ppermute | solution.py:60
  348.0 11.9 %collective-permute-start.35 = (bf16[2,2,48,1152]{3,2,1,0:T(8,128)(2,1)}, bf16[2,2,48,1152]{3,2,1,0:T(8,128)(2,1)}, u32[]{:S(2)}, u32[]{:S(2)}) collective-permute-start(bf16[2,2,48,1152]{3,2,1,0:T(8,128)(2,1)} %pad_maximum_fusion.8.refs_8_), channel_id=1, source_target_pairs={{0,2},{1,3},{2,0},{3,1},{4,6},{5,7},{6,4},{7,5},{8,10},{9,11},{10,... | collective-permute-start | bytes 1327112 | tf_op jit(solution)/shard_map/ppermute | solution.py:60
  349.4 19.4 %collective-permute-start.39 = (bf16[432,384]{1,0:T(8,128)(2,1)}, bf16[432,384]{1,0:T(8,128)(2,1)}, u32[]{:S(2)}, u32[]{:S(2)}) collective-permute-start(bf16[432,384]{1,0:T(8,128)(2,1)} %fusion.20), channel_id=1, source_target_pairs={{0,16},{4,20},{8,24},{12,28},{16,0},{20,4},{24,8},{28,12},{1,17},{... | collective-permute-start | bytes 995336 | tf_op jit(solution)/shard_map/ppermute | solution.py:60
  359.9 8.9 %collective-permute-start.40 = (f32[12,768]{1,0:T(8,128)S(1)}, f32[12,768]{1,0:T(8,128)S(1)}, u32[]{:S(2)}, u32[]{:S(2)}) collective-permute-start(f32[12,768]{1,0:T(8,128)S(1)} %add.427), channel_id=1, source_target_pairs={{0,2},{1,3},{2,0},{3,1},{4,6},{5,7},{6,4},{7,5},{8,10},{9,11},{10,... | collective-permute-start | bytes 110600 | tf_op jit(solution)/shard_map/ppermute | solution.py:60
  363.0 6.3 %collective-permute-start.38 = (bf16[2,48,1152]{2,1,0:T(8,128)(2,1)S(1)}, bf16[2,48,1152]{2,1,0:T(8,128)(2,1)S(1)}, u32[]{:S(2)}, u32[]{:S(2)}) collective-permute-start(bf16[2,48,1152]{2,1,0:T(8,128)(2,1)S(1)} %get-tuple-element.231), channel_id=1, source_target_pairs={{0,2},{1,3},{2,0},{3,1},{4,6},{5,7},{6,4},{7,5},{8,10},{9,11},{10,... | collective-permute-start | bytes 663560 | tf_op jit(solution)/shard_map/ppermute | solution.py:60
  364.4 5.9 %collective-permute-start.37 = (bf16[2,48,1152]{2,1,0:T(8,128)(2,1)S(1)}, bf16[2,48,1152]{2,1,0:T(8,128)(2,1)S(1)}, u32[]{:S(2)}, u32[]{:S(2)}) collective-permute-start(bf16[2,48,1152]{2,1,0:T(8,128)(2,1)S(1)} %get-tuple-element.232), channel_id=1, source_target_pairs={{0,4},{4,0},{8,12},{12,8},{16,20},{20,16},{24,28},{28,24},{1,5},{5... | collective-permute-start | bytes 663560 | tf_op jit(solution)/shard_map/ppermute | solution.py:60
  373.4 9.1 %collective-permute-start.43 = (f32[216,384]{1,0:T(8,128)S(1)}, f32[216,384]{1,0:T(8,128)S(1)}, u32[]{:S(2)}, u32[]{:S(2)}) collective-permute-start(f32[216,384]{1,0:T(8,128)S(1)} %dynamic-slice_bitcast_fusion), channel_id=1, source_target_pairs={{0,1},{1,0},{2,3},{3,2},{4,5},{5,4},{6,7},{7,6},{8,9},{9,8},{10,11... | collective-permute-start | bytes 995336 | tf_op jit(solution)/shard_map/ppermute | solution.py:60
  373.6 8.9 %collective-permute-start.41 = (bf16[2,48,1152]{2,1,0:T(8,128)(2,1)S(1)}, bf16[2,48,1152]{2,1,0:T(8,128)(2,1)S(1)}, u32[]{:S(2)}, u32[]{:S(2)}) collective-permute-start(bf16[2,48,1152]{2,1,0:T(8,128)(2,1)S(1)} %pad_maximum_fusion.12), channel_id=1, source_target_pairs={{0,8},{4,12},{8,0},{12,4},{16,24},{20,28},{24,16},{28,20},{1,9},{5... | collective-permute-start | bytes 663560 | tf_op jit(solution)/shard_map/ppermute | solution.py:60
  374.3 8.2 %collective-permute-start.42 = (f32[12,768]{1,0:T(8,128)S(1)}, f32[12,768]{1,0:T(8,128)S(1)}, u32[]{:S(2)}, u32[]{:S(2)}) collective-permute-start(f32[12,768]{1,0:T(8,128)S(1)} %add.434), channel_id=1, source_target_pairs={{0,8},{4,12},{8,0},{12,4},{16,24},{20,28},{24,16},{28,20},{1,9},{5... | collective-permute-start | bytes 110600 | tf_op jit(solution)/shard_map/ppermute | solution.py:60
  375.6 17.2 %copy-start.14 = (f32[2,48,1152]{2,1,0:T(8,128)S(1)}, f32[2,48,1152]{2,1,0:T(8,128)}, u32[]{:S(2)}) copy-start(f32[2,48,1152]{2,1,0:T(8,128)} %copy-done.13) | copy-start | bytes 1327108
  375.7 36.5 %collective-permute-start.49 = (bf16[1024,768]{1,0:T(8,128)(2,1)}, bf16[1024,768]{1,0:T(8,128)(2,1)}, u32[]{:S(2)}, u32[]{:S(2)}) collective-permute-start(bf16[1024,768]{1,0:T(8,128)(2,1)} %fusion), channel_id=1, source_target_pairs={{0,2},{1,3},{2,0},{3,1},{4,6},{5,7},{6,4},{7,5},{8,10},{9,11},{10,... | collective-permute-start | bytes 4718600 | tf_op jit(solution)/shard_map/ppermute | solution.py:60
  382.6 8.2 %collective-permute-start.45 = (f32[12,768]{1,0:T(8,128)S(1)}, f32[12,768]{1,0:T(8,128)S(1)}, u32[]{:S(2)}, u32[]{:S(2)}) collective-permute-start(f32[12,768]{1,0:T(8,128)S(1)} %add.438), channel_id=1, source_target_pairs={{0,16},{4,20},{8,24},{12,28},{16,0},{20,4},{24,8},{28,12},{1,17},{... | collective-permute-start | bytes 110600 | tf_op jit(solution)/shard_map/ppermute | solution.py:60
  384.7 8.2 %collective-permute-start.44 = (bf16[48,1152]{1,0:T(8,128)(2,1)S(1)}, bf16[48,1152]{1,0:T(8,128)(2,1)S(1)}, u32[]{:S(2)}, u32[]{:S(2)}) collective-permute-start(bf16[48,1152]{1,0:T(8,128)(2,1)S(1)} %fusion.27), channel_id=1, source_target_pairs={{0,16},{4,20},{8,24},{12,28},{16,0},{20,4},{24,8},{28,12},{1,17},{... | collective-permute-start | bytes 331784 | tf_op jit(solution)/shard_map/ppermute | solution.py:60
  385.6 26.6 %copy-start.1 = (f32[1,1024,768]{2,1,0:T(8,128)S(1)}, f32[1,1024,768]{2,1,0:T(8,128)}, u32[]{:S(2)}) copy-start(f32[1,1024,768]{2,1,0:T(8,128)} %token_grad.3) | copy-start | bytes 9437188
  394.5 13.8 %collective-permute-start.52 = (f32[24,1152]{1,0:T(8,128)S(1)}, f32[24,1152]{1,0:T(8,128)}, u32[]{:S(2)}, u32[]{:S(2)}) collective-permute-start(f32[24,1152]{1,0:T(8,128)S(1)} %dynamic-slice_bitcast_fusion.2), channel_id=1, source_target_pairs={{0,1},{1,0},{2,3},{3,2},{4,5},{5,4},{6,7},{7,6},{8,9},{9,8},{10,11... | collective-permute-start | bytes 331784 | tf_op jit(solution)/shard_map/ppermute | solution.py:60
  397.9 1.4 collective-permute-start.46
  399.9 3.6 collective-permute-start.47
  404.1 3.6 collective-permute-start.48
  416.2 4.4 %collective-permute-start.50 = (f32[1,1]{1,0:T(1,128)}, f32[1,1]{1,0:T(1,128)}, u32[]{:S(2)}, u32[]{:S(2)}) collective-permute-start(f32[1,1]{1,0:T(1,128)} %add.447), channel_id=1, source_target_pairs={{0,16},{4,20},{8,24},{12,28},{16,0},{20,4},{24,8},{28,12},{1,17},{... | collective-permute-start | bytes 20 | tf_op jit(solution)/shard_map/ppermute | solution.py:60
  421.2 3.6 collective-permute-start.51
  (44 other events, 114.1 us)
where the time goes:
time: 439 us; the launch traced here: 434 us
  Pallas kernels  239 us (54%)
  waiting for transfers between devices  68.3 us (16%)
  starting transfers between devices  51.3 us (12%)
  other arithmetic  44.4 us (10%)
  local copies, waits for them, and re-layouts  22.7 us (5%)
  between operations  8.21 us (2%)
    ppermute x53, waiting for transfers between devices, swap(): lax.ppermute(x, axis, [(i, i ^ bit) for i in range(lax.axis_size(axis))])  68.3 us
    pallas_call x2, Pallas kernels, attend_back(): pl.pallas_call(skipping(functools.partial(attend_back_kernel, blocks, sta...  56.6 us
    ppermute x53, starting transfers between devices, swap(): lax.ppermute(x, axis, [(i, i ^ bit) for i in range(lax.axis_size(axis))])  51.3 us
    pallas_call x1, Pallas kernels, feed(): pl.pallas_call(feed_kernel, grid_spec=pltpu.PrefetchScalarGridSpec(num_sc...  40.9 us
    pallas_call x2, Pallas kernels, feed_grad(): pl.pallas_call(functools.partial(feed_grad_kernel, added), grid_spec=pltp...  34.3 us
    pallas_call x2, Pallas kernels, attend(): pl.pallas_call(skipping(functools.partial(attend_kernel, blocks, start),...  28.4 us
    pallas_call x2, Pallas kernels, token_grad(): pl.pallas_call(skipping(functools.partial(token_grad_kernel, steps, sent,...  22.3 us
    pallas_call x1, Pallas kernels, project(): pl.pallas_call(skipping(functools.partial(project_kernel, spans, steps),...  19.9 us
  transfers between devices with their start and end apart: 53, of which 25 were waited for; matrix products, arithmetic and copies ran while one was open for 9% of the time, Pallas kernels for 38%

commit v1 on v0

--- a/solution.py
+++ b/solution.py
@@ -380,39 +380,42 @@
     def body(count):
         q = q_ref[0]
         do = do_ref[0]
-        q_heads = head_parts(q)
-        do_heads = head_parts(do)
+        q_both = jnp.concatenate(head_parts(q))
+        do_both = jnp.concatenate(head_parts(do))
         q_turned = q.T
         do_turned = do.T
         o = o_ref[0].astype(F32)
-        dk = [[], []]
-        dv = [[], []]
-        dq = []
-        for h in range(2):
-            rows = slice(h * head_dim, (h + 1) * head_dim)
-            shift = DISTILL - jnp.sum(do_heads[h].astype(F32) * o, axis=1, keepdims=True)
-            lse = lse_ref[0, 0][:, h * head_dim : h * head_dim + 1]
-            share_h = share_ref[0, 0][:, h * head_dim : h * head_dim + 1]
-            for j in range(count):
-                d = plan[r, 1 + j]
-                k = k_ref[d, 0]
-                p = jnp.exp(dot_nt(q_heads[h], k) + bias_scr[d] - lse)
-                dp = dot_nt(do_heads[h], v_ref[d, 0])
-                place = pl.multiple_of(jnp.bitwise_xor(seq_rank, d) * length, LANES)
-                t = (teach_ref[0, h, :, pl.ds(place, length)] * mask_scr[d]).astype(F32)
-                ds = (p * (dp + shift) - t * share_h).astype(BF16)
-                dv[h].append(dot(do_turned[rows], p.astype(BF16)))
-                dk[h].append(dot(q_turned[rows], ds))
-                part = dot(ds, k)
-                if j == 0:
-                    dq.append(part)
-                else:
-                    dq[h] = dq[h] + part
+        col = do_both.astype(F32) * jnp.concatenate([o, o])
+        shift = DISTILL - jnp.sum(col, axis=1, keepdims=True)
+
+        def columns(x):
+            return jnp.concatenate([x[:, :1], x[:, head_dim : head_dim + 1]])
+
+        lse = columns(lse_ref[0, 0])
+        share_both = columns(share_ref[0, 0])
+        dq = None
         for j in range(count):
             d = plan[r, 1 + j]
-            dk_ref[d, 0] = jnp.concatenate([dk[0][j], dk[1][j]]).astype(BF16).T
-            dv_ref[d, 0] = jnp.concatenate([dv[0][j], dv[1][j]]).astype(BF16).T
-        dq_ref[0] = (pick_lanes(dq[0], dq[1]) * head_dim**-0.5).astype(BF16)
+            k = k_ref[d, 0]
+            bias, mask = bias_scr[d], mask_scr[d]
+            p = jnp.exp(dot_nt(q_both, k) + jnp.concatenate([bias, bias]) - lse)
+            dp = dot_nt(do_both, v_ref[d, 0])
+            place = pl.multiple_of(jnp.bitwise_xor(seq_rank, d) * length, LANES)
+            t = teach_ref[0, :, :, pl.ds(place, length)].reshape(2 * length, length)
+            t = (t * jnp.concatenate([mask, mask])).astype(F32)
+            ds = (p * (dp + shift) - t * share_both).astype(BF16)
+            p = p.astype(BF16)
+            part = dot(ds, k)
+            dq = part if j == 0 else dq + part
+            dv, dk = [], []
+            for h in range(2):
+                rows = slice(h * head_dim, (h + 1) * head_dim)
+                mine = slice(h * length, (h + 1) * length)
+                dv.append(dot(do_turned[rows], p[mine]))
+                dk.append(dot(q_turned[rows], ds[mine]))
+            dk_ref[d, 0] = jnp.concatenate(dk).astype(BF16).T
+            dv_ref[d, 0] = jnp.concatenate(dv).astype(BF16).T
+        dq_ref[0] = (pick_lanes(dq[:length], dq[length:]) * head_dim**-0.5).astype(BF16)
 
     for count in range(1, blocks + 1):
         pl.when(plan[r, 0] == count)(functools.partial(body, count))
@@ -626,6 +629,13 @@
 
 def feed_grad_kernel(added, meta, h1_ref, du_ref, gl_ref, dz_ref, ol_ref, da_ref, *refs):
     got_ref = refs[0] if added else None
+
+    def turned(ref, index):
+        if added:
+            return ref[...]
+        refs[index][...] = ref[...].T
+        return refs[index][...]
+
     scr = refs[-1]
     step = pl.program_id(0)
     half = dz_ref.shape[1]
@@ -669,20 +679,20 @@
 
     @pl.when(step == 0)
     def _():
-        scr[:, :half] = dot_tn(ol_ref[...], da_ref[...])
+        scr[:, :half] = dot(turned(ol_ref, 3), da_ref[...])
         put_all(we_rows, slice(0, half))
 
     for u in range(2):
 
         @pl.when(step == u)
         def _(u=u):
-            scr[...] = dot_tn(h1_ref[...], du_ref[...])
+            scr[...] = dot(turned(h1_ref, 1), du_ref[...])
             for k in range(width // half):
                 put_all((2 * u + k) * SLAB, slice(k * half, (k + 1) * half))
 
     @pl.when(step >= 2)
     def _():
-        scr[:, :half] = dot_tn(gl_ref[...], dz_ref[...])
+        scr[:, :half] = dot(turned(gl_ref, 2), dz_ref[...])
         z = jnp.bitwise_xor(meta[20], step - 2)
         for x in range(2):
             for y in range(2):
@@ -692,7 +702,7 @@
 
 
 def feed_grad(meta, h1, du, gl, dz, ol, da, got):
-    tokens, width = h1.shape
+    tokens, width = du.shape[0], dz.shape[1]
     half = width // 2
     wide = lambda index: pl.BlockSpec((tokens, width), index)
     added = got is not None
@@ -702,6 +712,18 @@
         outs = [((4,), F32), ((2,), F32), ((2,), F32), ((2, 2), BF16), ((2, 2), BF16)]
     else:
         outs = [(every, BF16)]
+    left = (width, tokens) if added else (tokens, width)
+    low_full = pl.BlockSpec(left, lambda u, m: (0, 0))
+    tall = lambda index: pl.BlockSpec((width, tokens), index)
+    step_of = lambda u: jnp.clip(u - 2, 0, 3)
+    if added:
+        gl_spec = tall(lambda u, m: (step_of(u), 0))
+        turned_specs, turned_shapes = [], []
+    else:
+        gl_spec = wide(lambda u, m: (0, step_of(u)))
+        once = tall(lambda u, m: (0, 0))
+        turned_specs = [once, tall(lambda u, m: (step_of(u), 0)), once]
+        turned_shapes = [(width, tokens), (4 * width, tokens), (width, tokens)]
     slab_spec = lambda lead: pl.BlockSpec(lead + slab, lambda u, m: (0,) * (len(lead) + 2))
     return pl.pallas_call(
         functools.partial(feed_grad_kernel, added),
@@ -709,18 +731,19 @@
             num_scalar_prefetch=1,
             grid=(6,),
             in_specs=[
-                wide(lambda u, m: (0, 0)),
+                low_full,
                 wide(lambda u, m: (0, 2 * m[0] + jnp.minimum(u, 1))),
-                wide(lambda u, m: (0, jnp.clip(u - 2, 0, 3))),
+                gl_spec,
                 pl.BlockSpec((tokens, half), lambda u, m: (0, m[0])),
-                wide(lambda u, m: (0, 0)),
+                low_full,
                 pl.BlockSpec((tokens, half), lambda u, m: (0, m[0])),
             ]
             + [slab_spec(every)] * added,
-            out_specs=[slab_spec(lead) for lead, _ in outs],
+            out_specs=[slab_spec(lead) for lead, _ in outs] + turned_specs,
             scratch_shapes=[pltpu.VMEM((width, width), F32)],
         ),
-        out_shape=[jax.ShapeDtypeStruct(lead + slab, dtype) for lead, dtype in outs],
+        out_shape=[jax.ShapeDtypeStruct(lead + slab, dtype) for lead, dtype in outs]
+        + [jax.ShapeDtypeStruct(shape, BF16) for shape in turned_shapes],
         compiler_params=params(1),
         cost_estimate=cost(9 * tokens * width * width, 16 * tokens * width),
         name="feed_grad",
@@ -1032,14 +1055,13 @@
             ]
         )
         joint_z = jnp.concatenate([joint_pair, swap(joint_pair, "dp", 2)])
-        joint_z, rest_piece, tokens_core, tokens_y[0] = stage(
-            joint_z, rest_piece, tokens_core, tokens_y[0]
-        )
+        joint_z, rest_piece, tokens_core = stage(joint_z, rest_piece, tokens_core)
         shares = [share(teacher, segq, seg_row, 0, 2, (joint_z,))]
-        joint_y, joint_x, rest_got, shares[0] = stage(
+        joint_y, joint_x, rest_got, tokens_y[0], shares[0] = stage(
             swap(joint_z, "seq", 2),
             swap(joint_z, "dp", 1),
             swap(rest_piece, "dp", 4),
+            tokens_y[0],
             shares[0],
         )
         rest_pair = jnp.stack([rest_piece, rest_got])
@@ -1124,7 +1146,8 @@
     )
     layer_output = by_rows(layer_output)
     grad_args = (h1, du, gl, dz, flat(attended), da)
-    rest_theirs = feed_grad(meta_other, *grad_args, None)[0]
+    rest_theirs, h1, gl, turned = feed_grad(meta_other, *grad_args, None)
+    grad_args = (h1, du, gl, dz, turned, da)
     back_args = (
         meta, plan, q, k, v, by_rows(d_att), attended, lse, shares, teacher, segq, segk
     )

time: 439 us -> 433 us (0.986)
  waiting for transfers between devices: 68.3 us -> 48.2 us
  Pallas kernels: 239 us -> 250 us
    ppermute x53, waiting for transfers between devices: 68.3 us -> 48.2 us  [swap(): lax.ppermute(x, axis, [(i, i ^ bit) for i in range(lax.axis_size(axis))])]
    pallas_call x2, Pallas kernels: 56.6 us -> 61.1 us  [attend_back(): pl.pallas_call(skipping(functools.partial(attend_back_kernel, blocks, sta...]
  transfers between devices with their start and end apart: 53 -> 53, of which waited for: 25 -> 19; matrix products, arithmetic and copies ran while one was open for 9% -> 9% of each run, Pallas kernels for 38% -> 40%
where the time goes in v1:
time: 433 us; the launch traced here: 429 us
  Pallas kernels  250 us (58%)
  starting transfers between devices  54.1 us (12%)
  waiting for transfers between devices  48.2 us (11%)
  other arithmetic  44.4 us (10%)
  local copies, waits for them, and re-layouts  23.9 us (6%)
  between operations  8.3 us (2%)
    pallas_call x2, Pallas kernels, attend_back(): pl.pallas_call(skipping(functools.partial(attend_back_kernel, blocks, sta...  61.1 us
    ppermute x53, starting transfers between devices, swap(): lax.ppermute(x, axis, [(i, i ^ bit) for i in range(lax.axis_size(axis))])  54.1 us
    ppermute x53, waiting for transfers between devices, swap(): lax.ppermute(x, axis, [(i, i ^ bit) for i in range(lax.axis_size(axis))])  48.2 us
    pallas_call x1, Pallas kernels, feed(): pl.pallas_call(feed_kernel, grid_spec=pltpu.PrefetchScalarGridSpec(num_sc...  40.9 us
    pallas_call x2, Pallas kernels, feed_grad(): pl.pallas_call(functools.partial(feed_grad_kernel, added), grid_spec=pltp...  36.3 us
    pallas_call x2, Pallas kernels, attend(): pl.pallas_call(skipping(functools.partial(attend_kernel, blocks, start),...  30.5 us
    pallas_call x2, Pallas kernels, token_grad(): pl.pallas_call(skipping(functools.partial(token_grad_kernel, steps, sent,...  23.6 us
    pallas_call x1, Pallas kernels, project(): pl.pallas_call(skipping(functools.partial(project_kernel, spans, steps),...  21.5 us
  transfers between devices with their start and end apart: 53, of which 19 were waited for; matrix products, arithmetic and copies ran while one was open for 9% of the time, Pallas kernels for 40%

profile of v1, /device:TPU:0, one launch (start us, length us, event | category | flops | bytes accessed | tf_op | source)
XLA Modules:
  0.0 429.3 jit_solution(9744415101591881057)
XLA Ops:
  4.4 1.2 fusion.46
  6.4 3.7 collective-permute-start.1
  11.0 1.5 collective-permute-start.8
  13.4 3.3 collective-permute-done.1
  17.7 6.7 %collective-permute-done.2 = bf16[2,48,1280]{2,1,0:T(8,128)(2,1)S(1)} collective-permute-done((bf16[2,48,1280]{2,1,0:T(8,128)(2,1)S(1)}, bf16[2,48,1280]{2,1,0:T(8,128)(2,1)S(1)}, u32[]{:S(2)}, u32[]{:S(2)}) %collective-permute-start.2) | collective-permute-done | bytes 245792 | tf_op jit(solution)/shard_map/ppermute | solution.py:60
  25.3 1.4 collective-permute-start.6
  26.7 1.5 collective-permute-start.5
  28.6 2.7 collective-permute-start.7
  33.4 8.6 %share.2.refs_5_.refs_8_ = f32[2,6,256,128]{3,2,1,0:T(8,128)} custom-call(bf16[4,12,256,1024]{3,2,1,0:T(8,128)(2,1)} %refs_9_.3, s32[4,256,128]{2,1,0:T(8,128)} %broadcast_in_dim.62.refs_1_.refs_4_.refs_10_, s32[4,8,1024]{2,1,0:T(8,128)} %broadcast_in_dim.63.refs_2_, bf16[4,48,1280]{2,1,0:T(8,128)(2,1)} %pad_maximum_fusion.6.refs_3_.refs_8_), custom_call_target="tpu_custom_call" | custom-call | flops 25165824 | bytes 12582912 | tf_op jit(solution)/shard_map/share/pallas_call | solution.py:228
  42.1 3.4 collective-permute-done.7
  45.5 1.5 pad_maximum_fusion
  52.2 8.2 %share.3.refs_15_.refs_8_ = f32[2,6,256,128]{3,2,1,0:T(8,128)} custom-call(bf16[4,12,256,1024]{3,2,1,0:T(8,128)(2,1)} %refs_9_.3, s32[4,256,128]{2,1,0:T(8,128)} %broadcast_in_dim.62.refs_1_.refs_4_.refs_10_, s32[4,8,1024]{2,1,0:T(8,128)} %broadcast_in_dim.63.refs_2_, bf16[4,48,1280]{2,1,0:T(8,128)(2,1)} %copy-done.8, bf16[4,48,1280]{2,1,0:T(8,128)(2,1)} %copy-done.9, ...), custom_call_target="tpu_custom_call" | custom-call | flops 25165824 | bytes 12582912 | tf_op jit(solution)/shard_map/share/pallas_call | solution.py:228
  60.4 1.6 collective-permute-done.9.refs_11_
  64.4 3.5 collective-permute-done.13
  67.9 3.0 collective-permute-done.14
  71.7 1.3 pad_maximum_fusion.1.refs_0_
  73.0 1.6 collective-permute-start.17
  75.0 21.5 %project.1 = (bf16[1024,768]{1,0:T(8,128)(2,1)}, bf16[4,1024,768]{2,1,0:T(8,128)(2,1)}, bf16[4,1024,768]{2,1,0:T(8,128)(2,1)}, bf16[768,2304]{1,0:T(8,128)(2,1)}) custom-call(s32[23]{0:T(128)} %stack.146.refs_0_.meta, s32[4,4]{1,0:T(4,128)} %copy-done.42, bf16[1024,768]{1,0:T(8,128)(2,1)} %bitcast.252, bf16[1024,768]{1,0:T(8,128)(2,1)} %bitcast.44.refs_3_.refs_2_, ...), custom_call_target="tpu_custom_call" | custom-call | flops 10871635968 | bytes 12582912 | tf_op jit(solution)/shard_map/project/pallas_call | solution.py:179
  97.2 14.1 %attend.2 = (bf16[4,256,768]{2,1,0:T(8,128)(2,1)}, f32[4,6,256,128]{3,2,1,0:T(8,128)}) custom-call(s32[4,5]{1,0:T(4,128)} %pad_add_fusion.refs_0_.refs_1_, bf16[4,256,768]{2,1,0:T(8,128)(2,1)} %bitcast.255, bf16[4,4,256,768]{3,2,1,0:T(8,128)(2,1)} %bitcast.241, bf16[4,4,256,768]{3,2,1,0:T(8,128)(2,1)} %bitcast.245, ...), custom_call_target="tpu_custom_call" | custom-call | flops 6442450944 | bytes 3145728 | tf_op jit(solution)/shard_map/attend/pallas_call | solution.py:337
  113.7 2.8 collective-permute-start.19
  116.4 1.4 collective-permute-start.18
  118.4 16.4 %attend.3 = (bf16[4,256,768]{2,1,0:T(8,128)(2,1)}, f32[4,6,256,128]{3,2,1,0:T(8,128)}) custom-call(s32[4,5]{1,0:T(4,128)} %pad_add_fusion.refs_0_.refs_1_, bf16[4,256,768]{2,1,0:T(8,128)(2,1)} %bitcast.256, bf16[4,4,256,768]{3,2,1,0:T(8,128)(2,1)} %bitcast.242, bf16[4,4,256,768]{3,2,1,0:T(8,128)(2,1)} %bitcast.246, ...), custom_call_target="tpu_custom_call", output_to_operand_aliasing={{0}: (6, {}), {1}: (7, {})} | custom-call | flops 6442450944 | bytes 3145728 | tf_op jit(solution)/shard_map/attend/pallas_call | solution.py:337
  136.2 1.3 collective-permute-done.23.refs_8_
  138.9 40.9 %feed.1 = (bf16[1024,768]{1,0:T(8,128)(2,1)}, f32[1024,768]{1,0:T(8,128)}, bf16[1024,768]{1,0:T(8,128)(2,1)}, bf16[1024,3072]{1,0:T(8,128)(2,1)}, bf16[1024,3072...) custom-call(s32[23]{0:T(128)} %stack.146.refs_0_.meta, ...), custom_call_target="tpu_custom_call" | custom-call | flops 21743271936 | bytes 28311552 | tf_op jit(solution)/shard_map/feed/pallas_call | solution.py:590
  179.8 17.8 %feed_grad.2 = (bf16[2,2,4,432,384]{4,3,2,1,0:T(8,128)(2,1)}, bf16[768,1024]{1,0:T(8,128)(2,1)}, bf16[3072,1024]{1,0:T(8,128)(2,1)}, bf16[768,1024]{1,0:T(8,128)(2,1)}) custom-call(s32[23]{0:T(128)} %copy-done.54, bf16[1024,768]{1,0:T(8,128)(2,1)} %get-tuple-element.156.h1_ref, bf16[1024,3072]{1,0:T(8,128)(2,1)} %get-tuple-element.157.du_ref, ...), custom_call_target="tpu_custom_call" | custom-call | flops 5435817984 | bytes 12582912 | tf_op jit(solution)/shard_map/feed_grad/pallas_call | solution.py:728
  198.3 28.3 %attend_back.2 = (bf16[4,256,768]{2,1,0:T(8,128)(2,1)}, bf16[4,4,256,768]{3,2,1,0:T(8,128)(2,1)}, bf16[4,4,256,768]{3,2,1,0:T(8,128)(2,1)}) custom-call(s32[23]{0:T(128)} %stack.146.refs_0_.meta, s32[4,5]{1,0:T(4,128)} %pad_add_fusion.refs_0_.refs_1_, bf16[4,256,768]{2,1,0:T(8,128)(2,1)} %bitcast.257, bf16[4,4,256,768]{3,2,1,0:T(8,128)(2,1)} %bitcast.243, ...), custom_call_target="tpu_custom_call" | custom-call | flops 16106127360 | bytes 6291456 | tf_op jit(solution)/shard_map/attend_back/pallas_call | solution.py:441
  226.5 18.4 %feed_grad.3 = (f32[4,432,384]{2,1,0:T(8,128)}, f32[2,432,384]{2,1,0:T(8,128)}, f32[2,432,384]{2,1,0:T(8,128)}, bf16[2,2,432,384]{3,2,1,0:T(8,128)(2,1)}, bf16[2,2,432,384]{3,2,1,0:T(8,128)(2,1)}) custom-call(s32[23]{0:T(128)} %stack.146.refs_0_.meta, bf16[768,1024]{1,0:T(8,128)(2,1)} %get-tuple-element.165.h1_ref, ...), custom_call_target="tpu_custom_call" | custom-call | flops 5435817984 | bytes 12582912 | tf_op jit(solution)/shard_map/feed_grad/pallas_call | solution.py:728
  245.0 3.0 collective-permute-start.26
  248.0 1.6 collective-permute-start.27
  249.6 32.8 %attend_back.3 = (bf16[4,256,768]{2,1,0:T(8,128)(2,1)}, bf16[4,4,256,768]{3,2,1,0:T(8,128)(2,1)}, bf16[4,4,256,768]{3,2,1,0:T(8,128)(2,1)}) custom-call(s32[23]{0:T(128)} %stack.146.refs_0_.meta, s32[4,5]{1,0:T(4,128)} %pad_add_fusion.refs_0_.refs_1_, bf16[4,256,768]{2,1,0:T(8,128)(2,1)} %bitcast.258, ...), custom_call_target="tpu_custom_call", output_to_operand_aliasing={{0}: (12, {}), {1}: (13, {}), {2}: (14, {})} | custom-call | flops 16106127360 | bytes 6291456 | tf_op jit(solution)/shard_map/attend_back/pallas_call | solution.py:441
  283.5 1.6 convert_element_type.137
  286.4 1.6 copy-done.15
  289.1 19.8 %joint_grad.1 = (f32[2,2,4,48,1152]{4,3,2,1,0:T(8,128)}, bf16[2,2,4,48,1152]{4,3,2,1,0:T(8,128)(2,1)}, f32[8,768]{1,0:T(8,128)}) custom-call(s32[23]{0:T(128)} %stack.146.refs_0_.meta, bf16[1024,768]{1,0:T(8,128)(2,1)} %bitcast.254, bf16[1024,768]{1,0:T(8,128)(2,1)} %bitcast.44.refs_3_.refs_2_, bf16[512,768]{1,0:T(8,128)(2,1)} %bitcast.46.refs_4_.refs_3_, ...), custom_call_target="tpu_custom_call" | custom-call | flops 10871635968 | bytes 25165824 | tf_op jit(solution)/shard_map/joint_grad/pallas_call | solution.py:871
  308.8 2.7 fusion.4
  314.0 14.0 %token_grad.2 = (bf16[2,1024,768]{2,1,0:T(8,128)(2,1)}, bf16[1,1024,768]{2,1,0:T(8,128)(2,1)}) custom-call(s32[23]{0:T(128)} %stack.146.refs_0_.meta, s32[4,4]{1,0:T(4,128)} %copy-done.42, bf16[4,1024,768]{2,1,0:T(8,128)(2,1)} %bitcast.234, bf16[4,1024,768]{2,1,0:T(8,128)(2,1)} %bitcast.237, bf16[768,2304]{1,0:T(8,128)(2,1)} %get-tuple-element.173.refs_4_, ...), custom_call_target="tpu_custom_call" | custom-call | flops 7247757312 | bytes 14155776 | tf_op jit(solution)/shard_map/token_grad/pallas_call | solution.py:800
  330.2 1.3 collective-permute-start.32
  331.5 2.9 collective-permute-done.32
  335.3 3.0 fusion.44
  338.4 1.3 collective-permute-start.34
  342.6 3.0 collective-permute-start.39
  345.6 9.5 %token_grad.3 = f32[1,1024,768]{2,1,0:T(8,128)} custom-call(s32[23]{0:T(128)} %stack.146.refs_0_.meta, s32[4,4]{1,0:T(4,128)} %copy-done.42, bf16[4,1024,768]{2,1,0:T(8,128)(2,1)} %bitcast.235, bf16[4,1024,768]{2,1,0:T(8,128)(2,1)} %bitcast.238, bf16[768,2304]{1,0:T(8,128)(2,1)} %get-tuple-element.173.refs_4_, bf16[1024,768]{1,0:T(8,128)(2,1)} %bitcast.240, ...), custom_call_target="tpu_custom_call" | custom-call | flops 2415919104 | bytes 4718592 | tf_op jit(solution)/shard_map/token_grad/pallas_call | solution.py:800
  355.2 1.3 collective-permute-start.40
  360.4 3.2 fusion
  363.6 1.3 collective-permute-done.38
  365.7 1.8 multiply_reduce_fusion
  370.9 1.2 collective-permute-start.49
  372.1 5.6 %collective-permute-done.42 = f32[12,768]{1,0:T(8,128)S(1)} collective-permute-done((f32[12,768]{1,0:T(8,128)S(1)}, f32[12,768]{1,0:T(8,128)S(1)}, u32[]{:S(2)}, u32[]{:S(2)}) %collective-permute-start.42) | collective-permute-done | bytes 36896 | tf_op jit(solution)/shard_map/ppermute | solution.py:60
  378.6 2.2 collective-permute-start.44
  380.8 1.3 bitcast_select_fusion.1
  383.0 3.3 collective-permute-done.45
  388.1 1.6 multiply_reduce_fusion.1
  391.0 1.4 multiply_reduce_fusion.2
  393.1 1.5 collective-permute-start.46
  395.2 2.1 collective-permute-start.47
  397.2 1.6 collective-permute-done.47
  399.4 1.4 collective-permute-start.48
  400.8 2.3 collective-permute-done.48
  403.7 1.6 bitcast_select_fusion.3
  405.3 2.2 collective-permute-done.49
  407.5 4.0 bitcast_add_fusion
  411.4 2.0 collective-permute-start.50
  413.4 2.4 collective-permute-done.50
  416.5 2.6 collective-permute-start.51
  421.8 1.2 multiply_bitcast_fusion
  (302 shorter events, 56.1 us)
Async XLA Ops:
  2.9 3.4 collective-permute-start
  4.4 6.3 %copy-start.21 = (f32[96,768]{1,0:T(8,128)S(1)}, f32[96,768]{1,0:T(8,128)}, u32[]{:S(2)}) copy-start(f32[96,768]{1,0:T(8,128)} %param.29) | copy-start | bytes 884740
  6.4 10.3 %collective-permute-start.1 = (bf16[48,1280]{1,0:T(8,128)(2,1)S(1)}, bf16[48,1280]{1,0:T(8,128)(2,1)S(1)}, u32[]{:S(2)}, u32[]{:S(2)}) collective-permute-start(bf16[48,1280]{1,0:T(8,128)(2,1)S(1)} %maximum_select_fusion.1), channel_id=1, source_target_pairs={{0,16},{4,20},{8,24},{12,28},{16,0},{20,4},{24,8},{28,12},{1,17},{... | collective-permute-start | bytes 368648 | tf_op jit(solution)/shard_map/ppermute | solution.py:60
  10.8 6.7 %collective-permute-start.3 = (bf16[216,384]{1,0:T(8,128)(2,1)S(1)}, bf16[216,384]{1,0:T(8,128)(2,1)S(1)}, u32[]{:S(2)}, u32[]{:S(2)}) collective-permute-start(bf16[216,384]{1,0:T(8,128)(2,1)S(1)} %get-tuple-element.260), channel_id=1, source_target_pairs={{0,1},{1,0},{2,3},{3,2},{4,5},{5,4},{6,7},{7,6},{8,9},{9,8},{10,11... | collective-permute-start | bytes 497672 | tf_op jit(solution)/shard_map/ppermute | solution.py:60
  11.0 31.0 %collective-permute-start.8 = (bf16[2,256,768]{2,1,0:T(8,128)(2,1)}, bf16[2,256,768]{2,1,0:T(8,128)(2,1)}, u32[]{:S(2)}, u32[]{:S(2)}) collective-permute-start(bf16[2,256,768]{2,1,0:T(8,128)(2,1)} %get-tuple-element.128), channel_id=1, source_target_pairs={{0,2},{1,3},{2,0},{3,1},{4,6},{5,7},{6,4},{7,5},{8,10},{9,11},{10,... | collective-permute-start | bytes 2359304 | tf_op jit(solution)/shard_map/ppermute | solution.py:60
  12.6 12.7 %collective-permute-start.4 = (bf16[4,256,768]{2,1,0:T(8,128)(2,1)S(1)}, bf16[4,256,768]{2,1,0:T(8,128)(2,1)}, u32[]{:S(2)}, u32[]{:S(2)}) collective-permute-start(bf16[4,256,768]{2,1,0:T(8,128)(2,1)S(1)} %copy-done.11), channel_id=1, source_target_pairs={{0,1},{1,0},{2,3},{3,2},{4,5},{5,4},{6,7},{7,6},{8,9},{9,8},{10,11... | collective-permute-start | bytes 4718600 | tf_op jit(solution)/shard_map/ppermute | solution.py:60
  16.7 7.8 %collective-permute-start.2 = (bf16[2,48,1280]{2,1,0:T(8,128)(2,1)S(1)}, bf16[2,48,1280]{2,1,0:T(8,128)(2,1)S(1)}, u32[]{:S(2)}, u32[]{:S(2)}) collective-permute-start(bf16[2,48,1280]{2,1,0:T(8,128)(2,1)S(1)} %pad_maximum_fusion.11), channel_id=1, source_target_pairs={{0,8},{4,12},{8,0},{12,4},{16,24},{20,28},{24,16},{28,20},{1,9},{5... | collective-permute-start | bytes 737288 | tf_op jit(solution)/shard_map/ppermute | solution.py:60
  25.3 20.2 %collective-permute-start.6 = (bf16[4,48,1280]{2,1,0:T(8,128)(2,1)}, bf16[4,48,1280]{2,1,0:T(8,128)(2,1)S(1)}, u32[]{:S(2)}, u32[]{:S(2)}) collective-permute-start(bf16[4,48,1280]{2,1,0:T(8,128)(2,1)} %pad_maximum_fusion.6.refs_3_.refs_8_), channel_id=1, source_target_pairs={{0,4},{4,0},{8,12},{12,8},{16,20},{20,16},{24,28},{28,24},{1,5},{5... | collective-permute-start | bytes 1474568 | tf_op jit(solution)/shard_map/ppermute | solution.py:60
  26.7 18.8 %collective-permute-start.5 = (bf16[4,48,1280]{2,1,0:T(8,128)(2,1)}, bf16[4,48,1280]{2,1,0:T(8,128)(2,1)S(1)}, u32[]{:S(2)}, u32[]{:S(2)}) collective-permute-start(bf16[4,48,1280]{2,1,0:T(8,128)(2,1)} %pad_maximum_fusion.6.refs_3_.refs_8_), channel_id=1, source_target_pairs={{0,2},{1,3},{2,0},{3,1},{4,6},{5,7},{6,4},{7,5},{8,10},{9,11},{10,... | collective-permute-start | bytes 1474568 | tf_op jit(solution)/shard_map/ppermute | solution.py:60
  28.6 16.9 %collective-permute-start.7 = (bf16[432,384]{1,0:T(8,128)(2,1)S(1)}, bf16[432,384]{1,0:T(8,128)(2,1)S(1)}, u32[]{:S(2)}, u32[]{:S(2)}) collective-permute-start(bf16[432,384]{1,0:T(8,128)(2,1)S(1)} %pad_maximum_fusion.10), channel_id=1, source_target_pairs={{0,16},{4,20},{8,24},{12,28},{16,0},{20,4},{24,8},{28,12},{1,17},{... | collective-permute-start | bytes 995336 | tf_op jit(solution)/shard_map/ppermute | solution.py:60
  31.4 15.9 %copy-start.42 = (s32[4,4]{1,0:T(4,128)}, s32[4,4]{1,0:T(4,128)S(1)}, u32[]{:S(2)}) copy-start(s32[4,4]{1,0:T(4,128)S(1)} %get-tuple-element.236.refs_1_) | copy-start | bytes 196
  45.5 6.7 %copy-start.8 = (bf16[4,48,1280]{2,1,0:T(8,128)(2,1)}, bf16[4,48,1280]{2,1,0:T(8,128)(2,1)S(1)}, u32[]{:S(2)}) copy-start(bf16[4,48,1280]{2,1,0:T(8,128)(2,1)S(1)} %collective-permute-done.6.refs_3_.refs_10_) | copy-start | bytes 1474564
  47.1 15.0 %collective-permute-start.11 = (bf16[12,48,1280]{2,1,0:T(8,128)(2,1)S(1)}, bf16[12,48,1280]{2,1,0:T(8,128)(2,1)}, u32[]{:S(2)}, u32[]{:S(2)}) collective-permute-start(bf16[12,48,1280]{2,1,0:T(8,128)(2,1)S(1)} %pad_maximum_fusion), channel_id=1, source_target_pairs={{0,1},{1,0},{2,3},{3,2},{4,5},{5,4},{6,7},{7,6},{8,9},{9,8},{10,11... | collective-permute-start | bytes 4423688 | tf_op jit(solution)/shard_map/ppermute | solution.py:60
  48.2 13.8 %collective-permute-start.10 = (bf16[2,256,768]{2,1,0:T(8,128)(2,1)}, bf16[2,256,768]{2,1,0:T(8,128)(2,1)}, u32[]{:S(2)}, u32[]{:S(2)}) collective-permute-start(bf16[2,256,768]{2,1,0:T(8,128)(2,1)} %collective-permute-done.8), channel_id=1, source_target_pairs={{0,1},{1,0},{2,3},{3,2},{4,5},{5,4},{6,7},{7,6},{8,9},{9,8},{10,11... | collective-permute-start | bytes 2359304 | tf_op jit(solution)/shard_map/ppermute | solution.py:60
  48.8 13.3 %collective-permute-start.9 = (bf16[4,48,1280]{2,1,0:T(8,128)(2,1)S(1)}, bf16[4,48,1280]{2,1,0:T(8,128)(2,1)}, u32[]{:S(2)}, u32[]{:S(2)}) collective-permute-start(bf16[4,48,1280]{2,1,0:T(8,128)(2,1)S(1)} %collective-permute-done.5.refs_4_.refs_9_), channel_id=1, source_target_pairs={{0,4},{4,0},{8,12},{12,8},{16,20},{20,16},{24,28},{28,24},{1,5},{5... | collective-permute-start | bytes 1474568 | tf_op jit(solution)/shard_map/ppermute | solution.py:60
  51.0 16.9 %collective-permute-start.13 = (bf16[2,432,384]{2,1,0:T(8,128)(2,1)}, bf16[2,432,384]{2,1,0:T(8,128)(2,1)}, u32[]{:S(2)}, u32[]{:S(2)}) collective-permute-start(bf16[2,432,384]{2,1,0:T(8,128)(2,1)} %pad_maximum_fusion.2), channel_id=1, source_target_pairs={{0,8},{4,12},{8,0},{12,4},{16,24},{20,28},{24,16},{28,20},{1,9},{5... | collective-permute-start | bytes 1990664 | tf_op jit(solution)/shard_map/ppermute | solution.py:60
  51.7 19.2 %collective-permute-start.14 = (bf16[2,256,768]{2,1,0:T(8,128)(2,1)}, bf16[2,256,768]{2,1,0:T(8,128)(2,1)}, u32[]{:S(2)}, u32[]{:S(2)}) collective-permute-start(bf16[2,256,768]{2,1,0:T(8,128)(2,1)} %get-tuple-element.136), channel_id=1, source_target_pairs={{0,2},{1,3},{2,0},{3,1},{4,6},{5,7},{6,4},{7,5},{8,10},{9,11},{10,... | collective-permute-start | bytes 2359304 | tf_op jit(solution)/shard_map/ppermute | solution.py:60
  60.4 10.6 %copy-start.50 = (pred[8]{0:T(512)(128)(4,1)S(1)}, pred[8]{0:T(512)(128)(4,1)}, u32[]{:S(2)}) copy-start(pred[8]{0:T(512)(128)(4,1)} %constant.203.clone.1) | copy-start | bytes 28
  62.0 8.9 %collective-permute-start.12 = (bf16[4,48,1280]{2,1,0:T(8,128)(2,1)}, bf16[4,48,1280]{2,1,0:T(8,128)(2,1)S(1)}, u32[]{:S(2)}, u32[]{:S(2)}) collective-permute-start(bf16[4,48,1280]{2,1,0:T(8,128)(2,1)} %collective-permute-done.9.refs_11_), channel_id=1, source_target_pairs={{0,1},{1,0},{2,3},{3,2},{4,5},{5,4},{6,7},{7,6},{8,9},{9,8},{10,11... | collective-permute-start | bytes 1474568 | tf_op jit(solution)/shard_map/ppermute | solution.py:60
  70.9 4.1 collective-permute-start.15
  73.0 44.9 %copy-start.17 = (bf16[4,432,384]{2,1,0:T(8,128)(2,1)}, bf16[4,432,384]{2,1,0:T(8,128)(2,1)S(1)}, u32[]{:S(2)}) copy-start(bf16[4,432,384]{2,1,0:T(8,128)(2,1)S(1)} %pad_maximum_fusion.1.refs_0_) | copy-start | bytes 3981316
  73.0 38.4 %collective-permute-start.17 = (bf16[4,432,384]{2,1,0:T(8,128)(2,1)S(1)}, bf16[4,432,384]{2,1,0:T(8,128)(2,1)}, u32[]{:S(2)}, u32[]{:S(2)}) collective-permute-start(bf16[4,432,384]{2,1,0:T(8,128)(2,1)S(1)} %pad_maximum_fusion.1.refs_0_), channel_id=1, source_target_pairs={{0,4},{4,0},{8,12},{12,8},{16,20},{20,16},{24,28},{28,24},{1,5},{5... | collective-permute-start | bytes 3981320 | tf_op jit(solution)/shard_map/ppermute | solution.py:60
  74.5 36.8 %collective-permute-start.16 = (bf16[4,432,384]{2,1,0:T(8,128)(2,1)S(1)}, bf16[4,432,384]{2,1,0:T(8,128)(2,1)}, u32[]{:S(2)}, u32[]{:S(2)}) collective-permute-start(bf16[4,432,384]{2,1,0:T(8,128)(2,1)S(1)} %pad_maximum_fusion.1.refs_0_), channel_id=1, source_target_pairs={{0,2},{1,3},{2,0},{3,1},{4,6},{5,7},{6,4},{7,5},{8,10},{9,11},{10,... | collective-permute-start | bytes 3981320 | tf_op jit(solution)/shard_map/ppermute | solution.py:60
  113.7 21.2 %collective-permute-start.19 = (bf16[2,432,384]{2,1,0:T(8,128)(2,1)S(1)}, bf16[2,432,384]{2,1,0:T(8,128)(2,1)S(1)}, u32[]{:S(2)}, u32[]{:S(2)}) collective-permute-start(bf16[2,432,384]{2,1,0:T(8,128)(2,1)S(1)} %slice.234), channel_id=1, source_target_pairs={{0,2},{1,3},{2,0},{3,1},{4,6},{5,7},{6,4},{7,5},{8,10},{9,11},{10,... | collective-permute-start | bytes 1990664 | tf_op jit(solution)/shard_map/ppermute | solution.py:60
  116.4 18.4 %collective-permute-start.18 = (bf16[2,432,384]{2,1,0:T(8,128)(2,1)S(1)}, bf16[2,432,384]{2,1,0:T(8,128)(2,1)}, u32[]{:S(2)}, u32[]{:S(2)}) collective-permute-start(bf16[2,432,384]{2,1,0:T(8,128)(2,1)S(1)} %slice.233), channel_id=1, source_target_pairs={{0,4},{4,0},{8,12},{12,8},{16,20},{20,16},{24,28},{28,24},{1,5},{5... | collective-permute-start | bytes 1990664 | tf_op jit(solution)/shard_map/ppermute | solution.py:60
  117.9 18.3 %collective-permute-start.20 = (bf16[4,432,384]{2,1,0:T(8,128)(2,1)S(1)}, bf16[4,432,384]{2,1,0:T(8,128)(2,1)}, u32[]{:S(2)}, u32[]{:S(2)}) collective-permute-start(bf16[4,432,384]{2,1,0:T(8,128)(2,1)S(1)} %pad_maximum_fusion.1.refs_0_), channel_id=1, source_target_pairs={{0,1},{1,0},{2,3},{3,2},{4,5},{5,4},{6,7},{7,6},{8,9},{9,8},{10,11... | collective-permute-start | bytes 3981320 | tf_op jit(solution)/shard_map/ppermute | solution.py:60
  117.9 20.4 %collective-permute-start.21 = (bf16[4,432,384]{2,1,0:T(8,128)(2,1)}, bf16[4,432,384]{2,1,0:T(8,128)(2,1)}, u32[]{:S(2)}, u32[]{:S(2)}) collective-permute-start(bf16[4,432,384]{2,1,0:T(8,128)(2,1)} %collective-permute-done.16.refs_8_.refs_1_), channel_id=1, source_target_pairs={{0,1},{1,0},{2,3},{3,2},{4,5},{5,4},{6,7},{7,6},{8,9},{9,8},{10,11... | collective-permute-start | bytes 3981320 | tf_op jit(solution)/shard_map/ppermute | solution.py:60
  118.4 19.9 %collective-permute-start.22 = (bf16[4,432,384]{2,1,0:T(8,128)(2,1)}, bf16[4,432,384]{2,1,0:T(8,128)(2,1)}, u32[]{:S(2)}, u32[]{:S(2)}) collective-permute-start(bf16[4,432,384]{2,1,0:T(8,128)(2,1)} %collective-permute-done.17.refs_9_.refs_2_), channel_id=1, source_target_pairs={{0,1},{1,0},{2,3},{3,2},{4,5},{5,4},{6,7},{7,6},{8,9},{9,8},{10,11... | collective-permute-start | bytes 3981320 | tf_op jit(solution)/shard_map/ppermute | solution.py:60
  118.4 17.1 %copy-start.47 = (s32[23]{0:T(128)S(1)}, s32[23]{0:T(128)}, u32[]{:S(2)}) copy-start(s32[23]{0:T(128)} %stack.146.refs_0_.meta) | copy-start | bytes 280
  134.8 2.7 collective-permute-start.23
  135.4 2.8 collective-permute-start.24
  135.5 44.2 %copy-start.54 = (s32[23]{0:T(128)}, s32[23]{0:T(128)S(1)}, u32[]{:S(2)}) copy-start(s32[23]{0:T(128)S(1)} %constant_dynamic-update-slice_fusion.meta) | copy-start | bytes 280
  197.6 28.9 %collective-permute-start.25 = (bf16[2,2,4,432,384]{4,3,2,1,0:T(8,128)(2,1)}, bf16[2,2,4,432,384]{4,3,2,1,0:T(8,128)(2,1)}, u32[]{:S(2)}, u32[]{:S(2)}) collective-permute-start(bf16[2,2,4,432,384]{4,3,2,1,0:T(8,128)(2,1)} %get-tuple-element.161.refs_12_), channel_id=1, source_target_pairs={{0,1},{1,0},{2,3},{3,2},{4,5},{5,4},{6,7},{7,6},{8,9},{9,8},{10,11... | collective-permute-start | bytes 15925256 | tf_op jit(solution)/shard_map/ppermute | solution.py:60
  245.0 37.4 %collective-permute-start.26 = (bf16[2,2,432,384]{3,2,1,0:T(8,128)(2,1)}, bf16[2,2,432,384]{3,2,1,0:T(8,128)(2,1)S(1)}, u32[]{:S(2)}, u32[]{:S(2)}) collective-permute-start(bf16[2,2,432,384]{3,2,1,0:T(8,128)(2,1)} %get-tuple-element.169.refs_15_), channel_id=1, source_target_pairs={{0,4},{4,0},{8,12},{12,8},{16,20},{20,16},{24,28},{28,24},{1,5},{5... | collective-permute-start | bytes 3981320 | tf_op jit(solution)/shard_map/ppermute | solution.py:60
  248.0 34.4 %collective-permute-start.27 = (bf16[2,2,432,384]{3,2,1,0:T(8,128)(2,1)}, bf16[2,2,432,384]{3,2,1,0:T(8,128)(2,1)S(1)}, u32[]{:S(2)}, u32[]{:S(2)}) collective-permute-start(bf16[2,2,432,384]{3,2,1,0:T(8,128)(2,1)} %get-tuple-element.170.refs_16_), channel_id=1, source_target_pairs={{0,2},{1,3},{2,0},{3,1},{4,6},{5,7},{6,4},{7,5},{8,10},{9,11},{10,... | collective-permute-start | bytes 3981320 | tf_op jit(solution)/shard_map/ppermute | solution.py:60
  286.2 22.6 %collective-permute-start.28 = (bf16[2,432,384]{2,1,0:T(8,128)(2,1)}, bf16[2,432,384]{2,1,0:T(8,128)(2,1)}, u32[]{:S(2)}, u32[]{:S(2)}) collective-permute-start(bf16[2,432,384]{2,1,0:T(8,128)(2,1)} %fusion.8.refs_10_), channel_id=1, source_target_pairs={{0,4},{4,0},{8,12},{12,8},{16,20},{20,16},{24,28},{28,24},{1,5},{5... | collective-permute-start | bytes 1990664 | tf_op jit(solution)/shard_map/ppermute | solution.py:60
  288.2 20.6 %collective-permute-start.29 = (bf16[2,432,384]{2,1,0:T(8,128)(2,1)S(1)}, bf16[2,432,384]{2,1,0:T(8,128)(2,1)S(1)}, u32[]{:S(2)}, u32[]{:S(2)}) collective-permute-start(bf16[2,432,384]{2,1,0:T(8,128)(2,1)S(1)} %fusion.6.refs_11_), channel_id=1, source_target_pairs={{0,2},{1,3},{2,0},{3,1},{4,6},{5,7},{6,4},{7,5},{8,10},{9,11},{10,... | collective-permute-start | bytes 1990664 | tf_op jit(solution)/shard_map/ppermute | solution.py:60
  308.8 25.6 %collective-permute-start.31 = (bf16[2,2,4,48,1152]{4,3,2,1,0:T(8,128)(2,1)}, bf16[2,2,4,48,1152]{4,3,2,1,0:T(8,128)(2,1)}, u32[]{:S(2)}, u32[]{:S(2)}) collective-permute-start(bf16[2,2,4,48,1152]{4,3,2,1,0:T(8,128)(2,1)} %get-tuple-element.185), channel_id=1, source_target_pairs={{0,1},{1,0},{2,3},{3,2},{4,5},{5,4},{6,7},{7,6},{8,9},{9,8},{10,11... | collective-permute-start | bytes 5308424 | tf_op jit(solution)/shard_map/ppermute | solution.py:60
  313.1 21.3 %collective-permute-start.30 = (bf16[2,432,384]{2,1,0:T(8,128)(2,1)S(1)}, bf16[2,432,384]{2,1,0:T(8,128)(2,1)S(1)}, u32[]{:S(2)}, u32[]{:S(2)}) collective-permute-start(bf16[2,432,384]{2,1,0:T(8,128)(2,1)S(1)} %pad_maximum_fusion.3.refs_5_), channel_id=1, source_target_pairs={{0,8},{4,12},{8,0},{12,4},{16,24},{20,28},{24,16},{28,20},{1,9},{5... | collective-permute-start | bytes 1990664 | tf_op jit(solution)/shard_map/ppermute | solution.py:60
  314.0 14.5 %copy-start.44 = (f32[8,768]{1,0:T(8,128)S(1)}, f32[8,768]{1,0:T(8,128)}, u32[]{:S(2)}) copy-start(f32[8,768]{1,0:T(8,128)} %get-tuple-element.186) | copy-start | bytes 73732
  328.0 27.1 %collective-permute-start.33 = (bf16[2,1024,768]{2,1,0:T(8,128)(2,1)}, bf16[2,1024,768]{2,1,0:T(8,128)(2,1)}, u32[]{:S(2)}, u32[]{:S(2)}) collective-permute-start(bf16[2,1024,768]{2,1,0:T(8,128)(2,1)} %get-tuple-element.188), channel_id=1, source_target_pairs={{0,1},{1,0},{2,3},{3,2},{4,5},{5,4},{6,7},{7,6},{8,9},{9,8},{10,11... | collective-permute-start | bytes 9437192 | tf_op jit(solution)/shard_map/ppermute | solution.py:60
  330.2 4.2 collective-permute-start.32
  334.4 20.7 %collective-permute-start.36 = (f32[12,768]{1,0:T(8,128)S(1)}, f32[12,768]{1,0:T(8,128)S(1)}, u32[]{:S(2)}, u32[]{:S(2)}) collective-permute-start(f32[12,768]{1,0:T(8,128)S(1)} %fusion.36), channel_id=1, source_target_pairs={{0,1},{1,0},{2,3},{3,2},{4,5},{5,4},{6,7},{7,6},{8,9},{9,8},{10,11... | collective-permute-start | bytes 110600 | tf_op jit(solution)/shard_map/ppermute | solution.py:60
  338.4 7.2 %copy-start.10 = (bf16[2,2,48,1152]{3,2,1,0:T(8,128)(2,1)}, bf16[2,2,48,1152]{3,2,1,0:T(8,128)(2,1)S(1)}, u32[]{:S(2)}) copy-start(bf16[2,2,48,1152]{3,2,1,0:T(8,128)(2,1)S(1)} %pad_maximum_fusion.7.refs_7_) | copy-start | bytes 1327108
  338.4 16.7 %collective-permute-start.34 = (bf16[2,2,48,1152]{3,2,1,0:T(8,128)(2,1)S(1)}, bf16[2,2,48,1152]{3,2,1,0:T(8,128)(2,1)}, u32[]{:S(2)}, u32[]{:S(2)}) collective-permute-start(bf16[2,2,48,1152]{3,2,1,0:T(8,128)(2,1)S(1)} %pad_maximum_fusion.7.refs_7_), channel_id=1, source_target_pairs={{0,4},{4,0},{8,12},{12,8},{16,20},{20,16},{24,28},{28,24},{1,5},{5... | collective-permute-start | bytes 1327112 | tf_op jit(solution)/shard_map/ppermute | solution.py:60
  340.6 14.6 %collective-permute-start.35 = (bf16[2,2,48,1152]{3,2,1,0:T(8,128)(2,1)}, bf16[2,2,48,1152]{3,2,1,0:T(8,128)(2,1)}, u32[]{:S(2)}, u32[]{:S(2)}) collective-permute-start(bf16[2,2,48,1152]{3,2,1,0:T(8,128)(2,1)} %pad_maximum_fusion.8.refs_8_), channel_id=1, source_target_pairs={{0,2},{1,3},{2,0},{3,1},{4,6},{5,7},{6,4},{7,5},{8,10},{9,11},{10,... | collective-permute-start | bytes 1327112 | tf_op jit(solution)/shard_map/ppermute | solution.py:60
  342.6 21.1 %collective-permute-start.39 = (bf16[432,384]{1,0:T(8,128)(2,1)}, bf16[432,384]{1,0:T(8,128)(2,1)}, u32[]{:S(2)}, u32[]{:S(2)}) collective-permute-start(bf16[432,384]{1,0:T(8,128)(2,1)} %fusion.20), channel_id=1, source_target_pairs={{0,16},{4,20},{8,24},{12,28},{16,0},{20,4},{24,8},{28,12},{1,17},{... | collective-permute-start | bytes 995336 | tf_op jit(solution)/shard_map/ppermute | solution.py:60
  355.2 8.4 %collective-permute-start.40 = (f32[12,768]{1,0:T(8,128)S(1)}, f32[12,768]{1,0:T(8,128)S(1)}, u32[]{:S(2)}, u32[]{:S(2)}) collective-permute-start(f32[12,768]{1,0:T(8,128)S(1)} %add.427), channel_id=1, source_target_pairs={{0,2},{1,3},{2,0},{3,1},{4,6},{5,7},{6,4},{7,5},{8,10},{9,11},{10,... | collective-permute-start | bytes 110600 | tf_op jit(solution)/shard_map/ppermute | solution.py:60
  358.9 6.0 %collective-permute-start.38 = (bf16[2,48,1152]{2,1,0:T(8,128)(2,1)S(1)}, bf16[2,48,1152]{2,1,0:T(8,128)(2,1)S(1)}, u32[]{:S(2)}, u32[]{:S(2)}) collective-permute-start(bf16[2,48,1152]{2,1,0:T(8,128)(2,1)S(1)} %get-tuple-element.239), channel_id=1, source_target_pairs={{0,2},{1,3},{2,0},{3,1},{4,6},{5,7},{6,4},{7,5},{8,10},{9,11},{10,... | collective-permute-start | bytes 663560 | tf_op jit(solution)/shard_map/ppermute | solution.py:60
  359.7 5.9 %collective-permute-start.37 = (bf16[2,48,1152]{2,1,0:T(8,128)(2,1)S(1)}, bf16[2,48,1152]{2,1,0:T(8,128)(2,1)S(1)}, u32[]{:S(2)}, u32[]{:S(2)}) collective-permute-start(bf16[2,48,1152]{2,1,0:T(8,128)(2,1)S(1)} %get-tuple-element.240), channel_id=1, source_target_pairs={{0,4},{4,0},{8,12},{12,8},{16,20},{20,16},{24,28},{28,24},{1,5},{5... | collective-permute-start | bytes 663560 | tf_op jit(solution)/shard_map/ppermute | solution.py:60
  368.7 9.1 %collective-permute-start.43 = (f32[216,384]{1,0:T(8,128)S(1)}, f32[216,384]{1,0:T(8,128)S(1)}, u32[]{:S(2)}, u32[]{:S(2)}) collective-permute-start(f32[216,384]{1,0:T(8,128)S(1)} %dynamic-slice_bitcast_fusion), channel_id=1, source_target_pairs={{0,1},{1,0},{2,3},{3,2},{4,5},{5,4},{6,7},{7,6},{8,9},{9,8},{10,11... | collective-permute-start | bytes 995336 | tf_op jit(solution)/shard_map/ppermute | solution.py:60
  368.8 8.9 %collective-permute-start.41 = (bf16[2,48,1152]{2,1,0:T(8,128)(2,1)S(1)}, bf16[2,48,1152]{2,1,0:T(8,128)(2,1)S(1)}, u32[]{:S(2)}, u32[]{:S(2)}) collective-permute-start(bf16[2,48,1152]{2,1,0:T(8,128)(2,1)S(1)} %pad_maximum_fusion.12), channel_id=1, source_target_pairs={{0,8},{4,12},{8,0},{12,4},{16,24},{20,28},{24,16},{28,20},{1,9},{5... | collective-permute-start | bytes 663560 | tf_op jit(solution)/shard_map/ppermute | solution.py:60
  369.9 7.9 %collective-permute-start.42 = (f32[12,768]{1,0:T(8,128)S(1)}, f32[12,768]{1,0:T(8,128)S(1)}, u32[]{:S(2)}, u32[]{:S(2)}) collective-permute-start(f32[12,768]{1,0:T(8,128)S(1)} %add.434), channel_id=1, source_target_pairs={{0,8},{4,12},{8,0},{12,4},{16,24},{20,28},{24,16},{28,20},{1,9},{5... | collective-permute-start | bytes 110600 | tf_op jit(solution)/shard_map/ppermute | solution.py:60
  370.9 17.1 %copy-start.14 = (f32[2,48,1152]{2,1,0:T(8,128)S(1)}, f32[2,48,1152]{2,1,0:T(8,128)}, u32[]{:S(2)}) copy-start(f32[2,48,1152]{2,1,0:T(8,128)} %copy-done.13) | copy-start | bytes 1327108
  370.9 36.5 %collective-permute-start.49 = (bf16[1024,768]{1,0:T(8,128)(2,1)}, bf16[1024,768]{1,0:T(8,128)(2,1)}, u32[]{:S(2)}, u32[]{:S(2)}) collective-permute-start(bf16[1024,768]{1,0:T(8,128)(2,1)} %fusion), channel_id=1, source_target_pairs={{0,2},{1,3},{2,0},{3,1},{4,6},{5,7},{6,4},{7,5},{8,10},{9,11},{10,... | collective-permute-start | bytes 4718600 | tf_op jit(solution)/shard_map/ppermute | solution.py:60
  377.8 8.4 %collective-permute-start.45 = (f32[12,768]{1,0:T(8,128)S(1)}, f32[12,768]{1,0:T(8,128)S(1)}, u32[]{:S(2)}, u32[]{:S(2)}) collective-permute-start(f32[12,768]{1,0:T(8,128)S(1)} %add.438), channel_id=1, source_target_pairs={{0,16},{4,20},{8,24},{12,28},{16,0},{20,4},{24,8},{28,12},{1,17},{... | collective-permute-start | bytes 110600 | tf_op jit(solution)/shard_map/ppermute | solution.py:60
  378.6 9.5 %collective-permute-start.44 = (bf16[48,1152]{1,0:T(8,128)(2,1)S(1)}, bf16[48,1152]{1,0:T(8,128)(2,1)S(1)}, u32[]{:S(2)}, u32[]{:S(2)}) collective-permute-start(bf16[48,1152]{1,0:T(8,128)(2,1)S(1)} %fusion.27), channel_id=1, source_target_pairs={{0,16},{4,20},{8,24},{12,28},{16,0},{20,4},{24,8},{28,12},{1,17},{... | collective-permute-start | bytes 331784 | tf_op jit(solution)/shard_map/ppermute | solution.py:60
  380.8 26.6 %copy-start.1 = (f32[1,1024,768]{2,1,0:T(8,128)S(1)}, f32[1,1024,768]{2,1,0:T(8,128)}, u32[]{:S(2)}) copy-start(f32[1,1024,768]{2,1,0:T(8,128)} %token_grad.3) | copy-start | bytes 9437188
  389.6 14.1 %collective-permute-start.52 = (f32[24,1152]{1,0:T(8,128)S(1)}, f32[24,1152]{1,0:T(8,128)}, u32[]{:S(2)}, u32[]{:S(2)}) collective-permute-start(f32[24,1152]{1,0:T(8,128)S(1)} %dynamic-slice_bitcast_fusion.2), channel_id=1, source_target_pairs={{0,1},{1,0},{2,3},{3,2},{4,5},{5,4},{6,7},{7,6},{8,9},{9,8},{10,11... | collective-permute-start | bytes 331784 | tf_op jit(solution)/shard_map/ppermute | solution.py:60
  393.1 1.5 collective-permute-start.46
  395.2 3.7 collective-permute-start.47
  399.4 3.7 collective-permute-start.48
  411.4 4.4 %collective-permute-start.50 = (f32[1,1]{1,0:T(1,128)}, f32[1,1]{1,0:T(1,128)}, u32[]{:S(2)}, u32[]{:S(2)}) collective-permute-start(f32[1,1]{1,0:T(1,128)} %add.447), channel_id=1, source_target_pairs={{0,16},{4,20},{8,24},{12,28},{16,0},{20,4},{24,8},{28,12},{1,17},{... | collective-permute-start | bytes 20 | tf_op jit(solution)/shard_map/ppermute | solution.py:60
  416.5 3.6 collective-permute-start.51
  (44 other events, 110.4 us)

commit v2 on v1

--- a/solution.py
+++ b/solution.py
@@ -628,16 +628,12 @@
 
 
 def feed_grad_kernel(added, meta, h1_ref, du_ref, gl_ref, dz_ref, ol_ref, da_ref, *refs):
-    got_ref = refs[0] if added else None
-
-    def turned(ref, index):
-        if added:
-            return ref[...]
-        refs[index][...] = ref[...].T
-        return refs[index][...]
-
     scr = refs[-1]
     step = pl.program_id(0)
+    if added:
+        scr, got_ref, sem = refs[-3:]
+        copy = pltpu.make_async_copy(refs[0], got_ref, sem)
+        pl.when(step == 0)(copy.start)
     half = dz_ref.shape[1]
     width = 2 * half
     we_rows = 4 * SLAB
@@ -679,20 +675,22 @@
 
     @pl.when(step == 0)
     def _():
-        scr[:, :half] = dot(turned(ol_ref, 3), da_ref[...])
+        scr[:, :half] = dot_tn(ol_ref[...], da_ref[...])
+        if added:
+            copy.wait()
         put_all(we_rows, slice(0, half))
 
     for u in range(2):
 
         @pl.when(step == u)
         def _(u=u):
-            scr[...] = dot(turned(h1_ref, 1), du_ref[...])
+            scr[...] = dot_tn(h1_ref[...], du_ref[...])
             for k in range(width // half):
                 put_all((2 * u + k) * SLAB, slice(k * half, (k + 1) * half))
 
     @pl.when(step >= 2)
     def _():
-        scr[:, :half] = dot(turned(gl_ref, 2), dz_ref[...])
+        scr[:, :half] = dot_tn(gl_ref[...], dz_ref[...])
         z = jnp.bitwise_xor(meta[20], step - 2)
         for x in range(2):
             for y in range(2):
@@ -702,7 +700,7 @@
 
 
 def feed_grad(meta, h1, du, gl, dz, ol, da, got):
-    tokens, width = du.shape[0], dz.shape[1]
+    tokens, width = h1.shape
     half = width // 2
     wide = lambda index: pl.BlockSpec((tokens, width), index)
     added = got is not None
@@ -712,18 +710,6 @@
         outs = [((4,), F32), ((2,), F32), ((2,), F32), ((2, 2), BF16), ((2, 2), BF16)]
     else:
         outs = [(every, BF16)]
-    left = (width, tokens) if added else (tokens, width)
-    low_full = pl.BlockSpec(left, lambda u, m: (0, 0))
-    tall = lambda index: pl.BlockSpec((width, tokens), index)
-    step_of = lambda u: jnp.clip(u - 2, 0, 3)
-    if added:
-        gl_spec = tall(lambda u, m: (step_of(u), 0))
-        turned_specs, turned_shapes = [], []
-    else:
-        gl_spec = wide(lambda u, m: (0, step_of(u)))
-        once = tall(lambda u, m: (0, 0))
-        turned_specs = [once, tall(lambda u, m: (step_of(u), 0)), once]
-        turned_shapes = [(width, tokens), (4 * width, tokens), (width, tokens)]
     slab_spec = lambda lead: pl.BlockSpec(lead + slab, lambda u, m: (0,) * (len(lead) + 2))
     return pl.pallas_call(
         functools.partial(feed_grad_kernel, added),
@@ -731,19 +717,19 @@
             num_scalar_prefetch=1,
             grid=(6,),
             in_specs=[
-                low_full,
+                wide(lambda u, m: (0, 0)),
                 wide(lambda u, m: (0, 2 * m[0] + jnp.minimum(u, 1))),
-                gl_spec,
+                wide(lambda u, m: (0, jnp.clip(u - 2, 0, 3))),
                 pl.BlockSpec((tokens, half), lambda u, m: (0, m[0])),
-                low_full,
+                wide(lambda u, m: (0, 0)),
                 pl.BlockSpec((tokens, half), lambda u, m: (0, m[0])),
             ]
-            + [slab_spec(every)] * added,
-            out_specs=[slab_spec(lead) for lead, _ in outs] + turned_specs,
-            scratch_shapes=[pltpu.VMEM((width, width), F32)],
+            + [pl.BlockSpec(memory_space=pl.ANY)] * added,
+            out_specs=[slab_spec(lead) for lead, _ in outs],
+            scratch_shapes=[pltpu.VMEM((width, width), F32)]
+            + ([pltpu.VMEM(every + slab, BF16), pltpu.SemaphoreType.DMA] if added else []),
         ),
-        out_shape=[jax.ShapeDtypeStruct(lead + slab, dtype) for lead, dtype in outs]
-        + [jax.ShapeDtypeStruct(shape, BF16) for shape in turned_shapes],
+        out_shape=[jax.ShapeDtypeStruct(lead + slab, dtype) for lead, dtype in outs],
         compiler_params=params(1),
         cost_estimate=cost(9 * tokens * width * width, 16 * tokens * width),
         name="feed_grad",
@@ -1146,8 +1132,7 @@
     )
     layer_output = by_rows(layer_output)
     grad_args = (h1, du, gl, dz, flat(attended), da)
-    rest_theirs, h1, gl, turned = feed_grad(meta_other, *grad_args, None)
-    grad_args = (h1, du, gl, dz, turned, da)
+    rest_theirs = feed_grad(meta_other, *grad_args, None)[0]
     back_args = (
         meta, plan, q, k, v, by_rows(d_att), attended, lse, shares, teacher, segq, segk
     )

time: 433 us -> 432 us (level)
  Pallas kernels: 250 us -> 236 us
  starting transfers between devices: 54.1 us -> 64.7 us
  waiting for transfers between devices: 48.2 us -> 53 us
    ppermute x53, starting transfers between devices: 54.1 us -> 64.7 us  [swap(): lax.ppermute(x, axis, [(i, i ^ bit) for i in range(lax.axis_size(axis))])]
    pallas_call x2, Pallas kernels: 61.1 us -> 52.5 us  [attend_back(): pl.pallas_call(skipping(functools.partial(attend_back_kernel, blocks, sta...]
    ppermute x53, waiting for transfers between devices: 48.2 us -> 53 us  [swap(): lax.ppermute(x, axis, [(i, i ^ bit) for i in range(lax.axis_size(axis))])]
  transfers between devices with their start and end apart: 53 -> 53, of which waited for: 19 -> 21; matrix products, arithmetic and copies ran while one was open for 9% -> 9% of each run, Pallas kernels for 40% -> 37%
where the time goes in v2:
time: 432 us; the launch traced here: 429 us
  Pallas kernels  236 us (55%)
  starting transfers between devices  64.7 us (15%)
  waiting for transfers between devices  53 us (12%)
  other arithmetic  44.4 us (10%)
  local copies, waits for them, and re-layouts  22.6 us (5%)
  between operations  8.26 us (2%)
    ppermute x53, starting transfers between devices, swap(): lax.ppermute(x, axis, [(i, i ^ bit) for i in range(lax.axis_size(axis))])  64.7 us
    ppermute x53, waiting for transfers between devices, swap(): lax.ppermute(x, axis, [(i, i ^ bit) for i in range(lax.axis_size(axis))])  53 us
    pallas_call x2, Pallas kernels, attend_back(): pl.pallas_call(skipping(functools.partial(attend_back_kernel, blocks, sta...  52.5 us
    pallas_call x1, Pallas kernels, feed(): pl.pallas_call(feed_kernel, grid_spec=pltpu.PrefetchScalarGridSpec(num_sc...  40.9 us
    pallas_call x2, Pallas kernels, feed_grad(): pl.pallas_call(functools.partial(feed_grad_kernel, added), grid_spec=pltp...  35.1 us
    pallas_call x2, Pallas kernels, attend(): pl.pallas_call(skipping(functools.partial(attend_kernel, blocks, start),...  26.3 us
    pallas_call x2, Pallas kernels, token_grad(): pl.pallas_call(skipping(functools.partial(token_grad_kernel, steps, sent,...  23.9 us
    pallas_call x1, Pallas kernels, project(): pl.pallas_call(skipping(functools.partial(project_kernel, spans, steps),...  20.3 us
  transfers between devices with their start and end apart: 53, of which 21 were waited for; matrix products, arithmetic and copies ran while one was open for 9% of the time, Pallas kernels for 37%

profile of v2, /device:TPU:0, one launch (start us, length us, event | category | flops | bytes accessed | tf_op | source)
XLA Modules:
  0.0 428.6 jit_solution(14833625307345532714)
XLA Ops:
  4.4 1.2 fusion.46
  6.3 3.7 collective-permute-start.1
  11.0 1.5 collective-permute-start.8
  13.3 3.3 collective-permute-done.1
  17.7 6.7 %collective-permute-done.2 = bf16[2,48,1280]{2,1,0:T(8,128)(2,1)S(1)} collective-permute-done((bf16[2,48,1280]{2,1,0:T(8,128)(2,1)S(1)}, bf16[2,48,1280]{2,1,0:T(8,128)(2,1)S(1)}, u32[]{:S(2)}, u32[]{:S(2)}) %collective-permute-start.2) | collective-permute-done | bytes 245792 | tf_op jit(solution)/shard_map/ppermute | solution.py:60
  25.2 1.4 collective-permute-start.6
  26.6 1.5 collective-permute-start.5
  28.5 2.7 collective-permute-start.7
  33.4 8.6 %share.2.refs_5_.refs_8_ = f32[2,6,256,128]{3,2,1,0:T(8,128)} custom-call(bf16[4,12,256,1024]{3,2,1,0:T(8,128)(2,1)} %refs_9_.3, s32[4,256,128]{2,1,0:T(8,128)} %broadcast_in_dim.62.refs_1_.refs_4_.refs_10_, s32[4,8,1024]{2,1,0:T(8,128)} %broadcast_in_dim.63.refs_2_, bf16[4,48,1280]{2,1,0:T(8,128)(2,1)} %pad_maximum_fusion.6.refs_3_.refs_8_), custom_call_target="tpu_custom_call" | custom-call | flops 25165824 | bytes 12582912 | tf_op jit(solution)/shard_map/share/pallas_call | solution.py:228
  42.0 3.4 collective-permute-done.7
  45.5 1.5 pad_maximum_fusion
  52.2 8.2 %share.3.refs_15_.refs_8_ = f32[2,6,256,128]{3,2,1,0:T(8,128)} custom-call(bf16[4,12,256,1024]{3,2,1,0:T(8,128)(2,1)} %refs_9_.3, s32[4,256,128]{2,1,0:T(8,128)} %broadcast_in_dim.62.refs_1_.refs_4_.refs_10_, s32[4,8,1024]{2,1,0:T(8,128)} %broadcast_in_dim.63.refs_2_, bf16[4,48,1280]{2,1,0:T(8,128)(2,1)} %copy-done.8, bf16[4,48,1280]{2,1,0:T(8,128)(2,1)} %copy-done.9, ...), custom_call_target="tpu_custom_call" | custom-call | flops 25165824 | bytes 12582912 | tf_op jit(solution)/shard_map/share/pallas_call | solution.py:228
  60.4 1.6 collective-permute-done.9.refs_11_
  64.4 3.5 collective-permute-done.13
  67.8 3.0 collective-permute-done.14
  71.6 1.3 pad_maximum_fusion.1.refs_0_
  72.9 1.6 collective-permute-start.17
  75.0 20.3 %project.1 = (bf16[1024,768]{1,0:T(8,128)(2,1)}, bf16[4,1024,768]{2,1,0:T(8,128)(2,1)}, bf16[4,1024,768]{2,1,0:T(8,128)(2,1)}, bf16[768,2304]{1,0:T(8,128)(2,1)}) custom-call(s32[23]{0:T(128)} %stack.146.refs_0_.meta, s32[4,4]{1,0:T(4,128)} %copy-done.42, bf16[1024,768]{1,0:T(8,128)(2,1)} %bitcast.255, bf16[1024,768]{1,0:T(8,128)(2,1)} %bitcast.44.refs_3_.refs_2_, ...), custom_call_target="tpu_custom_call" | custom-call | flops 10871635968 | bytes 12582912 | tf_op jit(solution)/shard_map/project/pallas_call | solution.py:179
  96.0 12.0 %attend.2 = (bf16[4,256,768]{2,1,0:T(8,128)(2,1)}, f32[4,6,256,128]{3,2,1,0:T(8,128)}) custom-call(s32[4,5]{1,0:T(4,128)} %pad_add_fusion.refs_0_.refs_1_, bf16[4,256,768]{2,1,0:T(8,128)(2,1)} %bitcast.258, bf16[4,4,256,768]{3,2,1,0:T(8,128)(2,1)} %bitcast.244, bf16[4,4,256,768]{3,2,1,0:T(8,128)(2,1)} %bitcast.248, ...), custom_call_target="tpu_custom_call" | custom-call | flops 6442450944 | bytes 3145728 | tf_op jit(solution)/shard_map/attend/pallas_call | solution.py:337
  110.4 4.6 %collective-permute-start.19 = (bf16[2,432,384]{2,1,0:T(8,128)(2,1)S(1)}, bf16[2,432,384]{2,1,0:T(8,128)(2,1)S(1)}, u32[]{:S(2)}, u32[]{:S(2)}) collective-permute-start(bf16[2,432,384]{2,1,0:T(8,128)(2,1)S(1)} %slice.234), channel_id=1, source_target_pairs={{0,2},{1,3},{2,0},{3,1},{4,6},{5,7},{6,4},{7,5},{8,10},{9,11},{10,... | collective-permute-start | bytes 1990664 | tf_op jit(solution)/shard_map/ppermute | solution.py:60
  116.6 14.3 %attend.3 = (bf16[4,256,768]{2,1,0:T(8,128)(2,1)}, f32[4,6,256,128]{3,2,1,0:T(8,128)}) custom-call(s32[4,5]{1,0:T(4,128)} %pad_add_fusion.refs_0_.refs_1_, bf16[4,256,768]{2,1,0:T(8,128)(2,1)} %bitcast.259, bf16[4,4,256,768]{3,2,1,0:T(8,128)(2,1)} %bitcast.245, bf16[4,4,256,768]{3,2,1,0:T(8,128)(2,1)} %bitcast.249, ...), custom_call_target="tpu_custom_call", output_to_operand_aliasing={{0}: (6, {}), {1}: (7, {})} | custom-call | flops 6442450944 | bytes 3145728 | tf_op jit(solution)/shard_map/attend/pallas_call | solution.py:337
  130.9 1.8 collective-permute-done.18.refs_3_
  136.6 40.9 %feed.1 = (bf16[1024,768]{1,0:T(8,128)(2,1)}, f32[1024,768]{1,0:T(8,128)}, bf16[1024,768]{1,0:T(8,128)(2,1)}, bf16[1024,3072]{1,0:T(8,128)(2,1)}, bf16[1024,3072...) custom-call(s32[23]{0:T(128)} %stack.146.refs_0_.meta, ...), custom_call_target="tpu_custom_call" | custom-call | flops 21743271936 | bytes 28311552 | tf_op jit(solution)/shard_map/feed/pallas_call | solution.py:590
  177.5 15.8 %feed_grad.2.refs_12_ = bf16[2,2,4,432,384]{4,3,2,1,0:T(8,128)(2,1)} custom-call(s32[23]{0:T(128)} %copy-done.51, bf16[1024,768]{1,0:T(8,128)(2,1)} %get-tuple-element.152.h1_ref, bf16[1024,3072]{1,0:T(8,128)(2,1)} %get-tuple-element.153.du_ref, bf16[1024,3072]{1,0:T(8,128)(2,1)} %get-tuple-element.154.gl_ref, bf16[1024,768]{1,0:T(8,128)(2,1)} %get-tuple-element.155.dz_ref, ...), custom_call_target="tpu_custom_call" | custom-call | flops 5435817984 | bytes 12582912 | tf_op jit(solution)/shard_map/feed_grad/pallas_call | solution.py:714
  193.6 24.0 %attend_back.2 = (bf16[4,256,768]{2,1,0:T(8,128)(2,1)}, bf16[4,4,256,768]{3,2,1,0:T(8,128)(2,1)}, bf16[4,4,256,768]{3,2,1,0:T(8,128)(2,1)}) custom-call(s32[23]{0:T(128)} %stack.146.refs_0_.meta, s32[4,5]{1,0:T(4,128)} %pad_add_fusion.refs_0_.refs_1_, bf16[4,256,768]{2,1,0:T(8,128)(2,1)} %bitcast.260, bf16[4,4,256,768]{3,2,1,0:T(8,128)(2,1)} %bitcast.246, ...), custom_call_target="tpu_custom_call" | custom-call | flops 16106127360 | bytes 6291456 | tf_op jit(solution)/shard_map/attend_back/pallas_call | solution.py:441
  217.6 19.3 %feed_grad.3 = (f32[4,432,384]{2,1,0:T(8,128)}, f32[2,432,384]{2,1,0:T(8,128)}, f32[2,432,384]{2,1,0:T(8,128)}, bf16[2,2,432,384]{3,2,1,0:T(8,128)(2,1)}, bf16[2,2,432,384]{3,2,1,0:T(8,128)(2,1)}) custom-call(s32[23]{0:T(128)} %stack.146.refs_0_.meta, bf16[1024,768]{1,0:T(8,128)(2,1)} %get-tuple-element.152.h1_ref, ...), custom_call_target="tpu_custom_call" | custom-call | flops 5435817984 | bytes 12582912 | tf_op jit(solution)/shard_map/feed_grad/pallas_call | solution.py:714
  237.7 7.1 %collective-permute-start.27 = (bf16[2,2,432,384]{3,2,1,0:T(8,128)(2,1)}, bf16[2,2,432,384]{3,2,1,0:T(8,128)(2,1)S(1)}, u32[]{:S(2)}, u32[]{:S(2)}) collective-permute-start(bf16[2,2,432,384]{3,2,1,0:T(8,128)(2,1)} %get-tuple-element.162.refs_16_), channel_id=1, source_target_pairs={{0,2},{1,3},{2,0},{3,1},{4,6},{5,7},{6,4},{7,5},{8,10},{9,11},{10,... | collective-permute-start | bytes 3981320 | tf_op jit(solution)/shard_map/ppermute | solution.py:60
  244.8 28.5 %attend_back.3 = (bf16[4,256,768]{2,1,0:T(8,128)(2,1)}, bf16[4,4,256,768]{3,2,1,0:T(8,128)(2,1)}, bf16[4,4,256,768]{3,2,1,0:T(8,128)(2,1)}) custom-call(s32[23]{0:T(128)} %stack.146.refs_0_.meta, s32[4,5]{1,0:T(4,128)} %pad_add_fusion.refs_0_.refs_1_, bf16[4,256,768]{2,1,0:T(8,128)(2,1)} %bitcast.261, ...), custom_call_target="tpu_custom_call", output_to_operand_aliasing={{0}: (12, {}), {1}: (13, {}), {2}: (14, {})} | custom-call | flops 16106127360 | bytes 6291456 | tf_op jit(solution)/shard_map/attend_back/pallas_call | solution.py:441
  274.9 1.6 convert_element_type.137
  277.7 1.7 collective-permute-start.28
  279.7 1.3 copy-done.2
  281.0 2.2 collective-permute-start.29
  283.2 19.8 %joint_grad.1 = (f32[2,2,4,48,1152]{4,3,2,1,0:T(8,128)}, bf16[2,2,4,48,1152]{4,3,2,1,0:T(8,128)(2,1)}, f32[8,768]{1,0:T(8,128)}) custom-call(s32[23]{0:T(128)} %stack.146.refs_0_.meta, bf16[1024,768]{1,0:T(8,128)(2,1)} %bitcast.257, bf16[1024,768]{1,0:T(8,128)(2,1)} %bitcast.44.refs_3_.refs_2_, bf16[512,768]{1,0:T(8,128)(2,1)} %bitcast.46.refs_4_.refs_3_, ...), custom_call_target="tpu_custom_call" | custom-call | flops 10871635968 | bytes 25165824 | tf_op jit(solution)/shard_map/joint_grad/pallas_call | solution.py:857
  303.0 2.6 collective-permute-start.31
  305.6 2.7 fusion.4
  309.9 2.4 collective-permute-start.30
  312.3 14.4 %token_grad.2 = (bf16[2,1024,768]{2,1,0:T(8,128)(2,1)}, bf16[1,1024,768]{2,1,0:T(8,128)(2,1)}) custom-call(s32[23]{0:T(128)} %stack.146.refs_0_.meta, s32[4,4]{1,0:T(4,128)} %copy-done.42, bf16[4,1024,768]{2,1,0:T(8,128)(2,1)} %bitcast.234, bf16[4,1024,768]{2,1,0:T(8,128)(2,1)} %bitcast.237, bf16[768,2304]{1,0:T(8,128)(2,1)} %get-tuple-element.165.refs_4_, ...), custom_call_target="tpu_custom_call" | custom-call | flops 7247757312 | bytes 14155776 | tf_op jit(solution)/shard_map/token_grad/pallas_call | solution.py:786
  329.0 3.6 collective-permute-done.32
  333.5 3.0 fusion.44
  339.6 5.4 %collective-permute-start.39 = (bf16[432,384]{1,0:T(8,128)(2,1)}, bf16[432,384]{1,0:T(8,128)(2,1)}, u32[]{:S(2)}, u32[]{:S(2)}) collective-permute-start(bf16[432,384]{1,0:T(8,128)(2,1)} %fusion.20), channel_id=1, source_target_pairs={{0,16},{4,20},{8,24},{12,28},{16,0},{20,4},{24,8},{28,12},{1,17},{... | collective-permute-start | bytes 995336 | tf_op jit(solution)/shard_map/ppermute | solution.py:60
  345.0 9.6 %token_grad.3 = f32[1,1024,768]{2,1,0:T(8,128)} custom-call(s32[23]{0:T(128)} %stack.146.refs_0_.meta, s32[4,4]{1,0:T(4,128)} %copy-done.42, bf16[4,1024,768]{2,1,0:T(8,128)(2,1)} %bitcast.235, bf16[4,1024,768]{2,1,0:T(8,128)(2,1)} %bitcast.238, bf16[768,2304]{1,0:T(8,128)(2,1)} %get-tuple-element.165.refs_4_, bf16[1024,768]{1,0:T(8,128)(2,1)} %bitcast.243, ...), custom_call_target="tpu_custom_call" | custom-call | flops 2415919104 | bytes 4718592 | tf_op jit(solution)/shard_map/token_grad/pallas_call | solution.py:786
  359.4 3.2 fusion
  362.5 1.5 collective-permute-done.38
  365.1 1.8 multiply_reduce_fusion
  369.0 1.4 collective-permute-start.42
  371.3 5.9 %collective-permute-done.42 = f32[12,768]{1,0:T(8,128)S(1)} collective-permute-done((f32[12,768]{1,0:T(8,128)S(1)}, f32[12,768]{1,0:T(8,128)S(1)}, u32[]{:S(2)}, u32[]{:S(2)}) %collective-permute-start.42) | collective-permute-done | bytes 36896 | tf_op jit(solution)/shard_map/ppermute | solution.py:60
  378.0 2.2 collective-permute-start.44
  380.3 1.3 bitcast_select_fusion.1
  382.4 2.9 collective-permute-done.45
  386.0 1.5 collective-permute-done.44
  387.5 1.6 multiply_reduce_fusion.1
  390.5 1.4 multiply_reduce_fusion.2
  392.5 1.4 collective-permute-start.46
  394.5 1.7 collective-permute-start.47
  396.3 1.8 collective-permute-done.47
  398.7 1.4 collective-permute-start.48
  400.1 2.2 collective-permute-done.48
  402.9 1.6 bitcast_select_fusion.3
  404.5 2.5 collective-permute-done.49
  406.9 4.0 bitcast_add_fusion
  410.9 1.6 collective-permute-start.50
  412.5 2.8 collective-permute-done.50
  415.9 2.3 collective-permute-start.51
  418.1 1.3 collective-permute-done.51
  (302 shorter events, 57.6 us)
Async XLA Ops:
  2.9 3.4 collective-permute-start
  4.4 6.2 %copy-start.21 = (f32[96,768]{1,0:T(8,128)S(1)}, f32[96,768]{1,0:T(8,128)}, u32[]{:S(2)}) copy-start(f32[96,768]{1,0:T(8,128)} %param.29) | copy-start | bytes 884740
  6.3 10.3 %collective-permute-start.1 = (bf16[48,1280]{1,0:T(8,128)(2,1)S(1)}, bf16[48,1280]{1,0:T(8,128)(2,1)S(1)}, u32[]{:S(2)}, u32[]{:S(2)}) collective-permute-start(bf16[48,1280]{1,0:T(8,128)(2,1)S(1)} %maximum_select_fusion.1), channel_id=1, source_target_pairs={{0,16},{4,20},{8,24},{12,28},{16,0},{20,4},{24,8},{28,12},{1,17},{... | collective-permute-start | bytes 368648 | tf_op jit(solution)/shard_map/ppermute | solution.py:60
  10.8 6.7 %collective-permute-start.3 = (bf16[216,384]{1,0:T(8,128)(2,1)S(1)}, bf16[216,384]{1,0:T(8,128)(2,1)S(1)}, u32[]{:S(2)}, u32[]{:S(2)}) collective-permute-start(bf16[216,384]{1,0:T(8,128)(2,1)S(1)} %get-tuple-element.252), channel_id=1, source_target_pairs={{0,1},{1,0},{2,3},{3,2},{4,5},{5,4},{6,7},{7,6},{8,9},{9,8},{10,11... | collective-permute-start | bytes 497672 | tf_op jit(solution)/shard_map/ppermute | solution.py:60
  11.0 31.0 %collective-permute-start.8 = (bf16[2,256,768]{2,1,0:T(8,128)(2,1)}, bf16[2,256,768]{2,1,0:T(8,128)(2,1)}, u32[]{:S(2)}, u32[]{:S(2)}) collective-permute-start(bf16[2,256,768]{2,1,0:T(8,128)(2,1)} %get-tuple-element.124), channel_id=1, source_target_pairs={{0,2},{1,3},{2,0},{3,1},{4,6},{5,7},{6,4},{7,5},{8,10},{9,11},{10,... | collective-permute-start | bytes 2359304 | tf_op jit(solution)/shard_map/ppermute | solution.py:60
  12.5 12.7 %collective-permute-start.4 = (bf16[4,256,768]{2,1,0:T(8,128)(2,1)S(1)}, bf16[4,256,768]{2,1,0:T(8,128)(2,1)}, u32[]{:S(2)}, u32[]{:S(2)}) collective-permute-start(bf16[4,256,768]{2,1,0:T(8,128)(2,1)S(1)} %copy-done.11), channel_id=1, source_target_pairs={{0,1},{1,0},{2,3},{3,2},{4,5},{5,4},{6,7},{7,6},{8,9},{9,8},{10,11... | collective-permute-start | bytes 4718600 | tf_op jit(solution)/shard_map/ppermute | solution.py:60
  16.6 7.8 %collective-permute-start.2 = (bf16[2,48,1280]{2,1,0:T(8,128)(2,1)S(1)}, bf16[2,48,1280]{2,1,0:T(8,128)(2,1)S(1)}, u32[]{:S(2)}, u32[]{:S(2)}) collective-permute-start(bf16[2,48,1280]{2,1,0:T(8,128)(2,1)S(1)} %pad_maximum_fusion.11), channel_id=1, source_target_pairs={{0,8},{4,12},{8,0},{12,4},{16,24},{20,28},{24,16},{28,20},{1,9},{5... | collective-permute-start | bytes 737288 | tf_op jit(solution)/shard_map/ppermute | solution.py:60
  25.2 20.2 %collective-permute-start.6 = (bf16[4,48,1280]{2,1,0:T(8,128)(2,1)}, bf16[4,48,1280]{2,1,0:T(8,128)(2,1)S(1)}, u32[]{:S(2)}, u32[]{:S(2)}) collective-permute-start(bf16[4,48,1280]{2,1,0:T(8,128)(2,1)} %pad_maximum_fusion.6.refs_3_.refs_8_), channel_id=1, source_target_pairs={{0,4},{4,0},{8,12},{12,8},{16,20},{20,16},{24,28},{28,24},{1,5},{5... | collective-permute-start | bytes 1474568 | tf_op jit(solution)/shard_map/ppermute | solution.py:60
  26.6 18.8 %collective-permute-start.5 = (bf16[4,48,1280]{2,1,0:T(8,128)(2,1)}, bf16[4,48,1280]{2,1,0:T(8,128)(2,1)S(1)}, u32[]{:S(2)}, u32[]{:S(2)}) collective-permute-start(bf16[4,48,1280]{2,1,0:T(8,128)(2,1)} %pad_maximum_fusion.6.refs_3_.refs_8_), channel_id=1, source_target_pairs={{0,2},{1,3},{2,0},{3,1},{4,6},{5,7},{6,4},{7,5},{8,10},{9,11},{10,... | collective-permute-start | bytes 1474568 | tf_op jit(solution)/shard_map/ppermute | solution.py:60
  28.5 16.9 %collective-permute-start.7 = (bf16[432,384]{1,0:T(8,128)(2,1)S(1)}, bf16[432,384]{1,0:T(8,128)(2,1)S(1)}, u32[]{:S(2)}, u32[]{:S(2)}) collective-permute-start(bf16[432,384]{1,0:T(8,128)(2,1)S(1)} %pad_maximum_fusion.10), channel_id=1, source_target_pairs={{0,16},{4,20},{8,24},{12,28},{16,0},{20,4},{24,8},{28,12},{1,17},{... | collective-permute-start | bytes 995336 | tf_op jit(solution)/shard_map/ppermute | solution.py:60
  31.3 15.9 %copy-start.42 = (s32[4,4]{1,0:T(4,128)}, s32[4,4]{1,0:T(4,128)S(1)}, u32[]{:S(2)}) copy-start(s32[4,4]{1,0:T(4,128)S(1)} %get-tuple-element.228.refs_1_) | copy-start | bytes 196
  45.4 6.7 %copy-start.8 = (bf16[4,48,1280]{2,1,0:T(8,128)(2,1)}, bf16[4,48,1280]{2,1,0:T(8,128)(2,1)S(1)}, u32[]{:S(2)}) copy-start(bf16[4,48,1280]{2,1,0:T(8,128)(2,1)S(1)} %collective-permute-done.6.refs_3_.refs_10_) | copy-start | bytes 1474564
  47.0 15.0 %collective-permute-start.11 = (bf16[12,48,1280]{2,1,0:T(8,128)(2,1)S(1)}, bf16[12,48,1280]{2,1,0:T(8,128)(2,1)}, u32[]{:S(2)}, u32[]{:S(2)}) collective-permute-start(bf16[12,48,1280]{2,1,0:T(8,128)(2,1)S(1)} %pad_maximum_fusion), channel_id=1, source_target_pairs={{0,1},{1,0},{2,3},{3,2},{4,5},{5,4},{6,7},{7,6},{8,9},{9,8},{10,11... | collective-permute-start | bytes 4423688 | tf_op jit(solution)/shard_map/ppermute | solution.py:60
  48.2 13.8 %collective-permute-start.10 = (bf16[2,256,768]{2,1,0:T(8,128)(2,1)}, bf16[2,256,768]{2,1,0:T(8,128)(2,1)}, u32[]{:S(2)}, u32[]{:S(2)}) collective-permute-start(bf16[2,256,768]{2,1,0:T(8,128)(2,1)} %collective-permute-done.8), channel_id=1, source_target_pairs={{0,1},{1,0},{2,3},{3,2},{4,5},{5,4},{6,7},{7,6},{8,9},{9,8},{10,11... | collective-permute-start | bytes 2359304 | tf_op jit(solution)/shard_map/ppermute | solution.py:60
  48.7 13.3 %collective-permute-start.9 = (bf16[4,48,1280]{2,1,0:T(8,128)(2,1)S(1)}, bf16[4,48,1280]{2,1,0:T(8,128)(2,1)}, u32[]{:S(2)}, u32[]{:S(2)}) collective-permute-start(bf16[4,48,1280]{2,1,0:T(8,128)(2,1)S(1)} %collective-permute-done.5.refs_4_.refs_9_), channel_id=1, source_target_pairs={{0,4},{4,0},{8,12},{12,8},{16,20},{20,16},{24,28},{28,24},{1,5},{5... | collective-permute-start | bytes 1474568 | tf_op jit(solution)/shard_map/ppermute | solution.py:60
  51.0 16.9 %collective-permute-start.13 = (bf16[2,432,384]{2,1,0:T(8,128)(2,1)}, bf16[2,432,384]{2,1,0:T(8,128)(2,1)}, u32[]{:S(2)}, u32[]{:S(2)}) collective-permute-start(bf16[2,432,384]{2,1,0:T(8,128)(2,1)} %pad_maximum_fusion.2), channel_id=1, source_target_pairs={{0,8},{4,12},{8,0},{12,4},{16,24},{20,28},{24,16},{28,20},{1,9},{5... | collective-permute-start | bytes 1990664 | tf_op jit(solution)/shard_map/ppermute | solution.py:60
  51.7 19.2 %collective-permute-start.14 = (bf16[2,256,768]{2,1,0:T(8,128)(2,1)}, bf16[2,256,768]{2,1,0:T(8,128)(2,1)}, u32[]{:S(2)}, u32[]{:S(2)}) collective-permute-start(bf16[2,256,768]{2,1,0:T(8,128)(2,1)} %get-tuple-element.132), channel_id=1, source_target_pairs={{0,2},{1,3},{2,0},{3,1},{4,6},{5,7},{6,4},{7,5},{8,10},{9,11},{10,... | collective-permute-start | bytes 2359304 | tf_op jit(solution)/shard_map/ppermute | solution.py:60
  60.4 10.6 %copy-start.50 = (pred[8]{0:T(512)(128)(4,1)S(1)}, pred[8]{0:T(512)(128)(4,1)}, u32[]{:S(2)}) copy-start(pred[8]{0:T(512)(128)(4,1)} %constant.203.clone.1) | copy-start | bytes 28
  62.0 8.9 %collective-permute-start.12 = (bf16[4,48,1280]{2,1,0:T(8,128)(2,1)}, bf16[4,48,1280]{2,1,0:T(8,128)(2,1)S(1)}, u32[]{:S(2)}, u32[]{:S(2)}) collective-permute-start(bf16[4,48,1280]{2,1,0:T(8,128)(2,1)} %collective-permute-done.9.refs_11_), channel_id=1, source_target_pairs={{0,1},{1,0},{2,3},{3,2},{4,5},{5,4},{6,7},{7,6},{8,9},{9,8},{10,11... | collective-permute-start | bytes 1474568 | tf_op jit(solution)/shard_map/ppermute | solution.py:60
  70.9 4.1 collective-permute-start.15
  72.9 42.6 %copy-start.17 = (bf16[4,432,384]{2,1,0:T(8,128)(2,1)}, bf16[4,432,384]{2,1,0:T(8,128)(2,1)S(1)}, u32[]{:S(2)}) copy-start(bf16[4,432,384]{2,1,0:T(8,128)(2,1)S(1)} %pad_maximum_fusion.1.refs_0_) | copy-start | bytes 3981316
  72.9 35.1 %collective-permute-start.17 = (bf16[4,432,384]{2,1,0:T(8,128)(2,1)S(1)}, bf16[4,432,384]{2,1,0:T(8,128)(2,1)}, u32[]{:S(2)}, u32[]{:S(2)}) collective-permute-start(bf16[4,432,384]{2,1,0:T(8,128)(2,1)S(1)} %pad_maximum_fusion.1.refs_0_), channel_id=1, source_target_pairs={{0,4},{4,0},{8,12},{12,8},{16,20},{20,16},{24,28},{28,24},{1,5},{5... | collective-permute-start | bytes 3981320 | tf_op jit(solution)/shard_map/ppermute | solution.py:60
  74.5 33.6 %collective-permute-start.16 = (bf16[4,432,384]{2,1,0:T(8,128)(2,1)S(1)}, bf16[4,432,384]{2,1,0:T(8,128)(2,1)}, u32[]{:S(2)}, u32[]{:S(2)}) collective-permute-start(bf16[4,432,384]{2,1,0:T(8,128)(2,1)S(1)} %pad_maximum_fusion.1.refs_0_), channel_id=1, source_target_pairs={{0,2},{1,3},{2,0},{3,1},{4,6},{5,7},{6,4},{7,5},{8,10},{9,11},{10,... | collective-permute-start | bytes 3981320 | tf_op jit(solution)/shard_map/ppermute | solution.py:60
  110.4 20.5 %collective-permute-start.19 = (bf16[2,432,384]{2,1,0:T(8,128)(2,1)S(1)}, bf16[2,432,384]{2,1,0:T(8,128)(2,1)S(1)}, u32[]{:S(2)}, u32[]{:S(2)}) collective-permute-start(bf16[2,432,384]{2,1,0:T(8,128)(2,1)S(1)} %slice.234), channel_id=1, source_target_pairs={{0,2},{1,3},{2,0},{3,1},{4,6},{5,7},{6,4},{7,5},{8,10},{9,11},{10,... | collective-permute-start | bytes 1990664 | tf_op jit(solution)/shard_map/ppermute | solution.py:60
  114.9 17.8 %collective-permute-start.18 = (bf16[2,432,384]{2,1,0:T(8,128)(2,1)S(1)}, bf16[2,432,384]{2,1,0:T(8,128)(2,1)}, u32[]{:S(2)}, u32[]{:S(2)}) collective-permute-start(bf16[2,432,384]{2,1,0:T(8,128)(2,1)S(1)} %slice.233), channel_id=1, source_target_pairs={{0,4},{4,0},{8,12},{12,8},{16,20},{20,16},{24,28},{28,24},{1,5},{5... | collective-permute-start | bytes 1990664 | tf_op jit(solution)/shard_map/ppermute | solution.py:60
  115.5 18.4 %collective-permute-start.20 = (bf16[4,432,384]{2,1,0:T(8,128)(2,1)S(1)}, bf16[4,432,384]{2,1,0:T(8,128)(2,1)}, u32[]{:S(2)}, u32[]{:S(2)}) collective-permute-start(bf16[4,432,384]{2,1,0:T(8,128)(2,1)S(1)} %pad_maximum_fusion.1.refs_0_), channel_id=1, source_target_pairs={{0,1},{1,0},{2,3},{3,2},{4,5},{5,4},{6,7},{7,6},{8,9},{9,8},{10,11... | collective-permute-start | bytes 3981320 | tf_op jit(solution)/shard_map/ppermute | solution.py:60
  116.1 19.9 %collective-permute-start.21 = (bf16[4,432,384]{2,1,0:T(8,128)(2,1)}, bf16[4,432,384]{2,1,0:T(8,128)(2,1)}, u32[]{:S(2)}, u32[]{:S(2)}) collective-permute-start(bf16[4,432,384]{2,1,0:T(8,128)(2,1)} %collective-permute-done.16.refs_8_.refs_1_), channel_id=1, source_target_pairs={{0,1},{1,0},{2,3},{3,2},{4,5},{5,4},{6,7},{7,6},{8,9},{9,8},{10,11... | collective-permute-start | bytes 3981320 | tf_op jit(solution)/shard_map/ppermute | solution.py:60
  116.1 19.9 %collective-permute-start.22 = (bf16[4,432,384]{2,1,0:T(8,128)(2,1)}, bf16[4,432,384]{2,1,0:T(8,128)(2,1)}, u32[]{:S(2)}, u32[]{:S(2)}) collective-permute-start(bf16[4,432,384]{2,1,0:T(8,128)(2,1)} %collective-permute-done.17.refs_9_.refs_2_), channel_id=1, source_target_pairs={{0,1},{1,0},{2,3},{3,2},{4,5},{5,4},{6,7},{7,6},{8,9},{9,8},{10,11... | collective-permute-start | bytes 3981320 | tf_op jit(solution)/shard_map/ppermute | solution.py:60
  116.6 16.7 %copy-start.47 = (s32[23]{0:T(128)S(1)}, s32[23]{0:T(128)}, u32[]{:S(2)}) copy-start(s32[23]{0:T(128)} %stack.146.refs_0_.meta) | copy-start | bytes 280
  132.7 2.3 collective-permute-start.23
  133.1 2.8 collective-permute-start.24
  133.3 44.2 %copy-start.51 = (s32[23]{0:T(128)}, s32[23]{0:T(128)S(1)}, u32[]{:S(2)}) copy-start(s32[23]{0:T(128)S(1)} %constant_dynamic-update-slice_fusion.meta) | copy-start | bytes 280
  193.2 24.4 %collective-permute-start.25 = (bf16[2,2,4,432,384]{4,3,2,1,0:T(8,128)(2,1)}, bf16[2,2,4,432,384]{4,3,2,1,0:T(8,128)(2,1)}, u32[]{:S(2)}, u32[]{:S(2)}) collective-permute-start(bf16[2,2,4,432,384]{4,3,2,1,0:T(8,128)(2,1)} %feed_grad.2.refs_12_), channel_id=1, source_target_pairs={{0,1},{1,0},{2,3},{3,2},{4,5},{5,4},{6,7},{7,6},{8,9},{9,8},{10,11... | collective-permute-start | bytes 15925256 | tf_op jit(solution)/shard_map/ppermute | solution.py:60
  236.9 36.4 %collective-permute-start.26 = (bf16[2,2,432,384]{3,2,1,0:T(8,128)(2,1)}, bf16[2,2,432,384]{3,2,1,0:T(8,128)(2,1)S(1)}, u32[]{:S(2)}, u32[]{:S(2)}) collective-permute-start(bf16[2,2,432,384]{3,2,1,0:T(8,128)(2,1)} %get-tuple-element.161.refs_15_), channel_id=1, source_target_pairs={{0,4},{4,0},{8,12},{12,8},{16,20},{20,16},{24,28},{28,24},{1,5},{5... | collective-permute-start | bytes 3981320 | tf_op jit(solution)/shard_map/ppermute | solution.py:60
  237.7 36.1 %collective-permute-start.27 = (bf16[2,2,432,384]{3,2,1,0:T(8,128)(2,1)}, bf16[2,2,432,384]{3,2,1,0:T(8,128)(2,1)S(1)}, u32[]{:S(2)}, u32[]{:S(2)}) collective-permute-start(bf16[2,2,432,384]{3,2,1,0:T(8,128)(2,1)} %get-tuple-element.162.refs_16_), channel_id=1, source_target_pairs={{0,2},{1,3},{2,0},{3,1},{4,6},{5,7},{6,4},{7,5},{8,10},{9,11},{10,... | collective-permute-start | bytes 3981320 | tf_op jit(solution)/shard_map/ppermute | solution.py:60
  277.7 27.9 %collective-permute-start.28 = (bf16[2,432,384]{2,1,0:T(8,128)(2,1)}, bf16[2,432,384]{2,1,0:T(8,128)(2,1)}, u32[]{:S(2)}, u32[]{:S(2)}) collective-permute-start(bf16[2,432,384]{2,1,0:T(8,128)(2,1)} %fusion.8.refs_10_), channel_id=1, source_target_pairs={{0,4},{4,0},{8,12},{12,8},{16,20},{20,16},{24,28},{28,24},{1,5},{5... | collective-permute-start | bytes 1990664 | tf_op jit(solution)/shard_map/ppermute | solution.py:60
  281.0 24.6 %collective-permute-start.29 = (bf16[2,432,384]{2,1,0:T(8,128)(2,1)S(1)}, bf16[2,432,384]{2,1,0:T(8,128)(2,1)S(1)}, u32[]{:S(2)}, u32[]{:S(2)}) collective-permute-start(bf16[2,432,384]{2,1,0:T(8,128)(2,1)S(1)} %fusion.6.refs_11_), channel_id=1, source_target_pairs={{0,2},{1,3},{2,0},{3,1},{4,6},{5,7},{6,4},{7,5},{8,10},{9,11},{10,... | collective-permute-start | bytes 1990664 | tf_op jit(solution)/shard_map/ppermute | solution.py:60
  303.0 29.6 %collective-permute-start.31 = (bf16[2,2,4,48,1152]{4,3,2,1,0:T(8,128)(2,1)}, bf16[2,2,4,48,1152]{4,3,2,1,0:T(8,128)(2,1)}, u32[]{:S(2)}, u32[]{:S(2)}) collective-permute-start(bf16[2,2,4,48,1152]{4,3,2,1,0:T(8,128)(2,1)} %get-tuple-element.177), channel_id=1, source_target_pairs={{0,1},{1,0},{2,3},{3,2},{4,5},{5,4},{6,7},{7,6},{8,9},{9,8},{10,11... | collective-permute-start | bytes 5308424 | tf_op jit(solution)/shard_map/ppermute | solution.py:60
  309.9 22.7 %collective-permute-start.30 = (bf16[2,432,384]{2,1,0:T(8,128)(2,1)S(1)}, bf16[2,432,384]{2,1,0:T(8,128)(2,1)S(1)}, u32[]{:S(2)}, u32[]{:S(2)}) collective-permute-start(bf16[2,432,384]{2,1,0:T(8,128)(2,1)S(1)} %pad_maximum_fusion.3.refs_5_), channel_id=1, source_target_pairs={{0,8},{4,12},{8,0},{12,4},{16,24},{20,28},{24,16},{28,20},{1,9},{5... | collective-permute-start | bytes 1990664 | tf_op jit(solution)/shard_map/ppermute | solution.py:60
  312.3 14.4 %copy-start.44 = (f32[8,768]{1,0:T(8,128)S(1)}, f32[8,768]{1,0:T(8,128)}, u32[]{:S(2)}) copy-start(f32[8,768]{1,0:T(8,128)} %get-tuple-element.178) | copy-start | bytes 73732
  326.7 27.9 %collective-permute-start.33 = (bf16[2,1024,768]{2,1,0:T(8,128)(2,1)}, bf16[2,1024,768]{2,1,0:T(8,128)(2,1)}, u32[]{:S(2)}, u32[]{:S(2)}) collective-permute-start(bf16[2,1024,768]{2,1,0:T(8,128)(2,1)} %get-tuple-element.180), channel_id=1, source_target_pairs={{0,1},{1,0},{2,3},{3,2},{4,5},{5,4},{6,7},{7,6},{8,9},{9,8},{10,11... | collective-permute-start | bytes 9437192 | tf_op jit(solution)/shard_map/ppermute | solution.py:60
  328.4 4.2 collective-permute-start.32
  332.7 21.9 %collective-permute-start.36 = (f32[12,768]{1,0:T(8,128)S(1)}, f32[12,768]{1,0:T(8,128)S(1)}, u32[]{:S(2)}, u32[]{:S(2)}) collective-permute-start(f32[12,768]{1,0:T(8,128)S(1)} %fusion.36), channel_id=1, source_target_pairs={{0,1},{1,0},{2,3},{3,2},{4,5},{5,4},{6,7},{7,6},{8,9},{9,8},{10,11... | collective-permute-start | bytes 110600 | tf_op jit(solution)/shard_map/ppermute | solution.py:60
  336.6 8.4 %copy-start.10 = (bf16[2,2,48,1152]{3,2,1,0:T(8,128)(2,1)}, bf16[2,2,48,1152]{3,2,1,0:T(8,128)(2,1)S(1)}, u32[]{:S(2)}) copy-start(bf16[2,2,48,1152]{3,2,1,0:T(8,128)(2,1)S(1)} %pad_maximum_fusion.7.refs_7_) | copy-start | bytes 1327108
  336.6 18.0 %collective-permute-start.34 = (bf16[2,2,48,1152]{3,2,1,0:T(8,128)(2,1)S(1)}, bf16[2,2,48,1152]{3,2,1,0:T(8,128)(2,1)}, u32[]{:S(2)}, u32[]{:S(2)}) collective-permute-start(bf16[2,2,48,1152]{3,2,1,0:T(8,128)(2,1)S(1)} %pad_maximum_fusion.7.refs_7_), channel_id=1, source_target_pairs={{0,4},{4,0},{8,12},{12,8},{16,20},{20,16},{24,28},{28,24},{1,5},{5... | collective-permute-start | bytes 1327112 | tf_op jit(solution)/shard_map/ppermute | solution.py:60
  338.1 16.5 %collective-permute-start.35 = (bf16[2,2,48,1152]{3,2,1,0:T(8,128)(2,1)}, bf16[2,2,48,1152]{3,2,1,0:T(8,128)(2,1)}, u32[]{:S(2)}, u32[]{:S(2)}) collective-permute-start(bf16[2,2,48,1152]{3,2,1,0:T(8,128)(2,1)} %pad_maximum_fusion.8.refs_8_), channel_id=1, source_target_pairs={{0,2},{1,3},{2,0},{3,1},{4,6},{5,7},{6,4},{7,5},{8,10},{9,11},{10,... | collective-permute-start | bytes 1327112 | tf_op jit(solution)/shard_map/ppermute | solution.py:60
  339.6 23.0 %collective-permute-start.39 = (bf16[432,384]{1,0:T(8,128)(2,1)}, bf16[432,384]{1,0:T(8,128)(2,1)}, u32[]{:S(2)}, u32[]{:S(2)}) collective-permute-start(bf16[432,384]{1,0:T(8,128)(2,1)} %fusion.20), channel_id=1, source_target_pairs={{0,16},{4,20},{8,24},{12,28},{16,0},{20,4},{24,8},{28,12},{1,17},{... | collective-permute-start | bytes 995336 | tf_op jit(solution)/shard_map/ppermute | solution.py:60
  354.6 7.9 %collective-permute-start.40 = (f32[12,768]{1,0:T(8,128)S(1)}, f32[12,768]{1,0:T(8,128)S(1)}, u32[]{:S(2)}, u32[]{:S(2)}) collective-permute-start(f32[12,768]{1,0:T(8,128)S(1)} %add.427), channel_id=1, source_target_pairs={{0,2},{1,3},{2,0},{3,1},{4,6},{5,7},{6,4},{7,5},{8,10},{9,11},{10,... | collective-permute-start | bytes 110600 | tf_op jit(solution)/shard_map/ppermute | solution.py:60
  358.0 6.0 %collective-permute-start.38 = (bf16[2,48,1152]{2,1,0:T(8,128)(2,1)S(1)}, bf16[2,48,1152]{2,1,0:T(8,128)(2,1)S(1)}, u32[]{:S(2)}, u32[]{:S(2)}) collective-permute-start(bf16[2,48,1152]{2,1,0:T(8,128)(2,1)S(1)} %get-tuple-element.231), channel_id=1, source_target_pairs={{0,2},{1,3},{2,0},{3,1},{4,6},{5,7},{6,4},{7,5},{8,10},{9,11},{10,... | collective-permute-start | bytes 663560 | tf_op jit(solution)/shard_map/ppermute | solution.py:60
  359.2 5.9 %collective-permute-start.37 = (bf16[2,48,1152]{2,1,0:T(8,128)(2,1)S(1)}, bf16[2,48,1152]{2,1,0:T(8,128)(2,1)S(1)}, u32[]{:S(2)}, u32[]{:S(2)}) collective-permute-start(bf16[2,48,1152]{2,1,0:T(8,128)(2,1)S(1)} %get-tuple-element.232), channel_id=1, source_target_pairs={{0,4},{4,0},{8,12},{12,8},{16,20},{20,16},{24,28},{28,24},{1,5},{5... | collective-permute-start | bytes 663560 | tf_op jit(solution)/shard_map/ppermute | solution.py:60
  368.2 9.1 %collective-permute-start.43 = (f32[216,384]{1,0:T(8,128)S(1)}, f32[216,384]{1,0:T(8,128)S(1)}, u32[]{:S(2)}, u32[]{:S(2)}) collective-permute-start(f32[216,384]{1,0:T(8,128)S(1)} %dynamic-slice_bitcast_fusion), channel_id=1, source_target_pairs={{0,1},{1,0},{2,3},{3,2},{4,5},{5,4},{6,7},{7,6},{8,9},{9,8},{10,11... | collective-permute-start | bytes 995336 | tf_op jit(solution)/shard_map/ppermute | solution.py:60
  368.3 8.9 %collective-permute-start.41 = (bf16[2,48,1152]{2,1,0:T(8,128)(2,1)S(1)}, bf16[2,48,1152]{2,1,0:T(8,128)(2,1)S(1)}, u32[]{:S(2)}, u32[]{:S(2)}) collective-permute-start(bf16[2,48,1152]{2,1,0:T(8,128)(2,1)S(1)} %pad_maximum_fusion.12), channel_id=1, source_target_pairs={{0,8},{4,12},{8,0},{12,4},{16,24},{20,28},{24,16},{28,20},{1,9},{5... | collective-permute-start | bytes 663560 | tf_op jit(solution)/shard_map/ppermute | solution.py:60
  369.0 8.2 %collective-permute-start.42 = (f32[12,768]{1,0:T(8,128)S(1)}, f32[12,768]{1,0:T(8,128)S(1)}, u32[]{:S(2)}, u32[]{:S(2)}) collective-permute-start(f32[12,768]{1,0:T(8,128)S(1)} %add.434), channel_id=1, source_target_pairs={{0,8},{4,12},{8,0},{12,4},{16,24},{20,28},{24,16},{28,20},{1,9},{5... | collective-permute-start | bytes 110600 | tf_op jit(solution)/shard_map/ppermute | solution.py:60
  370.4 17.1 %copy-start.14 = (f32[2,48,1152]{2,1,0:T(8,128)S(1)}, f32[2,48,1152]{2,1,0:T(8,128)}, u32[]{:S(2)}) copy-start(f32[2,48,1152]{2,1,0:T(8,128)} %copy-done.13) | copy-start | bytes 1327108
  370.4 36.5 %collective-permute-start.49 = (bf16[1024,768]{1,0:T(8,128)(2,1)}, bf16[1024,768]{1,0:T(8,128)(2,1)}, u32[]{:S(2)}, u32[]{:S(2)}) collective-permute-start(bf16[1024,768]{1,0:T(8,128)(2,1)} %fusion), channel_id=1, source_target_pairs={{0,2},{1,3},{2,0},{3,1},{4,6},{5,7},{6,4},{7,5},{8,10},{9,11},{10,... | collective-permute-start | bytes 4718600 | tf_op jit(solution)/shard_map/ppermute | solution.py:60
  377.3 8.1 %collective-permute-start.45 = (f32[12,768]{1,0:T(8,128)S(1)}, f32[12,768]{1,0:T(8,128)S(1)}, u32[]{:S(2)}, u32[]{:S(2)}) collective-permute-start(f32[12,768]{1,0:T(8,128)S(1)} %add.438), channel_id=1, source_target_pairs={{0,16},{4,20},{8,24},{12,28},{16,0},{20,4},{24,8},{28,12},{1,17},{... | collective-permute-start | bytes 110600 | tf_op jit(solution)/shard_map/ppermute | solution.py:60
  378.0 9.5 %collective-permute-start.44 = (bf16[48,1152]{1,0:T(8,128)(2,1)S(1)}, bf16[48,1152]{1,0:T(8,128)(2,1)S(1)}, u32[]{:S(2)}, u32[]{:S(2)}) collective-permute-start(bf16[48,1152]{1,0:T(8,128)(2,1)S(1)} %fusion.27), channel_id=1, source_target_pairs={{0,16},{4,20},{8,24},{12,28},{16,0},{20,4},{24,8},{28,12},{1,17},{... | collective-permute-start | bytes 331784 | tf_op jit(solution)/shard_map/ppermute | solution.py:60
  380.3 26.6 %copy-start.1 = (f32[1,1024,768]{2,1,0:T(8,128)S(1)}, f32[1,1024,768]{2,1,0:T(8,128)}, u32[]{:S(2)}) copy-start(f32[1,1024,768]{2,1,0:T(8,128)} %token_grad.3) | copy-start | bytes 9437188
  389.1 13.8 %collective-permute-start.52 = (f32[24,1152]{1,0:T(8,128)S(1)}, f32[24,1152]{1,0:T(8,128)}, u32[]{:S(2)}, u32[]{:S(2)}) collective-permute-start(f32[24,1152]{1,0:T(8,128)S(1)} %dynamic-slice_bitcast_fusion.2), channel_id=1, source_target_pairs={{0,1},{1,0},{2,3},{3,2},{4,5},{5,4},{6,7},{7,6},{8,9},{9,8},{10,11... | collective-permute-start | bytes 331784 | tf_op jit(solution)/shard_map/ppermute | solution.py:60
  392.5 1.4 collective-permute-start.46
  394.5 3.6 collective-permute-start.47
  398.7 3.6 collective-permute-start.48
  410.9 4.4 %collective-permute-start.50 = (f32[1,1]{1,0:T(1,128)}, f32[1,1]{1,0:T(1,128)}, u32[]{:S(2)}, u32[]{:S(2)}) collective-permute-start(f32[1,1]{1,0:T(1,128)} %add.447), channel_id=1, source_target_pairs={{0,16},{4,20},{8,24},{12,28},{16,0},{20,4},{24,8},{28,12},{1,17},{... | collective-permute-start | bytes 20 | tf_op jit(solution)/shard_map/ppermute | solution.py:60
  415.9 3.6 collective-permute-start.51
  (44 other events, 113.1 us)

commit v3 on v2

--- a/solution.py
+++ b/solution.py
@@ -329,7 +329,7 @@
 def attend(plan, q, k, v, segq, segk, start, count, before, deps):
     blocks, rows, length, width = k.shape
     pairs = width // LANES
-    group = 2
+    group = 3
     lanes = group * LANES
     extra = (*before, *deps)
     kv_spec = pl.BlockSpec((blocks, 1, length, lanes), lambda r, p, *_: (0, r + start, 0, p))
@@ -628,12 +628,9 @@
 
 
 def feed_grad_kernel(added, meta, h1_ref, du_ref, gl_ref, dz_ref, ol_ref, da_ref, *refs):
+    got_ref = refs[0] if added else None
     scr = refs[-1]
     step = pl.program_id(0)
-    if added:
-        scr, got_ref, sem = refs[-3:]
-        copy = pltpu.make_async_copy(refs[0], got_ref, sem)
-        pl.when(step == 0)(copy.start)
     half = dz_ref.shape[1]
     width = 2 * half
     we_rows = 4 * SLAB
@@ -676,8 +673,6 @@
     @pl.when(step == 0)
     def _():
         scr[:, :half] = dot_tn(ol_ref[...], da_ref[...])
-        if added:
-            copy.wait()
         put_all(we_rows, slice(0, half))
 
     for u in range(2):
@@ -724,10 +719,9 @@
                 wide(lambda u, m: (0, 0)),
                 pl.BlockSpec((tokens, half), lambda u, m: (0, m[0])),
             ]
-            + [pl.BlockSpec(memory_space=pl.ANY)] * added,
+            + [slab_spec(every)] * added,
             out_specs=[slab_spec(lead) for lead, _ in outs],
-            scratch_shapes=[pltpu.VMEM((width, width), F32)]
-            + ([pltpu.VMEM(every + slab, BF16), pltpu.SemaphoreType.DMA] if added else []),
+            scratch_shapes=[pltpu.VMEM((width, width), F32)],
         ),
         out_shape=[jax.ShapeDtypeStruct(lead + slab, dtype) for lead, dtype in outs],
         compiler_params=params(1),

time: 432 us -> 431 us (level)
  Pallas kernels: 236 us -> 249 us
  starting transfers between devices: 64.7 us -> 54.2 us
    ppermute x53, starting transfers between devices: 64.7 us -> 54.2 us  [swap(): lax.ppermute(x, axis, [(i, i ^ bit) for i in range(lax.axis_size(axis))])]
    pallas_call x2, Pallas kernels: 52.5 us -> 61.2 us  [attend_back(): pl.pallas_call(skipping(functools.partial(attend_back_kernel, blocks, sta...]
    pallas_call x2, Pallas kernels: 26.3 us -> 31.1 us  [attend(): pl.pallas_call(skipping(functools.partial(attend_kernel, blocks, start),...]
  transfers between devices with their start and end apart: 53 -> 53, of which waited for: 21 -> 19; matrix products, arithmetic and copies ran while one was open for 9% -> 9% of each run, Pallas kernels for 37% -> 41%
where the time goes in v3:
time: 431 us; the launch traced here: 427 us
  Pallas kernels  249 us (58%)
  starting transfers between devices  54.2 us (13%)
  waiting for transfers between devices  48.7 us (11%)
  other arithmetic  44.4 us (10%)
  local copies, waits for them, and re-layouts  22.7 us (5%)
  between operations  8.29 us (2%)
    pallas_call x2, Pallas kernels, attend_back(): pl.pallas_call(skipping(functools.partial(attend_back_kernel, blocks, sta...  61.2 us
    ppermute x53, starting transfers between devices, swap(): lax.ppermute(x, axis, [(i, i ^ bit) for i in range(lax.axis_size(axis))])  54.2 us
    ppermute x53, waiting for transfers between devices, swap(): lax.ppermute(x, axis, [(i, i ^ bit) for i in range(lax.axis_size(axis))])  48.7 us
    pallas_call x1, Pallas kernels, feed(): pl.pallas_call(feed_kernel, grid_spec=pltpu.PrefetchScalarGridSpec(num_sc...  41.1 us
    pallas_call x2, Pallas kernels, feed_grad(): pl.pallas_call(functools.partial(feed_grad_kernel, added), grid_spec=pltp...  34.1 us
    pallas_call x2, Pallas kernels, attend(): pl.pallas_call(skipping(functools.partial(attend_kernel, blocks, start),...  31.1 us
    pallas_call x2, Pallas kernels, token_grad(): pl.pallas_call(skipping(functools.partial(token_grad_kernel, steps, sent,...  23.6 us
    pallas_call x1, Pallas kernels, project(): pl.pallas_call(skipping(functools.partial(project_kernel, spans, steps),...  21.5 us
  transfers between devices with their start and end apart: 53, of which 19 were waited for; matrix products, arithmetic and copies ran while one was open for 9% of the time, Pallas kernels for 41%

profile of v3, /device:TPU:0, one launch (start us, length us, event | category | flops | bytes accessed | tf_op | source)
XLA Modules:
  0.0 427.2 jit_solution(14418008808793015763)
XLA Ops:
  4.4 1.2 fusion.46
  6.3 3.7 collective-permute-start.1
  11.0 1.5 collective-permute-start.8
  13.3 3.3 collective-permute-done.1
  17.7 6.7 %collective-permute-done.2 = bf16[2,48,1280]{2,1,0:T(8,128)(2,1)S(1)} collective-permute-done((bf16[2,48,1280]{2,1,0:T(8,128)(2,1)S(1)}, bf16[2,48,1280]{2,1,0:T(8,128)(2,1)S(1)}, u32[]{:S(2)}, u32[]{:S(2)}) %collective-permute-start.2) | collective-permute-done | bytes 245792 | tf_op jit(solution)/shard_map/ppermute | solution.py:60
  25.2 1.4 collective-permute-start.6
  26.6 1.5 collective-permute-start.5
  28.5 2.7 collective-permute-start.7
  33.4 8.4 %share.2.refs_5_.refs_8_ = f32[2,6,256,128]{3,2,1,0:T(8,128)} custom-call(bf16[4,12,256,1024]{3,2,1,0:T(8,128)(2,1)} %refs_9_.3, s32[4,256,128]{2,1,0:T(8,128)} %broadcast_in_dim.62.refs_1_.refs_4_.refs_10_, s32[4,8,1024]{2,1,0:T(8,128)} %broadcast_in_dim.63.refs_2_, bf16[4,48,1280]{2,1,0:T(8,128)(2,1)} %pad_maximum_fusion.6.refs_3_.refs_8_), custom_call_target="tpu_custom_call" | custom-call | flops 25165824 | bytes 12582912 | tf_op jit(solution)/shard_map/share/pallas_call | solution.py:228
  41.8 3.6 collective-permute-done.7
  45.5 1.5 pad_maximum_fusion
  52.2 8.2 %share.3.refs_15_.refs_8_ = f32[2,6,256,128]{3,2,1,0:T(8,128)} custom-call(bf16[4,12,256,1024]{3,2,1,0:T(8,128)(2,1)} %refs_9_.3, s32[4,256,128]{2,1,0:T(8,128)} %broadcast_in_dim.62.refs_1_.refs_4_.refs_10_, s32[4,8,1024]{2,1,0:T(8,128)} %broadcast_in_dim.63.refs_2_, bf16[4,48,1280]{2,1,0:T(8,128)(2,1)} %copy-done.8, bf16[4,48,1280]{2,1,0:T(8,128)(2,1)} %copy-done.9, ...), custom_call_target="tpu_custom_call" | custom-call | flops 25165824 | bytes 12582912 | tf_op jit(solution)/shard_map/share/pallas_call | solution.py:228
  60.4 1.6 collective-permute-done.9.refs_11_
  64.4 3.5 collective-permute-done.13
  67.8 3.0 collective-permute-done.14
  71.6 1.3 pad_maximum_fusion.1.refs_0_
  72.9 1.6 collective-permute-start.17
  75.0 21.5 %project.1 = (bf16[1024,768]{1,0:T(8,128)(2,1)}, bf16[4,1024,768]{2,1,0:T(8,128)(2,1)}, bf16[4,1024,768]{2,1,0:T(8,128)(2,1)}, bf16[768,2304]{1,0:T(8,128)(2,1)}) custom-call(s32[23]{0:T(128)} %stack.146.refs_0_.meta, s32[4,4]{1,0:T(4,128)} %copy-done.42, bf16[1024,768]{1,0:T(8,128)(2,1)} %bitcast.255, bf16[1024,768]{1,0:T(8,128)(2,1)} %bitcast.44.refs_3_.refs_2_, ...), custom_call_target="tpu_custom_call" | custom-call | flops 10871635968 | bytes 12582912 | tf_op jit(solution)/shard_map/project/pallas_call | solution.py:179
  97.2 15.6 %attend.2 = (bf16[4,256,768]{2,1,0:T(8,128)(2,1)}, f32[4,6,256,128]{3,2,1,0:T(8,128)}) custom-call(s32[4,5]{1,0:T(4,128)} %pad_add_fusion.refs_0_.refs_1_, bf16[4,256,768]{2,1,0:T(8,128)(2,1)} %bitcast.258, bf16[4,4,256,768]{3,2,1,0:T(8,128)(2,1)} %bitcast.244, bf16[4,4,256,768]{3,2,1,0:T(8,128)(2,1)} %bitcast.248, ...), custom_call_target="tpu_custom_call" | custom-call | flops 6442450944 | bytes 3145728 | tf_op jit(solution)/shard_map/attend/pallas_call | solution.py:337
  115.2 2.5 collective-permute-start.19
  118.2 15.4 %attend.3 = (bf16[4,256,768]{2,1,0:T(8,128)(2,1)}, f32[4,6,256,128]{3,2,1,0:T(8,128)}) custom-call(s32[4,5]{1,0:T(4,128)} %pad_add_fusion.refs_0_.refs_1_, bf16[4,256,768]{2,1,0:T(8,128)(2,1)} %bitcast.259, bf16[4,4,256,768]{3,2,1,0:T(8,128)(2,1)} %bitcast.245, bf16[4,4,256,768]{3,2,1,0:T(8,128)(2,1)} %bitcast.249, ...), custom_call_target="tpu_custom_call", output_to_operand_aliasing={{0}: (6, {}), {1}: (7, {})} | custom-call | flops 6442450944 | bytes 3145728 | tf_op jit(solution)/shard_map/attend/pallas_call | solution.py:337
  134.9 1.3 collective-permute-done.23.refs_8_
  137.6 41.1 %feed.1 = (bf16[1024,768]{1,0:T(8,128)(2,1)}, f32[1024,768]{1,0:T(8,128)}, bf16[1024,768]{1,0:T(8,128)(2,1)}, bf16[1024,3072]{1,0:T(8,128)(2,1)}, bf16[1024,3072...) custom-call(s32[23]{0:T(128)} %stack.146.refs_0_.meta, ...), custom_call_target="tpu_custom_call" | custom-call | flops 21743271936 | bytes 28311552 | tf_op jit(solution)/shard_map/feed/pallas_call | solution.py:590
  178.7 15.7 %feed_grad.2.refs_12_ = bf16[2,2,4,432,384]{4,3,2,1,0:T(8,128)(2,1)} custom-call(s32[23]{0:T(128)} %copy-done.51, bf16[1024,768]{1,0:T(8,128)(2,1)} %get-tuple-element.152.h1_ref, bf16[1024,3072]{1,0:T(8,128)(2,1)} %get-tuple-element.153.du_ref, bf16[1024,3072]{1,0:T(8,128)(2,1)} %get-tuple-element.154.gl_ref, bf16[1024,768]{1,0:T(8,128)(2,1)} %get-tuple-element.155.dz_ref, ...), custom_call_target="tpu_custom_call" | custom-call | flops 5435817984 | bytes 12582912 | tf_op jit(solution)/shard_map/feed_grad/pallas_call | solution.py:709
  194.9 30.5 %attend_back.2 = (bf16[4,256,768]{2,1,0:T(8,128)(2,1)}, bf16[4,4,256,768]{3,2,1,0:T(8,128)(2,1)}, bf16[4,4,256,768]{3,2,1,0:T(8,128)(2,1)}) custom-call(s32[23]{0:T(128)} %stack.146.refs_0_.meta, s32[4,5]{1,0:T(4,128)} %pad_add_fusion.refs_0_.refs_1_, bf16[4,256,768]{2,1,0:T(8,128)(2,1)} %bitcast.260, bf16[4,4,256,768]{3,2,1,0:T(8,128)(2,1)} %bitcast.246, ...), custom_call_target="tpu_custom_call" | custom-call | flops 16106127360 | bytes 6291456 | tf_op jit(solution)/shard_map/attend_back/pallas_call | solution.py:441
  225.4 18.4 %feed_grad.3 = (f32[4,432,384]{2,1,0:T(8,128)}, f32[2,432,384]{2,1,0:T(8,128)}, f32[2,432,384]{2,1,0:T(8,128)}, bf16[2,2,432,384]{3,2,1,0:T(8,128)(2,1)}, bf16[2,2,432,384]{3,2,1,0:T(8,128)(2,1)}) custom-call(s32[23]{0:T(128)} %stack.146.refs_0_.meta, bf16[1024,768]{1,0:T(8,128)(2,1)} %get-tuple-element.152.h1_ref, ...), custom_call_target="tpu_custom_call" | custom-call | flops 5435817984 | bytes 12582912 | tf_op jit(solution)/shard_map/feed_grad/pallas_call | solution.py:709
  244.6 2.1 collective-permute-start.27
  246.7 30.8 %attend_back.3 = (bf16[4,256,768]{2,1,0:T(8,128)(2,1)}, bf16[4,4,256,768]{3,2,1,0:T(8,128)(2,1)}, bf16[4,4,256,768]{3,2,1,0:T(8,128)(2,1)}) custom-call(s32[23]{0:T(128)} %stack.146.refs_0_.meta, s32[4,5]{1,0:T(4,128)} %pad_add_fusion.refs_0_.refs_1_, bf16[4,256,768]{2,1,0:T(8,128)(2,1)} %bitcast.261, ...), custom_call_target="tpu_custom_call", output_to_operand_aliasing={{0}: (12, {}), {1}: (13, {}), {2}: (14, {})} | custom-call | flops 16106127360 | bytes 6291456 | tf_op jit(solution)/shard_map/attend_back/pallas_call | solution.py:441
  278.6 1.6 convert_element_type.137
  281.5 1.6 copy-done.15
  283.3 2.2 collective-permute-start.29
  285.5 19.8 %joint_grad.1 = (f32[2,2,4,48,1152]{4,3,2,1,0:T(8,128)}, bf16[2,2,4,48,1152]{4,3,2,1,0:T(8,128)(2,1)}, f32[8,768]{1,0:T(8,128)}) custom-call(s32[23]{0:T(128)} %stack.146.refs_0_.meta, bf16[1024,768]{1,0:T(8,128)(2,1)} %bitcast.257, bf16[1024,768]{1,0:T(8,128)(2,1)} %bitcast.44.refs_3_.refs_2_, bf16[512,768]{1,0:T(8,128)(2,1)} %bitcast.46.refs_4_.refs_3_, ...), custom_call_target="tpu_custom_call" | custom-call | flops 10871635968 | bytes 25165824 | tf_op jit(solution)/shard_map/joint_grad/pallas_call | solution.py:851
  305.3 2.7 fusion.4
  309.6 3.0 collective-permute-start.30
  312.6 14.0 %token_grad.2 = (bf16[2,1024,768]{2,1,0:T(8,128)(2,1)}, bf16[1,1024,768]{2,1,0:T(8,128)(2,1)}) custom-call(s32[23]{0:T(128)} %stack.146.refs_0_.meta, s32[4,4]{1,0:T(4,128)} %copy-done.42, bf16[4,1024,768]{2,1,0:T(8,128)(2,1)} %bitcast.234, bf16[4,1024,768]{2,1,0:T(8,128)(2,1)} %bitcast.237, bf16[768,2304]{1,0:T(8,128)(2,1)} %get-tuple-element.165.refs_4_, ...), custom_call_target="tpu_custom_call" | custom-call | flops 7247757312 | bytes 14155776 | tf_op jit(solution)/shard_map/token_grad/pallas_call | solution.py:780
  328.4 1.8 collective-permute-start.32
  330.2 2.4 collective-permute-done.32
  333.5 3.0 fusion.44
  336.6 1.8 collective-permute-start.34
  340.6 3.1 collective-permute-start.39
  343.7 9.6 %token_grad.3 = f32[1,1024,768]{2,1,0:T(8,128)} custom-call(s32[23]{0:T(128)} %stack.146.refs_0_.meta, s32[4,4]{1,0:T(4,128)} %copy-done.42, bf16[4,1024,768]{2,1,0:T(8,128)(2,1)} %bitcast.235, bf16[4,1024,768]{2,1,0:T(8,128)(2,1)} %bitcast.238, bf16[768,2304]{1,0:T(8,128)(2,1)} %get-tuple-element.165.refs_4_, bf16[1024,768]{1,0:T(8,128)(2,1)} %bitcast.243, ...), custom_call_target="tpu_custom_call" | custom-call | flops 2415919104 | bytes 4718592 | tf_op jit(solution)/shard_map/token_grad/pallas_call | solution.py:780
  353.3 1.2 collective-permute-start.40
  358.3 3.2 fusion
  361.5 1.5 collective-permute-done.38
  363.8 1.8 multiply_reduce_fusion
  366.9 1.3 collective-permute-start.41
  370.2 5.7 %collective-permute-done.42 = f32[12,768]{1,0:T(8,128)S(1)} collective-permute-done((f32[12,768]{1,0:T(8,128)S(1)}, f32[12,768]{1,0:T(8,128)S(1)}, u32[]{:S(2)}, u32[]{:S(2)}) %collective-permute-start.42) | collective-permute-done | bytes 36896 | tf_op jit(solution)/shard_map/ppermute | solution.py:60
  376.7 2.2 collective-permute-start.44
  378.9 1.3 bitcast_select_fusion.1
  381.1 3.4 collective-permute-done.45
  386.3 1.6 multiply_reduce_fusion.1
  389.3 1.4 multiply_reduce_fusion.2
  391.3 1.4 collective-permute-start.46
  393.3 1.8 collective-permute-start.47
  395.2 1.7 collective-permute-done.47
  397.5 1.4 collective-permute-start.48
  398.9 2.2 collective-permute-done.48
  401.7 1.6 bitcast_select_fusion.3
  403.3 2.3 collective-permute-done.49
  405.6 4.0 bitcast_add_fusion
  409.5 1.9 collective-permute-start.50
  411.4 2.5 collective-permute-done.50
  414.5 2.5 collective-permute-start.51
  419.8 1.2 multiply_bitcast_fusion
  (302 shorter events, 53.8 us)
Async XLA Ops:
  2.9 3.4 collective-permute-start
  4.4 6.2 %copy-start.21 = (f32[96,768]{1,0:T(8,128)S(1)}, f32[96,768]{1,0:T(8,128)}, u32[]{:S(2)}) copy-start(f32[96,768]{1,0:T(8,128)} %param.29) | copy-start | bytes 884740
  6.3 10.3 %collective-permute-start.1 = (bf16[48,1280]{1,0:T(8,128)(2,1)S(1)}, bf16[48,1280]{1,0:T(8,128)(2,1)S(1)}, u32[]{:S(2)}, u32[]{:S(2)}) collective-permute-start(bf16[48,1280]{1,0:T(8,128)(2,1)S(1)} %maximum_select_fusion.1), channel_id=1, source_target_pairs={{0,16},{4,20},{8,24},{12,28},{16,0},{20,4},{24,8},{28,12},{1,17},{... | collective-permute-start | bytes 368648 | tf_op jit(solution)/shard_map/ppermute | solution.py:60
  10.8 6.7 %collective-permute-start.3 = (bf16[216,384]{1,0:T(8,128)(2,1)S(1)}, bf16[216,384]{1,0:T(8,128)(2,1)S(1)}, u32[]{:S(2)}, u32[]{:S(2)}) collective-permute-start(bf16[216,384]{1,0:T(8,128)(2,1)S(1)} %get-tuple-element.252), channel_id=1, source_target_pairs={{0,1},{1,0},{2,3},{3,2},{4,5},{5,4},{6,7},{7,6},{8,9},{9,8},{10,11... | collective-permute-start | bytes 497672 | tf_op jit(solution)/shard_map/ppermute | solution.py:60
  11.0 30.8 %collective-permute-start.8 = (bf16[2,256,768]{2,1,0:T(8,128)(2,1)}, bf16[2,256,768]{2,1,0:T(8,128)(2,1)}, u32[]{:S(2)}, u32[]{:S(2)}) collective-permute-start(bf16[2,256,768]{2,1,0:T(8,128)(2,1)} %get-tuple-element.124), channel_id=1, source_target_pairs={{0,2},{1,3},{2,0},{3,1},{4,6},{5,7},{6,4},{7,5},{8,10},{9,11},{10,... | collective-permute-start | bytes 2359304 | tf_op jit(solution)/shard_map/ppermute | solution.py:60
  12.5 12.7 %collective-permute-start.4 = (bf16[4,256,768]{2,1,0:T(8,128)(2,1)S(1)}, bf16[4,256,768]{2,1,0:T(8,128)(2,1)}, u32[]{:S(2)}, u32[]{:S(2)}) collective-permute-start(bf16[4,256,768]{2,1,0:T(8,128)(2,1)S(1)} %copy-done.11), channel_id=1, source_target_pairs={{0,1},{1,0},{2,3},{3,2},{4,5},{5,4},{6,7},{7,6},{8,9},{9,8},{10,11... | collective-permute-start | bytes 4718600 | tf_op jit(solution)/shard_map/ppermute | solution.py:60
  16.6 7.8 %collective-permute-start.2 = (bf16[2,48,1280]{2,1,0:T(8,128)(2,1)S(1)}, bf16[2,48,1280]{2,1,0:T(8,128)(2,1)S(1)}, u32[]{:S(2)}, u32[]{:S(2)}) collective-permute-start(bf16[2,48,1280]{2,1,0:T(8,128)(2,1)S(1)} %pad_maximum_fusion.11), channel_id=1, source_target_pairs={{0,8},{4,12},{8,0},{12,4},{16,24},{20,28},{24,16},{28,20},{1,9},{5... | collective-permute-start | bytes 737288 | tf_op jit(solution)/shard_map/ppermute | solution.py:60
  25.2 20.2 %collective-permute-start.6 = (bf16[4,48,1280]{2,1,0:T(8,128)(2,1)}, bf16[4,48,1280]{2,1,0:T(8,128)(2,1)S(1)}, u32[]{:S(2)}, u32[]{:S(2)}) collective-permute-start(bf16[4,48,1280]{2,1,0:T(8,128)(2,1)} %pad_maximum_fusion.6.refs_3_.refs_8_), channel_id=1, source_target_pairs={{0,4},{4,0},{8,12},{12,8},{16,20},{20,16},{24,28},{28,24},{1,5},{5... | collective-permute-start | bytes 1474568 | tf_op jit(solution)/shard_map/ppermute | solution.py:60
  26.6 18.8 %collective-permute-start.5 = (bf16[4,48,1280]{2,1,0:T(8,128)(2,1)}, bf16[4,48,1280]{2,1,0:T(8,128)(2,1)S(1)}, u32[]{:S(2)}, u32[]{:S(2)}) collective-permute-start(bf16[4,48,1280]{2,1,0:T(8,128)(2,1)} %pad_maximum_fusion.6.refs_3_.refs_8_), channel_id=1, source_target_pairs={{0,2},{1,3},{2,0},{3,1},{4,6},{5,7},{6,4},{7,5},{8,10},{9,11},{10,... | collective-permute-start | bytes 1474568 | tf_op jit(solution)/shard_map/ppermute | solution.py:60
  28.5 16.9 %collective-permute-start.7 = (bf16[432,384]{1,0:T(8,128)(2,1)S(1)}, bf16[432,384]{1,0:T(8,128)(2,1)S(1)}, u32[]{:S(2)}, u32[]{:S(2)}) collective-permute-start(bf16[432,384]{1,0:T(8,128)(2,1)S(1)} %pad_maximum_fusion.10), channel_id=1, source_target_pairs={{0,16},{4,20},{8,24},{12,28},{16,0},{20,4},{24,8},{28,12},{1,17},{... | collective-permute-start | bytes 995336 | tf_op jit(solution)/shard_map/ppermute | solution.py:60
  31.3 15.9 %copy-start.42 = (s32[4,4]{1,0:T(4,128)}, s32[4,4]{1,0:T(4,128)S(1)}, u32[]{:S(2)}) copy-start(s32[4,4]{1,0:T(4,128)S(1)} %get-tuple-element.228.refs_1_) | copy-start | bytes 196
  45.4 6.7 %copy-start.8 = (bf16[4,48,1280]{2,1,0:T(8,128)(2,1)}, bf16[4,48,1280]{2,1,0:T(8,128)(2,1)S(1)}, u32[]{:S(2)}) copy-start(bf16[4,48,1280]{2,1,0:T(8,128)(2,1)S(1)} %collective-permute-done.6.refs_3_.refs_10_) | copy-start | bytes 1474564
  47.0 15.0 %collective-permute-start.11 = (bf16[12,48,1280]{2,1,0:T(8,128)(2,1)S(1)}, bf16[12,48,1280]{2,1,0:T(8,128)(2,1)}, u32[]{:S(2)}, u32[]{:S(2)}) collective-permute-start(bf16[12,48,1280]{2,1,0:T(8,128)(2,1)S(1)} %pad_maximum_fusion), channel_id=1, source_target_pairs={{0,1},{1,0},{2,3},{3,2},{4,5},{5,4},{6,7},{7,6},{8,9},{9,8},{10,11... | collective-permute-start | bytes 4423688 | tf_op jit(solution)/shard_map/ppermute | solution.py:60
  48.2 13.8 %collective-permute-start.10 = (bf16[2,256,768]{2,1,0:T(8,128)(2,1)}, bf16[2,256,768]{2,1,0:T(8,128)(2,1)}, u32[]{:S(2)}, u32[]{:S(2)}) collective-permute-start(bf16[2,256,768]{2,1,0:T(8,128)(2,1)} %collective-permute-done.8), channel_id=1, source_target_pairs={{0,1},{1,0},{2,3},{3,2},{4,5},{5,4},{6,7},{7,6},{8,9},{9,8},{10,11... | collective-permute-start | bytes 2359304 | tf_op jit(solution)/shard_map/ppermute | solution.py:60
  48.7 13.3 %collective-permute-start.9 = (bf16[4,48,1280]{2,1,0:T(8,128)(2,1)S(1)}, bf16[4,48,1280]{2,1,0:T(8,128)(2,1)}, u32[]{:S(2)}, u32[]{:S(2)}) collective-permute-start(bf16[4,48,1280]{2,1,0:T(8,128)(2,1)S(1)} %collective-permute-done.5.refs_4_.refs_9_), channel_id=1, source_target_pairs={{0,4},{4,0},{8,12},{12,8},{16,20},{20,16},{24,28},{28,24},{1,5},{5... | collective-permute-start | bytes 1474568 | tf_op jit(solution)/shard_map/ppermute | solution.py:60
  51.0 16.9 %collective-permute-start.13 = (bf16[2,432,384]{2,1,0:T(8,128)(2,1)}, bf16[2,432,384]{2,1,0:T(8,128)(2,1)}, u32[]{:S(2)}, u32[]{:S(2)}) collective-permute-start(bf16[2,432,384]{2,1,0:T(8,128)(2,1)} %pad_maximum_fusion.2), channel_id=1, source_target_pairs={{0,8},{4,12},{8,0},{12,4},{16,24},{20,28},{24,16},{28,20},{1,9},{5... | collective-permute-start | bytes 1990664 | tf_op jit(solution)/shard_map/ppermute | solution.py:60
  51.7 19.2 %collective-permute-start.14 = (bf16[2,256,768]{2,1,0:T(8,128)(2,1)}, bf16[2,256,768]{2,1,0:T(8,128)(2,1)}, u32[]{:S(2)}, u32[]{:S(2)}) collective-permute-start(bf16[2,256,768]{2,1,0:T(8,128)(2,1)} %get-tuple-element.132), channel_id=1, source_target_pairs={{0,2},{1,3},{2,0},{3,1},{4,6},{5,7},{6,4},{7,5},{8,10},{9,11},{10,... | collective-permute-start | bytes 2359304 | tf_op jit(solution)/shard_map/ppermute | solution.py:60
  60.4 10.6 %copy-start.50 = (pred[8]{0:T(512)(128)(4,1)S(1)}, pred[8]{0:T(512)(128)(4,1)}, u32[]{:S(2)}) copy-start(pred[8]{0:T(512)(128)(4,1)} %constant.203.clone.1) | copy-start | bytes 28
  62.0 8.9 %collective-permute-start.12 = (bf16[4,48,1280]{2,1,0:T(8,128)(2,1)}, bf16[4,48,1280]{2,1,0:T(8,128)(2,1)S(1)}, u32[]{:S(2)}, u32[]{:S(2)}) collective-permute-start(bf16[4,48,1280]{2,1,0:T(8,128)(2,1)} %collective-permute-done.9.refs_11_), channel_id=1, source_target_pairs={{0,1},{1,0},{2,3},{3,2},{4,5},{5,4},{6,7},{7,6},{8,9},{9,8},{10,11... | collective-permute-start | bytes 1474568 | tf_op jit(solution)/shard_map/ppermute | solution.py:60
  70.9 4.1 collective-permute-start.15
  72.9 44.7 %copy-start.17 = (bf16[4,432,384]{2,1,0:T(8,128)(2,1)}, bf16[4,432,384]{2,1,0:T(8,128)(2,1)S(1)}, u32[]{:S(2)}) copy-start(bf16[4,432,384]{2,1,0:T(8,128)(2,1)S(1)} %pad_maximum_fusion.1.refs_0_) | copy-start | bytes 3981316
  72.9 39.9 %collective-permute-start.17 = (bf16[4,432,384]{2,1,0:T(8,128)(2,1)S(1)}, bf16[4,432,384]{2,1,0:T(8,128)(2,1)}, u32[]{:S(2)}, u32[]{:S(2)}) collective-permute-start(bf16[4,432,384]{2,1,0:T(8,128)(2,1)S(1)} %pad_maximum_fusion.1.refs_0_), channel_id=1, source_target_pairs={{0,4},{4,0},{8,12},{12,8},{16,20},{20,16},{24,28},{28,24},{1,5},{5... | collective-permute-start | bytes 3981320 | tf_op jit(solution)/shard_map/ppermute | solution.py:60
  74.5 38.3 %collective-permute-start.16 = (bf16[4,432,384]{2,1,0:T(8,128)(2,1)S(1)}, bf16[4,432,384]{2,1,0:T(8,128)(2,1)}, u32[]{:S(2)}, u32[]{:S(2)}) collective-permute-start(bf16[4,432,384]{2,1,0:T(8,128)(2,1)S(1)} %pad_maximum_fusion.1.refs_0_), channel_id=1, source_target_pairs={{0,2},{1,3},{2,0},{3,1},{4,6},{5,7},{6,4},{7,5},{8,10},{9,11},{10,... | collective-permute-start | bytes 3981320 | tf_op jit(solution)/shard_map/ppermute | solution.py:60
  115.2 18.5 %collective-permute-start.19 = (bf16[2,432,384]{2,1,0:T(8,128)(2,1)S(1)}, bf16[2,432,384]{2,1,0:T(8,128)(2,1)S(1)}, u32[]{:S(2)}, u32[]{:S(2)}) collective-permute-start(bf16[2,432,384]{2,1,0:T(8,128)(2,1)S(1)} %slice.234), channel_id=1, source_target_pairs={{0,2},{1,3},{2,0},{3,1},{4,6},{5,7},{6,4},{7,5},{8,10},{9,11},{10,... | collective-permute-start | bytes 1990664 | tf_op jit(solution)/shard_map/ppermute | solution.py:60
  117.6 16.0 %collective-permute-start.18 = (bf16[2,432,384]{2,1,0:T(8,128)(2,1)S(1)}, bf16[2,432,384]{2,1,0:T(8,128)(2,1)}, u32[]{:S(2)}, u32[]{:S(2)}) collective-permute-start(bf16[2,432,384]{2,1,0:T(8,128)(2,1)S(1)} %slice.233), channel_id=1, source_target_pairs={{0,4},{4,0},{8,12},{12,8},{16,20},{20,16},{24,28},{28,24},{1,5},{5... | collective-permute-start | bytes 1990664 | tf_op jit(solution)/shard_map/ppermute | solution.py:60
  117.6 17.3 %collective-permute-start.20 = (bf16[4,432,384]{2,1,0:T(8,128)(2,1)S(1)}, bf16[4,432,384]{2,1,0:T(8,128)(2,1)}, u32[]{:S(2)}, u32[]{:S(2)}) collective-permute-start(bf16[4,432,384]{2,1,0:T(8,128)(2,1)S(1)} %pad_maximum_fusion.1.refs_0_), channel_id=1, source_target_pairs={{0,1},{1,0},{2,3},{3,2},{4,5},{5,4},{6,7},{7,6},{8,9},{9,8},{10,11... | collective-permute-start | bytes 3981320 | tf_op jit(solution)/shard_map/ppermute | solution.py:60
  117.6 19.3 %collective-permute-start.21 = (bf16[4,432,384]{2,1,0:T(8,128)(2,1)}, bf16[4,432,384]{2,1,0:T(8,128)(2,1)}, u32[]{:S(2)}, u32[]{:S(2)}) collective-permute-start(bf16[4,432,384]{2,1,0:T(8,128)(2,1)} %collective-permute-done.16.refs_8_.refs_1_), channel_id=1, source_target_pairs={{0,1},{1,0},{2,3},{3,2},{4,5},{5,4},{6,7},{7,6},{8,9},{9,8},{10,11... | collective-permute-start | bytes 3981320 | tf_op jit(solution)/shard_map/ppermute | solution.py:60
  118.1 18.8 %collective-permute-start.22 = (bf16[4,432,384]{2,1,0:T(8,128)(2,1)}, bf16[4,432,384]{2,1,0:T(8,128)(2,1)}, u32[]{:S(2)}, u32[]{:S(2)}) collective-permute-start(bf16[4,432,384]{2,1,0:T(8,128)(2,1)} %collective-permute-done.17.refs_9_.refs_2_), channel_id=1, source_target_pairs={{0,1},{1,0},{2,3},{3,2},{4,5},{5,4},{6,7},{7,6},{8,9},{9,8},{10,11... | collective-permute-start | bytes 3981320 | tf_op jit(solution)/shard_map/ppermute | solution.py:60
  118.2 16.0 %copy-start.47 = (s32[23]{0:T(128)S(1)}, s32[23]{0:T(128)}, u32[]{:S(2)}) copy-start(s32[23]{0:T(128)} %stack.146.refs_0_.meta) | copy-start | bytes 280
  133.6 2.6 collective-permute-start.23
  134.1 2.8 collective-permute-start.24
  134.2 44.5 %copy-start.51 = (s32[23]{0:T(128)}, s32[23]{0:T(128)S(1)}, u32[]{:S(2)}) copy-start(s32[23]{0:T(128)S(1)} %constant_dynamic-update-slice_fusion.meta) | copy-start | bytes 280
  194.5 30.9 %collective-permute-start.25 = (bf16[2,2,4,432,384]{4,3,2,1,0:T(8,128)(2,1)}, bf16[2,2,4,432,384]{4,3,2,1,0:T(8,128)(2,1)}, u32[]{:S(2)}, u32[]{:S(2)}) collective-permute-start(bf16[2,2,4,432,384]{4,3,2,1,0:T(8,128)(2,1)} %feed_grad.2.refs_12_), channel_id=1, source_target_pairs={{0,1},{1,0},{2,3},{3,2},{4,5},{5,4},{6,7},{7,6},{8,9},{9,8},{10,11... | collective-permute-start | bytes 15925256 | tf_op jit(solution)/shard_map/ppermute | solution.py:60
  243.7 33.8 %collective-permute-start.26 = (bf16[2,2,432,384]{3,2,1,0:T(8,128)(2,1)}, bf16[2,2,432,384]{3,2,1,0:T(8,128)(2,1)S(1)}, u32[]{:S(2)}, u32[]{:S(2)}) collective-permute-start(bf16[2,2,432,384]{3,2,1,0:T(8,128)(2,1)} %get-tuple-element.161.refs_15_), channel_id=1, source_target_pairs={{0,4},{4,0},{8,12},{12,8},{16,20},{20,16},{24,28},{28,24},{1,5},{5... | collective-permute-start | bytes 3981320 | tf_op jit(solution)/shard_map/ppermute | solution.py:60
  244.6 32.9 %collective-permute-start.27 = (bf16[2,2,432,384]{3,2,1,0:T(8,128)(2,1)}, bf16[2,2,432,384]{3,2,1,0:T(8,128)(2,1)S(1)}, u32[]{:S(2)}, u32[]{:S(2)}) collective-permute-start(bf16[2,2,432,384]{3,2,1,0:T(8,128)(2,1)} %get-tuple-element.162.refs_16_), channel_id=1, source_target_pairs={{0,2},{1,3},{2,0},{3,1},{4,6},{5,7},{6,4},{7,5},{8,10},{9,11},{10,... | collective-permute-start | bytes 3981320 | tf_op jit(solution)/shard_map/ppermute | solution.py:60
  281.3 24.0 %collective-permute-start.28 = (bf16[2,432,384]{2,1,0:T(8,128)(2,1)}, bf16[2,432,384]{2,1,0:T(8,128)(2,1)}, u32[]{:S(2)}, u32[]{:S(2)}) collective-permute-start(bf16[2,432,384]{2,1,0:T(8,128)(2,1)} %fusion.8.refs_10_), channel_id=1, source_target_pairs={{0,4},{4,0},{8,12},{12,8},{16,20},{20,16},{24,28},{28,24},{1,5},{5... | collective-permute-start | bytes 1990664 | tf_op jit(solution)/shard_map/ppermute | solution.py:60
  283.3 22.0 %collective-permute-start.29 = (bf16[2,432,384]{2,1,0:T(8,128)(2,1)S(1)}, bf16[2,432,384]{2,1,0:T(8,128)(2,1)S(1)}, u32[]{:S(2)}, u32[]{:S(2)}) collective-permute-start(bf16[2,432,384]{2,1,0:T(8,128)(2,1)S(1)} %fusion.6.refs_11_), channel_id=1, source_target_pairs={{0,2},{1,3},{2,0},{3,1},{4,6},{5,7},{6,4},{7,5},{8,10},{9,11},{10,... | collective-permute-start | bytes 1990664 | tf_op jit(solution)/shard_map/ppermute | solution.py:60
  305.3 27.3 %collective-permute-start.31 = (bf16[2,2,4,48,1152]{4,3,2,1,0:T(8,128)(2,1)}, bf16[2,2,4,48,1152]{4,3,2,1,0:T(8,128)(2,1)}, u32[]{:S(2)}, u32[]{:S(2)}) collective-permute-start(bf16[2,2,4,48,1152]{4,3,2,1,0:T(8,128)(2,1)} %get-tuple-element.177), channel_id=1, source_target_pairs={{0,1},{1,0},{2,3},{3,2},{4,5},{5,4},{6,7},{7,6},{8,9},{9,8},{10,11... | collective-permute-start | bytes 5308424 | tf_op jit(solution)/shard_map/ppermute | solution.py:60
  309.6 23.0 %collective-permute-start.30 = (bf16[2,432,384]{2,1,0:T(8,128)(2,1)S(1)}, bf16[2,432,384]{2,1,0:T(8,128)(2,1)S(1)}, u32[]{:S(2)}, u32[]{:S(2)}) collective-permute-start(bf16[2,432,384]{2,1,0:T(8,128)(2,1)S(1)} %pad_maximum_fusion.3.refs_5_), channel_id=1, source_target_pairs={{0,8},{4,12},{8,0},{12,4},{16,24},{20,28},{24,16},{28,20},{1,9},{5... | collective-permute-start | bytes 1990664 | tf_op jit(solution)/shard_map/ppermute | solution.py:60
  312.6 14.0 %copy-start.44 = (f32[8,768]{1,0:T(8,128)S(1)}, f32[8,768]{1,0:T(8,128)}, u32[]{:S(2)}) copy-start(f32[8,768]{1,0:T(8,128)} %get-tuple-element.178) | copy-start | bytes 73732
  326.6 26.6 %collective-permute-start.33 = (bf16[2,1024,768]{2,1,0:T(8,128)(2,1)}, bf16[2,1024,768]{2,1,0:T(8,128)(2,1)}, u32[]{:S(2)}, u32[]{:S(2)}) collective-permute-start(bf16[2,1024,768]{2,1,0:T(8,128)(2,1)} %get-tuple-element.180), channel_id=1, source_target_pairs={{0,1},{1,0},{2,3},{3,2},{4,5},{5,4},{6,7},{7,6},{8,9},{9,8},{10,11... | collective-permute-start | bytes 9437192 | tf_op jit(solution)/shard_map/ppermute | solution.py:60
  328.4 4.2 collective-permute-start.32
  332.6 20.6 %collective-permute-start.36 = (f32[12,768]{1,0:T(8,128)S(1)}, f32[12,768]{1,0:T(8,128)S(1)}, u32[]{:S(2)}, u32[]{:S(2)}) collective-permute-start(f32[12,768]{1,0:T(8,128)S(1)} %fusion.36), channel_id=1, source_target_pairs={{0,1},{1,0},{2,3},{3,2},{4,5},{5,4},{6,7},{7,6},{8,9},{9,8},{10,11... | collective-permute-start | bytes 110600 | tf_op jit(solution)/shard_map/ppermute | solution.py:60
  336.6 7.1 %copy-start.10 = (bf16[2,2,48,1152]{3,2,1,0:T(8,128)(2,1)}, bf16[2,2,48,1152]{3,2,1,0:T(8,128)(2,1)S(1)}, u32[]{:S(2)}) copy-start(bf16[2,2,48,1152]{3,2,1,0:T(8,128)(2,1)S(1)} %pad_maximum_fusion.7.refs_7_) | copy-start | bytes 1327108
  336.6 16.6 %collective-permute-start.34 = (bf16[2,2,48,1152]{3,2,1,0:T(8,128)(2,1)S(1)}, bf16[2,2,48,1152]{3,2,1,0:T(8,128)(2,1)}, u32[]{:S(2)}, u32[]{:S(2)}) collective-permute-start(bf16[2,2,48,1152]{3,2,1,0:T(8,128)(2,1)S(1)} %pad_maximum_fusion.7.refs_7_), channel_id=1, source_target_pairs={{0,4},{4,0},{8,12},{12,8},{16,20},{20,16},{24,28},{28,24},{1,5},{5... | collective-permute-start | bytes 1327112 | tf_op jit(solution)/shard_map/ppermute | solution.py:60
  339.2 14.0 %collective-permute-start.35 = (bf16[2,2,48,1152]{3,2,1,0:T(8,128)(2,1)}, bf16[2,2,48,1152]{3,2,1,0:T(8,128)(2,1)}, u32[]{:S(2)}, u32[]{:S(2)}) collective-permute-start(bf16[2,2,48,1152]{3,2,1,0:T(8,128)(2,1)} %pad_maximum_fusion.8.refs_8_), channel_id=1, source_target_pairs={{0,2},{1,3},{2,0},{3,1},{4,6},{5,7},{6,4},{7,5},{8,10},{9,11},{10,... | collective-permute-start | bytes 1327112 | tf_op jit(solution)/shard_map/ppermute | solution.py:60
  340.6 20.9 %collective-permute-start.39 = (bf16[432,384]{1,0:T(8,128)(2,1)}, bf16[432,384]{1,0:T(8,128)(2,1)}, u32[]{:S(2)}, u32[]{:S(2)}) collective-permute-start(bf16[432,384]{1,0:T(8,128)(2,1)} %fusion.20), channel_id=1, source_target_pairs={{0,16},{4,20},{8,24},{12,28},{16,0},{20,4},{24,8},{28,12},{1,17},{... | collective-permute-start | bytes 995336 | tf_op jit(solution)/shard_map/ppermute | solution.py:60
  353.3 8.2 %collective-permute-start.40 = (f32[12,768]{1,0:T(8,128)S(1)}, f32[12,768]{1,0:T(8,128)S(1)}, u32[]{:S(2)}, u32[]{:S(2)}) collective-permute-start(f32[12,768]{1,0:T(8,128)S(1)} %add.427), channel_id=1, source_target_pairs={{0,2},{1,3},{2,0},{3,1},{4,6},{5,7},{6,4},{7,5},{8,10},{9,11},{10,... | collective-permute-start | bytes 110600 | tf_op jit(solution)/shard_map/ppermute | solution.py:60
  356.9 6.0 %collective-permute-start.38 = (bf16[2,48,1152]{2,1,0:T(8,128)(2,1)S(1)}, bf16[2,48,1152]{2,1,0:T(8,128)(2,1)S(1)}, u32[]{:S(2)}, u32[]{:S(2)}) collective-permute-start(bf16[2,48,1152]{2,1,0:T(8,128)(2,1)S(1)} %get-tuple-element.231), channel_id=1, source_target_pairs={{0,2},{1,3},{2,0},{3,1},{4,6},{5,7},{6,4},{7,5},{8,10},{9,11},{10,... | collective-permute-start | bytes 663560 | tf_op jit(solution)/shard_map/ppermute | solution.py:60
  357.8 5.9 %collective-permute-start.37 = (bf16[2,48,1152]{2,1,0:T(8,128)(2,1)S(1)}, bf16[2,48,1152]{2,1,0:T(8,128)(2,1)S(1)}, u32[]{:S(2)}, u32[]{:S(2)}) collective-permute-start(bf16[2,48,1152]{2,1,0:T(8,128)(2,1)S(1)} %get-tuple-element.232), channel_id=1, source_target_pairs={{0,4},{4,0},{8,12},{12,8},{16,20},{20,16},{24,28},{28,24},{1,5},{5... | collective-permute-start | bytes 663560 | tf_op jit(solution)/shard_map/ppermute | solution.py:60
  366.8 9.1 %collective-permute-start.43 = (f32[216,384]{1,0:T(8,128)S(1)}, f32[216,384]{1,0:T(8,128)S(1)}, u32[]{:S(2)}, u32[]{:S(2)}) collective-permute-start(f32[216,384]{1,0:T(8,128)S(1)} %dynamic-slice_bitcast_fusion), channel_id=1, source_target_pairs={{0,1},{1,0},{2,3},{3,2},{4,5},{5,4},{6,7},{7,6},{8,9},{9,8},{10,11... | collective-permute-start | bytes 995336 | tf_op jit(solution)/shard_map/ppermute | solution.py:60
  366.9 8.9 %collective-permute-start.41 = (bf16[2,48,1152]{2,1,0:T(8,128)(2,1)S(1)}, bf16[2,48,1152]{2,1,0:T(8,128)(2,1)S(1)}, u32[]{:S(2)}, u32[]{:S(2)}) collective-permute-start(bf16[2,48,1152]{2,1,0:T(8,128)(2,1)S(1)} %pad_maximum_fusion.12), channel_id=1, source_target_pairs={{0,8},{4,12},{8,0},{12,4},{16,24},{20,28},{24,16},{28,20},{1,9},{5... | collective-permute-start | bytes 663560 | tf_op jit(solution)/shard_map/ppermute | solution.py:60
  368.3 7.6 %collective-permute-start.42 = (f32[12,768]{1,0:T(8,128)S(1)}, f32[12,768]{1,0:T(8,128)S(1)}, u32[]{:S(2)}, u32[]{:S(2)}) collective-permute-start(f32[12,768]{1,0:T(8,128)S(1)} %add.434), channel_id=1, source_target_pairs={{0,8},{4,12},{8,0},{12,4},{16,24},{20,28},{24,16},{28,20},{1,9},{5... | collective-permute-start | bytes 110600 | tf_op jit(solution)/shard_map/ppermute | solution.py:60
  369.0 17.3 %copy-start.14 = (f32[2,48,1152]{2,1,0:T(8,128)S(1)}, f32[2,48,1152]{2,1,0:T(8,128)}, u32[]{:S(2)}) copy-start(f32[2,48,1152]{2,1,0:T(8,128)} %copy-done.13) | copy-start | bytes 1327108
  369.0 36.5 %collective-permute-start.49 = (bf16[1024,768]{1,0:T(8,128)(2,1)}, bf16[1024,768]{1,0:T(8,128)(2,1)}, u32[]{:S(2)}, u32[]{:S(2)}) collective-permute-start(bf16[1024,768]{1,0:T(8,128)(2,1)} %fusion), channel_id=1, source_target_pairs={{0,2},{1,3},{2,0},{3,1},{4,6},{5,7},{6,4},{7,5},{8,10},{9,11},{10,... | collective-permute-start | bytes 4718600 | tf_op jit(solution)/shard_map/ppermute | solution.py:60
  375.9 8.6 %collective-permute-start.45 = (f32[12,768]{1,0:T(8,128)S(1)}, f32[12,768]{1,0:T(8,128)S(1)}, u32[]{:S(2)}, u32[]{:S(2)}) collective-permute-start(f32[12,768]{1,0:T(8,128)S(1)} %add.438), channel_id=1, source_target_pairs={{0,16},{4,20},{8,24},{12,28},{16,0},{20,4},{24,8},{28,12},{1,17},{... | collective-permute-start | bytes 110600 | tf_op jit(solution)/shard_map/ppermute | solution.py:60
  376.7 9.6 %collective-permute-start.44 = (bf16[48,1152]{1,0:T(8,128)(2,1)S(1)}, bf16[48,1152]{1,0:T(8,128)(2,1)S(1)}, u32[]{:S(2)}, u32[]{:S(2)}) collective-permute-start(bf16[48,1152]{1,0:T(8,128)(2,1)S(1)} %fusion.27), channel_id=1, source_target_pairs={{0,16},{4,20},{8,24},{12,28},{16,0},{20,4},{24,8},{28,12},{1,17},{... | collective-permute-start | bytes 331784 | tf_op jit(solution)/shard_map/ppermute | solution.py:60
  378.9 26.6 %copy-start.1 = (f32[1,1024,768]{2,1,0:T(8,128)S(1)}, f32[1,1024,768]{2,1,0:T(8,128)}, u32[]{:S(2)}) copy-start(f32[1,1024,768]{2,1,0:T(8,128)} %token_grad.3) | copy-start | bytes 9437188
  387.9 13.8 %collective-permute-start.52 = (f32[24,1152]{1,0:T(8,128)S(1)}, f32[24,1152]{1,0:T(8,128)}, u32[]{:S(2)}, u32[]{:S(2)}) collective-permute-start(f32[24,1152]{1,0:T(8,128)S(1)} %dynamic-slice_bitcast_fusion.2), channel_id=1, source_target_pairs={{0,1},{1,0},{2,3},{3,2},{4,5},{5,4},{6,7},{7,6},{8,9},{9,8},{10,11... | collective-permute-start | bytes 331784 | tf_op jit(solution)/shard_map/ppermute | solution.py:60
  391.3 1.4 collective-permute-start.46
  393.3 3.6 collective-permute-start.47
  397.5 3.6 collective-permute-start.48
  409.5 4.4 %collective-permute-start.50 = (f32[1,1]{1,0:T(1,128)}, f32[1,1]{1,0:T(1,128)}, u32[]{:S(2)}, u32[]{:S(2)}) collective-permute-start(f32[1,1]{1,0:T(1,128)} %add.447), channel_id=1, source_target_pairs={{0,16},{4,20},{8,24},{12,28},{16,0},{20,4},{24,8},{28,12},{1,17},{... | collective-permute-start | bytes 20 | tf_op jit(solution)/shard_map/ppermute | solution.py:60
  414.5 3.6 collective-permute-start.51
  (44 other events, 113.7 us)
